TPU v7x, 32 devices: a whole 2x2x4 slice. The times are simulated.
32 devices in a mesh: groups: 2 (over y), theta: 16 (over z, x, core).
Axes of the slice: x: 2, y: 2, z: 4, core: 2. Of those that a mesh axis runs over, the one named last changes fastest.
Arguments:
- state_now: float32 [5, 2, 64, 256, 128], P(None, None, 'theta', 'groups'), parts along dimension 3, may hold values from -6 to 6
- state_prev: float32 [5, 2, 64, 256, 128], P(None, None, 'theta', 'groups'), parts along dimension 3, may hold values from -6 to 6
- eddy_visc: float32 [2, 64, 256, 128], P(None, 'theta', 'groups'), parts along dimension 2, may hold values from 0.01 to 0.2
- mean_flow: float32 [2, 4], replicated, may hold values from 0.5 to 1
- offset: int32 [2], P('groups'), parts along dimension 0, may hold values from 0 to 63
Outputs:
- field: float32 [5, 2, 64, 256, 128], P(None, None, 'theta', 'groups'), parts along dimension 3
There are 2 independent parts, one for each index of `groups`. A program takes and returns all parts, laid end to end along the dimension named above; an argument that names none is the same for every part. Nothing has to cross between parts.
All inputs are finite; a program needn't handle non-finite values.
Results may differ from a plain program's by a relative error of at most 0.00002.
Values sent between devices are 32-bit elements; how exact they have to be, the bound alone decides.
No kernel may reach another device: no remote copies, remote signals or barrier semaphores. Data moves between devices by JAX's collectives and lax.ppermute only.
A program may use at most 128 MiB of HBM per device.

v0:
```python
import jax
import jax.numpy as jnp
from jax import lax
from jax.experimental import pallas as pl
from jax.experimental.pallas import tpu as pltpu
from jax.sharding import PartitionSpec as P

ITERS = 2
PSEUDO_STEP = 0.2
PHYS_STEP = 1.0
SECTION_WEIGHTS = (0.6, 0.6, 1.0)
COMPS = 5
CHUNK = 32
STRIP = 8
EDGE = 4
NEED = 6
HALF = 32
PARTS = 2
PIECES = 4


def scalars_of(mean_flow, sign):
    flow = jnp.concatenate([mean_flow, 1.0 / mean_flow[:, 2:3]], axis=1).reshape(-1)
    return jnp.concatenate([flow, jnp.broadcast_to(sign, (6,))])


def coefficients(scalars, row, weight):
    a = weight * PSEUDO_STEP
    axial, swirl, density, sound, inverse = (scalars[row * 5 + i] for i in range(5))
    sign = scalars[10]
    half = 0.5 * a
    mass, lift = half * density, half * inverse
    return half * axial, half * swirl * sign, mass, mass * sound * sound, lift, lift * sign, sign, a


def advance(k, f, up, down, low, high, behind, ahead, base, fixed, eddy):
    e = k[7] * eddy
    damp = 6.0 * e + (1.5 / PHYS_STEP) * k[7]
    da = [ahead[c] - behind[c] for c in range(COMPS)]
    dt = [down[c] - up[c] for c in range(COMPS)]
    dr = [high[c] - low[c] if c >= 3 else None for c in range(COMPS)]
    div = da[1] + k[6] * dt[2] + dr[3]
    push = (k[2] * div, k[4] * da[4], k[5] * dt[4], k[4] * dr[4], k[3] * div)
    new = []
    for c in range(COMPS):
        around = ((up[c] + down[c]) + (low[c] + high[c])) + (behind[c] + ahead[c])
        kept = (base[c] - k[7] * fixed[c]) - damp * f[c]
        new.append(kept + e * around - k[0] * da[c] - k[1] * dt[c] - push[c])
    return new


def fixed_part(now, prev):
    return (prev - 4.0 * now) * (0.5 / PHYS_STEP)


def layer_rows(ref, row, size, first=0):
    return lambda c, r, n: ref[pl.ds((c * 2 + row) * size + r - first, n), :]


def joined(refs, row, size):
    def read(c, r, n):
        p, q = r // size, (r + n - 1) // size
        if p == q:
            return layer_rows(refs[p], row, size, p * size)(c, r, n)
        cut = q * size - r
        return jnp.concatenate(
            [layer_rows(refs[p], row, size, p * size)(c, r, cut), layer_rows(refs[q], row, size, q * size)(c, r + cut, n - cut)]
        )

    return read


def pieces(refs, row, size, piece):
    def read(c, r, n):
        at, first = divmod((c * 2 + row) * size + r, piece)
        return refs[at][pl.ds(first, n), :]

    return read


def plain_rows(ref, row, layer):
    return lambda c, r, n: ref[c, row, layer, pl.ds(r, n), :]


def update_rows(row, r0, radial, ghost_at, center, before, after, base, now, prev, eddy, ghosts, coef, store):
    ghost = ghosts[pl.ds(r0, CHUNK), :]
    axial = ghost.shape[-1]
    lane = lax.broadcasted_iota(jnp.int32, ghost.shape, 1)
    first, last = lane == 0, lane == axial - 1
    f, low, high, behind, ahead = [], [], [], [], []
    for c in range(COMPS):
        f.append(center(c, r0, CHUNK))
        wall = -1.0 if c == 3 else 1.0
        if r0 == 0:
            low.append(jnp.concatenate([f[c][:1] * wall, center(c, 0, CHUNK - 1)], axis=0))
        else:
            low.append(center(c, r0 - 1, CHUNK))
        if r0 + CHUNK == radial:
            high.append(jnp.concatenate([center(c, r0 + 1, CHUNK - 1), f[c][-1:] * wall], axis=0))
        else:
            high.append(center(c, r0 + 1, CHUNK))
        at = ghost_at(c)
        lower, upper = pltpu.roll(f[c], 1, 1), pltpu.roll(f[c], axial - 1, 1)
        if row == 0:
            lower = jnp.where(first, 0.0, lower)
            upper = jnp.where(last, pltpu.roll(ghost, (axial - 1 - at) % axial, 1), upper)
        else:
            lower = jnp.where(first, pltpu.roll(ghost, (axial - at) % axial, 1), lower)
            upper = jnp.where(last, f[c], upper)
        behind.append(lower)
        ahead.append(upper)
    every = range(COMPS)
    read = lambda source: [source(c, r0, CHUNK) for c in every]
    new = advance(
        coef[row], f, read(before), read(after), low, high, behind, ahead,
        read(base), [fixed_part(now(c, r0, CHUNK), prev(c, r0, CHUNK)) for c in every], eddy(r0, CHUNK),
    )
    for c in every:
        store(c, r0, new[c])


def pack_columns(tile, lines, radial, columns):
    axial = tile.shape[-1]
    lane = lax.broadcasted_iota(jnp.int32, (CHUNK, axial), 1)
    for r0 in range(0, radial, CHUNK):
        packed = jnp.zeros((CHUNK, axial), jnp.float32)
        for i, (row, c, center) in enumerate(columns):
            value, shift = center(c, r0, CHUNK), (i - (axial - 1 if row == 0 else 0)) % axial
            packed = jnp.where(lane == i, pltpu.roll(value, shift, 1) if shift else value, packed)
        tile[pl.ds(r0, CHUNK), :] = packed
    lines[...] = tile[...].T


def ghost_columns(tile, columns, faces):
    tile[...] = jnp.zeros_like(tile)
    for i, (strip, side) in enumerate(faces):
        face = 0 if side == 0 else STRIP - 1
        tile[pl.ds(i, 1), :] = strip[pl.ds(face, 1), :]
    columns[...] = tile[...].T


def strip_layer(coef, side, cur, up, down, lines, base, now, prev, eddy):
    radial = eddy.shape[-1]
    sub = lax.broadcasted_iota(jnp.int32, (STRIP, radial), 0)
    lane = lax.broadcasted_iota(jnp.int32, (STRIP, radial), 1)
    low, high, behind, ahead = [], [], [], []
    for c in range(COMPS):
        value = cur[c]
        wall = -value if c == 3 else value
        lower, upper = pltpu.roll(value, 1, 0), pltpu.roll(value, STRIP - 1, 0)
        if side == 0:
            lower = jnp.where(sub == 0, lines[c], lower)
        else:
            upper = jnp.where(sub == STRIP - 1, lines[c], upper)
        low.append(jnp.where(lane == 0, wall, pltpu.roll(value, 1, 1)))
        high.append(jnp.where(lane == radial - 1, wall, pltpu.roll(value, radial - 1, 1)))
        behind.append(lower)
        ahead.append(upper)
    fixed = [fixed_part(now[c], prev[c]) for c in range(COMPS)]
    return advance(coef[1 - side], cur, up, down, low, high, behind, ahead, base, fixed, eddy)


def edge_of(ref, side, c, separate, offset):
    if separate:
        return ref[side, c]
    got = ref[pl.ds(offset + EDGE * (side * COMPS + c), EDGE), :]
    rest = jnp.zeros((STRIP - EDGE, got.shape[1]), jnp.float32)
    return jnp.concatenate([got, rest] if side == 0 else [rest, got], axis=0)


def put_edge(ref, side, c, value, offset):
    start = 0 if side == 0 else STRIP - EDGE
    ref[pl.ds(offset + EDGE * (side * COMPS + c), EDGE), :] = value[start : start + EDGE]


class Plan:
    def __init__(self, n, shape):
        self.weight = SECTION_WEIGHTS[(n - 1) % len(SECTION_WEIGHTS)]
        self.n, self.total = n, ITERS * len(SECTION_WEIGHTS)
        self.cells, self.radial, self.axial = shape[2:]
        self.depth, self.size = self.cells - 1, self.radial // PARTS
        self.piece = 2 * COMPS * self.radial // PIECES
        self.final = n == self.total
        self.strips = n < self.total
        self.edges = n < self.total - 1


def place_of(scalars, depth):
    odd = scalars[10] < 0.0
    return jnp.where(odd, depth, 0), jnp.where(odd, -1, 1)


def outer_kernel(plan, p, refs):
    size, radial = plan.size, plan.radial
    scalars, eddy, prev, inner, strip = (refs.pop(0) for _ in range(5))
    place = place_of(scalars, plan.depth)
    coef = [coefficients(scalars, row, plan.weight) for row in range(2)]
    mine = [refs.pop(0) for _ in range(PARTS)]
    now, base, across = refs.pop(0), refs.pop(0), refs.pop(0)
    works = p == 0 and plan.strips
    if works:
        edges = refs.pop(0) if plan.n == 1 else across
        strip_inner, strip_now, strip_prev, strip_eddy = (refs.pop(0) for _ in range(4))
        strip_base = refs.pop(0)
    if p > 0 and not plan.final:
        refs.pop(0)
    if plan.final:
        refs.pop(0)
    out = refs.pop(0)
    if works:
        strip_out = refs.pop(0)
    tile, columns = refs.pop(0), refs.pop(0)
    if plan.final:
        made, sem = refs.pop(0), refs.pop(0)
    else:
        made = out
    ghost_columns(tile, columns, [(strip.at[side, c], side) for side in range(2) for c in range(COMPS)])
    for row in range(2):
        for r0 in range(p * size, (p + 1) * size, CHUNK):

            def store(c, r, value):
                made[pl.ds((c * 2 + row) * size + r - p * size, CHUNK), :] = value

            inside = plain_rows(inner, row, place[0] + place[1] if plan.n == 1 else 0)
            part = lambda ref: layer_rows(ref, row, size, p * size)
            update_rows(
                row, r0, radial, lambda c: row * COMPS + c, joined(mine, row, size), part(across), inside, part(base),
                part(now), part(prev), lambda r, n: eddy[row, pl.ds(r, n), :], columns, coef, store,
            )
    if plan.final:
        copies = []
        for c in range(COMPS):
            for row in range(2):
                source = made.at[pl.ds((c * 2 + row) * size, size), :]
                target = out.at[c, row, place[0], pl.ds(p * size, size), :]
                copies.append(pltpu.make_async_copy(source, target, sem.at[c * 2 + row]))
                copies[-1].start()
        for copy in copies:
            copy.wait()
    if works:
        lines = tile
        pack_columns(
            columns, lines, radial, [(row, c, joined(mine, row, size)) for row in range(2) for c in range(COMPS)]
        )
        every = range(COMPS)
        for side in range(2):
            result = strip_layer(
                coef, side, [strip[side, c] for c in every],
                [edge_of(edges, side, c, plan.n == 1, 2 * COMPS * size) for c in every],
                [strip_inner[side, c, 0] for c in every], [lines[pl.ds(side * COMPS + c, 1), :] for c in every],
                [strip_base[side, c] for c in every], [strip_now[side, c] for c in every],
                [strip_prev[side, c] for c in every], strip_eddy[side],
            )
            for c in every:
                strip_out[side, c] = result[c]
                if plan.edges:
                    put_edge(out, side, c, result[c], 2 * COMPS * size)


def inner_kernel(plan, refs):
    size, radial, depth = plan.size, plan.radial, plan.depth
    scalars, eddy, prev, now, inner, strip = (refs.pop(0) for _ in range(6))
    place = place_of(scalars, plan.depth)
    coef = [coefficients(scalars, row, plan.weight) for row in range(2)]
    if plan.n == 1:
        inner = now
    outer = [refs.pop(0) for _ in range(PARTS)]
    partner, base = [refs.pop(0) for _ in range(1 if plan.n == 1 else PIECES)], refs.pop(0)
    if plan.strips:
        edges = refs.pop(0) if plan.n == 1 else partner[-1]
        strip_outer, strip_now, strip_prev, strip_eddy, strip_base = (refs.pop(0) for _ in range(5))
    if plan.strips:
        refs.pop(0)
    made = refs.pop(0)
    if plan.strips:
        border, strip_out = [refs.pop(0) for _ in range(PIECES)], refs.pop(0)
    tile, columns = refs.pop(0), refs.pop(0)
    if plan.final:
        out, made, sem = made, refs.pop(0), refs.pop(0)
    ghost_columns(
        tile, columns, [(strip.at[side, c, j], side) for side in range(2) for c in range(COMPS) for j in range(depth)]
    )
    copies = []
    at = lambda j: place[0] + place[1] * (j + 1)
    own = lambda j: at(j) if plan.n == 1 else j
    for j in range(depth):
        for row in range(2):
            for r0 in range(0, radial, CHUNK):

                def store(c, r, value):
                    made[c, row, j, pl.ds(r, CHUNK), :] = value
                    if plan.strips and j == depth - 1:
                        piece, at_row = divmod((c * 2 + row) * radial + r, plan.piece)
                        border[piece][pl.ds(at_row, CHUNK), :] = value

                before = joined(outer, row, size) if j == 0 else plain_rows(inner, row, own(j - 1))
                after = pieces(partner, row, radial, partner[0].shape[0]) if j == depth - 1 else plain_rows(inner, row, own(j + 1))
                first = plan.n <= len(SECTION_WEIGHTS)
                update_rows(
                    row, r0, radial, lambda c: (row * COMPS + c) * depth + j, plain_rows(inner, row, own(j)), before,
                    after, plain_rows(base, row, at(j) if first else j), plain_rows(now, row, at(j)),
                    plain_rows(prev, row, at(j)), lambda r, n: eddy[row, at(j), pl.ds(r, n), :], columns, coef, store,
                )
        if plan.final:
            copies.append(pltpu.make_async_copy(made.at[:, :, j], out.at[:, :, at(j)], sem.at[j]))
            copies[-1].start()
    for copy in copies:
        copy.wait()
    if plan.strips:
        lines = tile
        pack_columns(
            columns, lines, radial,
            [(row, c, plain_rows(inner, row, own(j))) for row in range(2) for c in range(COMPS) for j in range(depth)],
        )
        every = range(COMPS)
        for side in range(2):
            for j in range(depth):
                if j < depth - 1:
                    down = [strip[side, c, j + 1] for c in every]
                else:
                    down = [edge_of(edges, side, c, plan.n == 1, plan.piece) for c in every]
                result = strip_layer(
                    coef, side, [strip[side, c, j] for c in every],
                    [strip_outer[side, c] if j == 0 else strip[side, c, j - 1] for c in every], down,
                    [lines[pl.ds((side * COMPS + c) * depth + j, 1), :] for c in every],
                    [strip_base[side, c, j] for c in every], [strip_now[side, c, j] for c in every],
                    [strip_prev[side, c, j] for c in every], strip_eddy[side, j],
                )
                for c in every:
                    strip_out[side, c, j] = result[c]
                    if j == depth - 1 and plan.edges:
                        put_edge(border[-1], side, c, result[c], plan.piece)


def strip_items():
    now = [(0, c, NEED, c * NEED) for c in range(COMPS)]
    rest = [(1, c, NEED - 1, c * (NEED - 1)) for c in range(COMPS)]
    return now + rest + [(2, 0, NEED - 1, COMPS * (NEED - 1))]


def gather_kernel(scalars, now, prev, eddy, *outs):
    _, _, cells, radial, axial = now.shape
    depth, size = cells - 1, radial // PARTS
    first, step = place_of(scalars, depth)
    border, now_outer, prev_outer, eddy_outer = outs[2], outs[3 : 3 + PARTS], outs[3 + PARTS : -1], outs[-1]
    for c in range(COMPS):
        for row in range(2):
            for r0 in range(0, radial, CHUNK):
                rows = pl.ds(r0, CHUNK)
                border[pl.ds((c * 2 + row) * radial + r0, CHUNK), :] = now[c, row, first + step * depth, rows, :]
                p, at_row = r0 // size, (c * 2 + row) * size + r0 % size
                now_outer[p][pl.ds(at_row, CHUNK), :] = now[c, row, first, rows, :]
                prev_outer[p][pl.ds(at_row, CHUNK), :] = prev[c, row, first, rows, :]
    for row in range(2):
        eddy_outer[row] = eddy[row, first]
    per_tile = axial // STRIP
    block = lax.broadcasted_iota(jnp.int32, (radial, axial), 1) // STRIP
    items = [(item, t) for item in strip_items() for t in range(cells)]
    outs[0][...] = jnp.zeros_like(outs[0])
    outs[1][...] = jnp.zeros_like(outs[1])
    for row in range(2):
        mine, other = outs[row], outs[1 - row]
        begin = axial - STRIP if row == 0 else 0
        for p in range(0, len(items), per_tile):
            tile = jnp.zeros((radial, axial), jnp.float32)
            for q, ((kind, c, _, _), t) in enumerate(items[p : p + per_tile]):
                value = eddy[row, t] if kind == 2 else (now, prev)[kind][c, row, t]
                shift = (q * STRIP - begin) % axial
                tile = jnp.where(block == q, pltpu.roll(value, shift, 1) if shift else value, tile)
            turned = tile.T
            for q, ((kind, _, count, at), t) in enumerate(items[p : p + per_tile]):
                start = q * STRIP + (STRIP - count if row == 0 else 0)
                value = turned[start : start + count]
                mine[pl.ds((2 * t + (kind > 0)) * HALF + at, count), :] = value
                if kind == 0 and t == (0 if row == 0 else depth):
                    other[pl.ds(2 * cells * HALF + at, count), :] = value


def align_kernel(depth, within, rotor, stator, rotor_behind, stator_ahead, *outs):
    cells = depth + 1
    edge = 2 * cells * HALF

    def block(own, side, sidestart, far, theta, half):
        at = lambda x: pl.multiple_of((2 * jnp.clip(x, 0, depth) + half) * HALF, HALF)
        near = own[pl.ds(at(theta), HALF), :]
        beside = side[pl.ds(at(theta - sidestart), HALF), :]
        value = jnp.where((theta >= 0) & (theta < cells), near, beside)
        if half == 0:
            value = jnp.where(theta == (cells if sidestart < 0 else -1), far[pl.ds(edge, HALF), :], value)
        return value

    for row, out in enumerate(outs):
        own, side, far = (rotor, rotor_behind, stator_ahead) if row == 0 else (stator, stator_ahead, rotor_behind)
        start = -within[0] if row == 0 else within[0]
        sidestart = -cells if row == 0 else cells
        for k in range(-1, cells + 1):
            for half in range(2):
                if half and k in (-1, cells):
                    continue
                at_row = 0 if k < 0 else (1 + 2 * k + half) * HALF
                out[pl.ds(at_row, HALF), :] = block(own, side, sidestart, far, start + k, half)


def scatter_kernel(depth, scalars, rotor, stator, *outs):
    cells = depth + 1
    radial = rotor.shape[-1]
    now_out, now_in, prev_out, prev_in, eddy_out, eddy_in, across, partner = outs
    first, step = place_of(scalars, depth)
    for side, ref in enumerate((stator, rotor)):
        for kind, c, count, at in strip_items():

            def read(row):
                value = ref[pl.ds(row, count), :]
                rest = jnp.zeros((STRIP - count, radial), jnp.float32)
                return jnp.concatenate([value, rest] if side == 0 else [rest, value], axis=0)

            for j in range(cells):
                start = (1 + 2 * (first + step * j) + (kind > 0)) * HALF
                value = read(pl.multiple_of(start, HALF) + at)
                if kind == 2 and j == 0:
                    eddy_out[side] = value
                elif kind == 2:
                    eddy_in[side, j - 1] = value
                elif j == 0:
                    (now_out, prev_out)[kind][side, c] = value
                else:
                    (now_in, prev_in)[kind][side, c, j - 1] = value
            if kind == 0:
                low, high = read(at), read((1 + 2 * cells) * HALF + at)
                across[side, c] = jnp.where(step > 0, low, high)
                partner[side, c] = jnp.where(step > 0, high, low)


VMEM = pl.BlockSpec(memory_space=pltpu.VMEM)
SMEM = pl.BlockSpec(memory_space=pltpu.SMEM)
ANY = pl.BlockSpec(memory_space=pl.ANY)


def run(kernel, scalars, arrays, outs, scratch, name, final=None, out_shape=None, pinned=True):
    scalars, arrays = list(scalars), list(arrays)
    if pinned:
        arrays = [pltpu.with_memory_space_constraint(x, pltpu.VMEM) for x in arrays]
    in_specs = [SMEM] * len(scalars) + [VMEM] * len(arrays)
    if out_shape is not None:
        outs, out_specs = jax.ShapeDtypeStruct(out_shape, jnp.float32), ANY
    else:
        out_specs = (VMEM,) * len(outs)
    aliases = {}
    if final is not None:
        aliases = {len(in_specs): 0}
        in_specs, arrays = in_specs + [ANY], arrays + [final]
    return pl.pallas_call(
        lambda *refs: kernel(list(refs)),
        out_shape=outs,
        in_specs=in_specs,
        out_specs=out_specs,
        input_output_aliases=aliases,
        scratch_shapes=scratch,
        compiler_params=pltpu.CompilerParams(vmem_limit_bytes=16 << 20),
        cost_estimate=pl.CostEstimate(flops=1, bytes_accessed=1, transcendentals=0),
        name=name,
    )(*scalars, *arrays)


def call_gather(scalars, now, prev, eddy):
    cells, radial, axial = now.shape[2:]
    plain = lambda *shape: jax.ShapeDtypeStruct(shape, jnp.float32)
    strips = plain(2 * HALF * cells + HALF, radial)
    part = plain(2 * COMPS * radial // PARTS, axial)
    outs = (strips,) * 2 + (plain(2 * COMPS * radial, axial),) + (part,) * (2 * PARTS) + (plain(2, radial, axial),)
    got = run(lambda refs: gather_kernel(*refs), [scalars], [now, prev, eddy], outs, [], "gather_strips")
    return got[:2], got[2], got[3 : 3 + PARTS], got[3 + PARTS : -1], got[-1]


def call_align(within, strips, cells):
    rotor, stator = strips
    moved = [shifted(rotor, 1), shifted(stator, -1)]
    rows = jax.ShapeDtypeStruct((2 * HALF * (cells + 1), rotor.shape[1]), jnp.float32)
    return run(
        lambda refs: align_kernel(cells - 1, *refs), [within.reshape(1)], [rotor, stator, *moved], (rows, rows), [],
        "align_strips", pinned=False,
    )


def call_scatter(scalars, rotor, stator, cells):
    radial = rotor.shape[1]
    shape = lambda *lead: pltpu.VMEM((2, *lead, STRIP, radial), jnp.float32)
    both = [shape(COMPS), shape(COMPS, cells - 1)]
    outs = (*both, *both, shape(), shape(cells - 1), shape(COMPS), shape(COMPS))
    return run(
        lambda refs: scatter_kernel(cells - 1, *refs), [scalars], [rotor, stator], outs, [], "scatter_strips",
        pinned=False,
    )


def shifted(value, steps):
    count = lax.axis_size("theta")
    return lax.ppermute(value, "theta", [(i, (i + steps) % count) for i in range(count)])


def across_chips(value):
    count = lax.axis_size("theta")
    pairs = [(i, (i - 1 if i % 2 == 0 else i + 1) % count) for i in range(count)]
    return lax.ppermute(value, "theta", pairs)


def within_chip(value):
    count = lax.axis_size("theta")
    return lax.ppermute(value, "theta", [(i, i ^ 1) for i in range(count)])


def faced(outer, border, rotor, stator, sectors):
    count = lax.axis_size("theta")
    if count <= 16:

        def branch(steps):
            def exchange(outer, border, rotor, stator):
                return across_chips(outer), within_chip(border), shifted(rotor, steps), shifted(stator, -steps)

            return exchange

        return lax.switch(sectors, [branch(i) for i in range(count)], outer, border, rotor, stator)
    amounts = jnp.stack([sectors, count - sectors]) % count
    stacked = jnp.stack([rotor, stator])
    for level in range((count - 1).bit_length()):
        taken = ((amounts >> level) & 1) == 1
        stacked = jnp.where(taken[:, None, None], shifted(stacked, 1 << level), stacked)
    return across_chips(outer), within_chip(border), stacked[0], stacked[1]


def per_device(state_now, state_prev, eddy_visc, mean_flow, offset):
    shape = state_now.shape
    cells, radial, axial = shape[2:]
    count = lax.axis_size("theta")
    core = lax.axis_index("theta") % 2
    scalars = scalars_of(mean_flow, jnp.where(core == 1, -1.0, 1.0).astype(jnp.float32))
    shift_cells = offset[0] % (cells * count)
    depth, size = cells - 1, radial // PARTS

    early = lax.dynamic_index_in_dim(state_now[:, :, :, :size], core * depth, 2, keepdims=False)
    across = [across_chips(early.reshape(2 * COMPS * size, axial))]
    strips, border, outer, prev_outer, eddy_outer = call_gather(scalars, state_now, state_prev, eddy_visc)
    rotor, stator = call_align(shift_cells % cells, strips, cells)
    sectors = lax.optimization_barrier((shift_cells // cells, across))[0]
    late, border, rotor, stator = faced(outer[1], border, rotor, stator, sectors)
    across.append(late)
    partner = [border]
    now_out, now_in, prev_out, prev_in, eddy_out, eddy_in, edge_across, edge_within = call_scatter(
        scalars, rotor, stator, cells
    )

    now_outer, inner, strip_out, strip_in = outer, state_now, now_out, now_in
    f32 = jnp.float32
    square = pltpu.VMEM((radial, axial), f32)
    n = 0
    for _ in range(ITERS):
        base_outer, base_inner, base_out, base_in = outer, inner, strip_out, strip_in
        for _ in SECTION_WEIGHTS:
            n += 1
            plan = Plan(n, shape)

            def outer_call(p, ordered):
                arrays = [eddy_outer, prev_outer[p], inner, strip_out, *outer, now_outer[p], base_outer[p], across[p]]
                outs = [pltpu.VMEM((2 * COMPS * size, axial), f32)]
                if p == 0 and plan.edges:
                    outs = [pltpu.VMEM((2 * COMPS * (size + EDGE), axial), f32)]
                if p == 0 and plan.strips:
                    arrays += [edge_across] if n == 1 else []
                    arrays += [strip_in, now_out, prev_out, eddy_out, base_out]
                    outs.append(pltpu.VMEM(strip_out.shape, f32))
                scratch = [square, square]
                if plan.final:
                    scratch += [pltpu.VMEM((2 * COMPS * size, axial), f32), pltpu.SemaphoreType.DMA((2 * COMPS,))]
                elif p > 0:
                    arrays.append(ordered)
                return run(
                    lambda refs: outer_kernel(plan, p, refs), [scalars], arrays, tuple(outs), scratch, "outer",
                    ordered if plan.final else None, shape if plan.final else None, n > 1,
                )

            def inner_call(ordered):
                arrays = [eddy_visc, state_prev, state_now, inner, strip_in, *outer, *partner, base_inner]
                outs = [pltpu.VMEM((COMPS, 2, depth, radial, axial), f32)]
                if plan.strips:
                    arrays += [edge_within] if n == 1 else []
                    arrays += [strip_out, now_in, prev_in, eddy_in, base_in, ordered]
                    outs += [pltpu.VMEM((plan.piece, axial), f32)] * (PIECES - 1)
                    rows = plan.piece + (2 * COMPS * EDGE if plan.edges else 0)
                    outs += [pltpu.VMEM((rows, axial), f32), pltpu.VMEM(strip_in.shape, f32)]
                scratch = [square, square]
                if plan.final:
                    scratch += [pltpu.VMEM((COMPS, 2, depth, radial, axial), f32), pltpu.SemaphoreType.DMA((depth,))]
                return run(
                    lambda refs: inner_kernel(plan, refs), [scalars], arrays, tuple(outs), scratch, "inner", None,
                    shape if plan.final else None, n > 1,
                )

            if plan.final:
                made = inner_call(None)
                for p in range(PARTS):
                    made = outer_call(p, made)
                return made
            new_outer = []
            for p in range(PARTS):
                got = outer_call(p, new_outer[-1] if p else None)
                new_outer.append(got[0])
                if p == 0:
                    new_strip_out = got[1]
            made = inner_call(new_outer[-1])
            across = [across_chips(x) for x in new_outer]
            partner = [within_chip(x) for x in made[1:-1]]
            inner, strip_in = made[0], made[-1]
            outer, strip_out = new_outer, new_strip_out


def solution(mesh):
    placed = (
        P(None, None, "theta", "groups", None),
        P(None, None, "theta", "groups", None),
        P(None, "theta", "groups", None),
        P(),
        P("groups"),
    )
    return jax.shard_map(
        per_device,
        mesh=mesh,
        in_specs=placed,
        out_specs=P(None, None, "theta", "groups", None),
        check_vma=False,
    )
```

profile of v0, /device:TPU:1, one launch (start us, length us, event | category | flops | bytes accessed | tf_op | source)
XLA Modules:
  0.0 130.4 jit_solution(447794611378255652)
XLA Ops:
  0.0 1.3 %slice-done = f32[5,2,4,64,128]{4,3,2,1,0:T(8,128)S(1)} async-done(((f32[5,2,4,128,128]{4,3,2,1,0:T(8,128)}), f32[5,2,4,64,128]{4,3,2,1,0:T(8,128)S(1)}, s32[]{:S(2)}) %slice-start) | async-done | bytes 1310744 | tf_op jit(solution)/shard_map/slice | solution.py:540
  2.1 2.6 %collective-permute-start.64 = (f32[640,128]{1,0:T(8,128)}, f32[640,128]{1,0:T(8,128)}, u32[]{:S(2)}, u32[]{:S(2)}) collective-permute-start(f32[640,128]{1,0:T(8,128)} %bitcast.1), channel_id=1, source_target_pairs={{0,15},{1,2},{2,1},{3,4},{4,3},{5,6},{6,5},{7,8},{8,7},{9,10},{10,... | collective-permute-start | bytes 983048 | tf_op jit(solution)/shard_map/ppermute | solution.py:504
  5.0 1.7 %copy-done = f32[5,2,4,128,128]{4,3,2,1,0:T(8,128)S(1)} copy-done((f32[5,2,4,128,128]{4,3,2,1,0:T(8,128)S(1)}, f32[5,2,4,128,128]{4,3,2,1,0:T(8,128)}, u32[]{:S(2)}) %copy-start) | copy-done | bytes 2621464
  6.7 1.7 %copy-done.2 = f32[5,2,4,128,128]{4,3,2,1,0:T(8,128)S(1)} copy-done((f32[5,2,4,128,128]{4,3,2,1,0:T(8,128)S(1)}, f32[5,2,4,128,128]{4,3,2,1,0:T(8,128)}, u32[]{:S(2)}) %copy-start.2) | copy-done | bytes 2621464
  8.4 1.0 copy-done.4
  9.5 3.3 %gather_strips.1 = (f32[288,128]{1,0:T(8,128)}, f32[288,128]{1,0:T(8,128)}, f32[1280,128]{1,0:T(8,128)}, f32[640,128]{1,0:T(8,128)S(1)}, f32[640,128]{1,0:T(8,12...) custom-call(f32[16]{0:T(128)S(1)} %concatenate.7.refs_0_, ...), custom_call_target="tpu_custom_call" | custom-call | flops 1 | bytes 1 | tf_op jit(solution)/shard_map/gather_strips/pallas_call | solution.py:452
  14.2 2.9 %collective-permute-start.66 = (f32[288,128]{1,0:T(8,128)}, f32[288,128]{1,0:T(8,128)}, u32[]{:S(2)}, u32[]{:S(2)}) collective-permute-start(f32[288,128]{1,0:T(8,128)} %get-tuple-element.266.refs_2_), channel_id=1, source_target_pairs={{0,15},{1,0},{2,1},{3,2},{4,3},{5,4},{6,5},{7,6},{8,7},{9,8},{10,9... | collective-permute-start | bytes 442376 | tf_op jit(solution)/shard_map/ppermute | solution.py:498
  19.1 1.9 %align_strips.1 = (f32[320,128]{1,0:T(8,128)}, f32[320,128]{1,0:T(8,128)}) custom-call(s32[1]{0:T(128)} %bitcast.2.refs_0_, f32[288,128]{1,0:T(8,128)} %get-tuple-element.265.refs_1_, f32[288,128]{1,0:T(8,128)} %get-tuple-element.266.refs_2_, f32[288,128]{1,0:T(8,128)} %collective-permute-done.65.refs_3_, f32[288,128]{1,0:T(8,128)} %collective-permute-done.66.refs_4_), custom_call_target="tpu_custom_call" | custom-call | flops 1 | bytes 1 | tf_op jit(solution)/shard_map/align_strips/pallas_call | solution.py:452
  21.0 19.7 %conditional.1 = (f32[640,128]{1,0:T(8,128)}, f32[1280,128]{1,0:T(8,128)}, f32[320,128]{1,0:T(8,128)}, f32[320,128]{1,0:T(8,128)}) conditional(s32[]{:T(128)} %clamp.3, (f32[640,128]{1,0:T(8,128)S(1)}, f32[1280,128]{1,0:T(8,128)}, f32[320,128]{1,0:T(8,128)}, f32[320,128]{1,0:T(8,128)}) %tuple.71, ...), branch_computations={%region_0.1_spmd, %region_1.2_spmd, %region_2.3_spmd, %region_3.4_... | conditional | bytes 5243072 | solution.py:522
  21.0 5.6 %collective-permute-start.21 = (f32[1280,128]{1,0:T(8,128)}, f32[1280,128]{1,0:T(8,128)}, u32[]{:S(2)}, u32[]{:S(2)}) collective-permute-start(f32[1280,128]{1,0:T(8,128)} %get-tuple-element.154), channel_id=1, source_target_pairs={{0,1},{1,0},{2,3},{3,2},{4,5},{5,4},{6,7},{7,6},{8,9},{9,8},{10,11... | collective-permute-start | bytes 1966088 | tf_op jit(solution)/shard_map/cond/branch_5_fun/ppermute | solution.py:509
  26.6 3.5 %collective-permute-start.23 = (f32[320,128]{1,0:T(8,128)}, f32[320,128]{1,0:T(8,128)}, u32[]{:S(2)}, u32[]{:S(2)}) collective-permute-start(f32[320,128]{1,0:T(8,128)} %get-tuple-element.156), channel_id=1, source_target_pairs={{0,11},{1,12},{2,13},{3,14},{4,15},{5,0},{6,1},{7,2},{8,3},{9,4},{... | collective-permute-start | bytes 491528 | tf_op jit(solution)/shard_map/cond/branch_5_fun/ppermute | solution.py:498
  30.1 8.7 %collective-permute-done.22 = f32[320,128]{1,0:T(8,128)} collective-permute-done((f32[320,128]{1,0:T(8,128)}, f32[320,128]{1,0:T(8,128)}, u32[]{:S(2)}, u32[]{:S(2)}) %collective-permute-start.22) | collective-permute-done | bytes 163872 | tf_op jit(solution)/shard_map/cond/branch_5_fun/ppermute | solution.py:498
  38.8 1.9 %collective-permute-done.23 = f32[320,128]{1,0:T(8,128)} collective-permute-done((f32[320,128]{1,0:T(8,128)}, f32[320,128]{1,0:T(8,128)}, u32[]{:S(2)}, u32[]{:S(2)}) %collective-permute-start.23) | collective-permute-done | bytes 163872 | tf_op jit(solution)/shard_map/cond/branch_5_fun/ppermute | solution.py:498
  40.7 1.1 scatter_strips.1
  41.8 1.0 copy-done.9
  42.7 1.7 %outer.12 = (f32[680,128]{1,0:T(8,128)S(1)}, f32[2,5,8,128]{3,2,1,0:T(8,128)S(1)}) custom-call(f32[16]{0:T(128)S(1)} %concatenate.7.refs_0_, f32[2,128,128]{2,1,0:T(8,128)S(1)} %get-tuple-element.260.refs_1_, f32[640,128]{1,0:T(8,128)S(1)} %copy-done.9, f32[5,2,4,128,128]{4,3,2,1,0:T(8,128)S(1)} %copy-done.1, ...), custom_call_target="tpu_custom_call" | custom-call | flops 1 | bytes 1 | tf_op jit(solution)/shard_map/outer/pallas_call | solution.py:452
  45.0 1.6 %outer.13.refs_16_.refs_6_.refs_7_ = f32[640,128]{1,0:T(8,128)S(1)} custom-call(f32[16]{0:T(128)S(1)} %concatenate.7.refs_0_, f32[2,128,128]{2,1,0:T(8,128)S(1)} %get-tuple-element.260.refs_1_, f32[640,128]{1,0:T(8,128)S(1)} %copy-done.7, f32[5,2,4,128,128]{4,3,2,1,0:T(8,128)S(1)} %copy-done.1, ...), custom_call_target="tpu_custom_call" | custom-call | flops 1 | bytes 1 | tf_op jit(solution)/shard_map/outer/pallas_call | solution.py:452
  46.6 1.3 collective-permute-start.71
  47.9 3.9 %inner.6 = (f32[5,2,3,128,128]{4,3,2,1,0:T(8,128)S(1)}, f32[320,128]{1,0:T(8,128)S(1)}, f32[320,128]{1,0:T(8,128)S(1)}, f32[320,128]{1,0:T(8,128)S(1)}, f32[360,...) custom-call(f32[16]{0:T(128)S(1)} %concatenate.7.refs_0_, f32[2,4,128,128]{3,2,1,0:T(8,128)S(1)} %copy-done.5, ...), custom_call_target="tpu_custom_call" | custom-call | flops 1 | bytes 1 | tf_op jit(solution)/shard_map/inner/pallas_call | solution.py:452
  51.8 4.8 %collective-permute-done.72.refs_9_ = f32[680,128]{1,0:T(8,128)S(1)} collective-permute-done((f32[680,128]{1,0:T(8,128)S(1)}, f32[680,128]{1,0:T(8,128)S(1)}, u32[]{:S(2)}, u32[]{:S(2)}) %collective-permute-start.72) | collective-permute-done | bytes 348192 | tf_op jit(solution)/shard_map/ppermute | solution.py:504
  56.5 1.2 outer.14
  57.7 2.5 %collective-permute-start.78 = (f32[680,128]{1,0:T(8,128)S(1)}, f32[680,128]{1,0:T(8,128)S(1)}, u32[]{:S(2)}, u32[]{:S(2)}) collective-permute-start(f32[680,128]{1,0:T(8,128)S(1)} %get-tuple-element.291.refs_10_.refs_5_.refs_6_), channel_id=1, source_target_pairs={{0,15},{1,2},{2,1},{3,4},{4,3},{5,6},{6,5},{7,8},{8,7},{9,10},{10,... | collective-permute-start | bytes 1044488 | tf_op jit(solution)/shard_map/ppermute | solution.py:504
  60.8 3.0 %collective-permute-done.71.refs_9_ = f32[640,128]{1,0:T(8,128)S(1)} collective-permute-done((f32[640,128]{1,0:T(8,128)S(1)}, f32[640,128]{1,0:T(8,128)S(1)}, u32[]{:S(2)}, u32[]{:S(2)}) %collective-permute-start.71) | collective-permute-done | bytes 327712 | tf_op jit(solution)/shard_map/ppermute | solution.py:504
  63.8 1.0 outer.15.refs_18_.refs_6_.refs_7_
  64.8 2.5 %collective-permute-start.77 = (f32[640,128]{1,0:T(8,128)S(1)}, f32[640,128]{1,0:T(8,128)S(1)}, u32[]{:S(2)}, u32[]{:S(2)}) collective-permute-start(f32[640,128]{1,0:T(8,128)S(1)} %outer.15.refs_18_.refs_6_.refs_7_), channel_id=1, source_target_pairs={{0,15},{1,2},{2,1},{3,4},{4,3},{5,6},{6,5},{7,8},{8,7},{9,10},{10,... | collective-permute-start | bytes 983048 | tf_op jit(solution)/shard_map/ppermute | solution.py:504
  67.3 3.6 %inner.7 = (f32[5,2,3,128,128]{4,3,2,1,0:T(8,128)S(1)}, f32[320,128]{1,0:T(8,128)S(1)}, f32[320,128]{1,0:T(8,128)S(1)}, f32[320,128]{1,0:T(8,128)S(1)}, f32[360,...) custom-call(f32[16]{0:T(128)S(1)} %concatenate.7.refs_0_, f32[2,4,128,128]{3,2,1,0:T(8,128)S(1)} %copy-done.5, ...), custom_call_target="tpu_custom_call" | custom-call | flops 1 | bytes 1 | tf_op jit(solution)/shard_map/inner/pallas_call | solution.py:452
  70.9 1.3 outer.16
  72.5 4.2 %collective-permute-start.73 = (f32[320,128]{1,0:T(8,128)S(1)}, f32[320,128]{1,0:T(8,128)S(1)}, u32[]{:S(2)}, u32[]{:S(2)}) collective-permute-start(f32[320,128]{1,0:T(8,128)S(1)} %get-tuple-element.294), channel_id=1, source_target_pairs={{0,1},{1,0},{2,3},{3,2},{4,5},{5,4},{6,7},{7,6},{8,9},{9,8},{10,11... | collective-permute-start | bytes 491528 | tf_op jit(solution)/shard_map/ppermute | solution.py:509
  77.3 1.0 outer.17.refs_18_.refs_6_.refs_8_.refs_7_
  78.6 3.8 %inner.8 = (f32[5,2,3,128,128]{4,3,2,1,0:T(8,128)S(1)}, f32[320,128]{1,0:T(8,128)S(1)}, f32[320,128]{1,0:T(8,128)S(1)}, f32[320,128]{1,0:T(8,128)S(1)}, f32[360,...) custom-call(f32[16]{0:T(128)S(1)} %concatenate.7.refs_0_, f32[2,4,128,128]{3,2,1,0:T(8,128)S(1)} %copy-done.5, ...), custom_call_target="tpu_custom_call" | custom-call | flops 1 | bytes 1 | tf_op jit(solution)/shard_map/inner/pallas_call | solution.py:452
  82.4 1.3 outer.18
  83.7 2.4 %collective-permute-start.90 = (f32[680,128]{1,0:T(8,128)S(1)}, f32[680,128]{1,0:T(8,128)S(1)}, u32[]{:S(2)}, u32[]{:S(2)}) collective-permute-start(f32[680,128]{1,0:T(8,128)S(1)} %get-tuple-element.307.refs_10_.refs_5_.refs_6_), channel_id=1, source_target_pairs={{0,15},{1,2},{2,1},{3,4},{4,3},{5,6},{6,5},{7,8},{8,7},{9,10},{10,... | collective-permute-start | bytes 1044488 | tf_op jit(solution)/shard_map/ppermute | solution.py:504
  86.1 3.8 %collective-permute-start.79 = (f32[320,128]{1,0:T(8,128)S(1)}, f32[320,128]{1,0:T(8,128)S(1)}, u32[]{:S(2)}, u32[]{:S(2)}) collective-permute-start(f32[320,128]{1,0:T(8,128)S(1)} %get-tuple-element.302), channel_id=1, source_target_pairs={{0,1},{1,0},{2,3},{3,2},{4,5},{5,4},{6,7},{7,6},{8,9},{9,8},{10,11... | collective-permute-start | bytes 491528 | tf_op jit(solution)/shard_map/ppermute | solution.py:509
  90.4 1.7 %collective-permute-done.83.refs_9_ = f32[640,128]{1,0:T(8,128)S(1)} collective-permute-done((f32[640,128]{1,0:T(8,128)S(1)}, f32[640,128]{1,0:T(8,128)S(1)}, u32[]{:S(2)}, u32[]{:S(2)}) %collective-permute-start.83) | collective-permute-done | bytes 327712 | tf_op jit(solution)/shard_map/ppermute | solution.py:504
  92.1 1.0 outer.19.refs_18_.refs_6_.refs_7_
  93.5 3.6 %inner.9 = (f32[5,2,3,128,128]{4,3,2,1,0:T(8,128)S(1)}, f32[320,128]{1,0:T(8,128)S(1)}, f32[320,128]{1,0:T(8,128)S(1)}, f32[320,128]{1,0:T(8,128)S(1)}, f32[360,...) custom-call(f32[16]{0:T(128)S(1)} %concatenate.7.refs_0_, f32[2,4,128,128]{3,2,1,0:T(8,128)S(1)} %copy-done.5, ...), custom_call_target="tpu_custom_call" | custom-call | flops 1 | bytes 1 | tf_op jit(solution)/shard_map/inner/pallas_call | solution.py:452
  97.1 6.0 %collective-permute-start.88 = (f32[360,128]{1,0:T(8,128)S(1)}, f32[360,128]{1,0:T(8,128)S(1)}, u32[]{:S(2)}, u32[]{:S(2)}) collective-permute-start(f32[360,128]{1,0:T(8,128)S(1)} %get-tuple-element.313), channel_id=1, source_target_pairs={{0,1},{1,0},{2,3},{3,2},{4,5},{5,4},{6,7},{7,6},{8,9},{9,8},{10,11... | collective-permute-start | bytes 552968 | tf_op jit(solution)/shard_map/ppermute | solution.py:509
  103.7 1.2 outer.20
  104.9 1.6 %collective-permute-done.89.refs_9_ = f32[640,128]{1,0:T(8,128)S(1)} collective-permute-done((f32[640,128]{1,0:T(8,128)S(1)}, f32[640,128]{1,0:T(8,128)S(1)}, u32[]{:S(2)}, u32[]{:S(2)}) %collective-permute-start.89) | collective-permute-done | bytes 327712 | tf_op jit(solution)/shard_map/ppermute | solution.py:504
  106.6 1.0 outer.21.refs_18_.refs_7_.refs_6_
  107.7 3.6 %inner.10 = (f32[5,2,3,128,128]{4,3,2,1,0:T(8,128)S(1)}, f32[320,128]{1,0:T(8,128)S(1)}, f32[320,128]{1,0:T(8,128)S(1)}, f32[320,128]{1,0:T(8,128)S(1)}, f32[320...) custom-call(f32[16]{0:T(128)S(1)} %concatenate.7.refs_0_, f32[2,4,128,128]{3,2,1,0:T(8,128)S(1)} %copy-done.5, ...), custom_call_target="tpu_custom_call" | custom-call | flops 1 | bytes 1 | tf_op jit(solution)/shard_map/inner/pallas_call | solution.py:452
  111.4 1.7 %collective-permute-start.91 = (f32[640,128]{1,0:T(8,128)S(1)}, f32[640,128]{1,0:T(8,128)S(1)}, u32[]{:S(2)}, u32[]{:S(2)}) collective-permute-start(f32[640,128]{1,0:T(8,128)S(1)} %outer.21.refs_18_.refs_7_.refs_6_), channel_id=1, source_target_pairs={{0,15},{1,2},{2,1},{3,4},{4,3},{5,6},{6,5},{7,8},{8,7},{9,10},{10,... | collective-permute-start | bytes 983048 | tf_op jit(solution)/shard_map/ppermute | solution.py:504
  113.1 3.1 %collective-permute-start.94 = (f32[320,128]{1,0:T(8,128)S(1)}, f32[320,128]{1,0:T(8,128)S(1)}, u32[]{:S(2)}, u32[]{:S(2)}) collective-permute-start(f32[320,128]{1,0:T(8,128)S(1)} %get-tuple-element.320), channel_id=1, source_target_pairs={{0,1},{1,0},{2,3},{3,2},{4,5},{5,4},{6,7},{7,6},{8,9},{9,8},{10,11... | collective-permute-start | bytes 491528 | tf_op jit(solution)/shard_map/ppermute | solution.py:509
  117.9 3.9 %inner.11.refs_10_ = f32[5,2,4,128,128]{4,3,2,1,0:T(8,128)} custom-call(f32[16]{0:T(128)S(1)} %concatenate.7.refs_0_, f32[2,4,128,128]{3,2,1,0:T(8,128)S(1)} %copy-done.5, f32[5,2,4,128,128]{4,3,2,1,0:T(8,128)S(1)} %copy-done.3, f32[5,2,4,128,128]{4,3,2,1,0:T(8,128)S(1)} %copy-done.1, f32[5,2,3,128,128]{4,3,2,1,0:T(8,128)S(1)} %get-tuple-element.316.refs_4_.refs_3_, ...), custom_call_target="tpu_custom_call" | custom-call | flops 1 | bytes 1 | tf_op jit(solution)/shard_map/inner/pallas_call | solution.py:452
  121.8 3.1 %collective-permute-done.92.refs_9_ = f32[640,128]{1,0:T(8,128)S(1)} collective-permute-done((f32[640,128]{1,0:T(8,128)S(1)}, f32[640,128]{1,0:T(8,128)S(1)}, u32[]{:S(2)}, u32[]{:S(2)}) %collective-permute-start.92) | collective-permute-done | bytes 327712 | tf_op jit(solution)/shard_map/ppermute | solution.py:504
  124.9 1.8 %outer.22.refs_10_ = f32[5,2,4,128,128]{4,3,2,1,0:T(8,128)} custom-call(f32[16]{0:T(128)S(1)} %concatenate.7.refs_0_, f32[2,128,128]{2,1,0:T(8,128)S(1)} %get-tuple-element.260.refs_1_, f32[640,128]{1,0:T(8,128)S(1)} %copy-done.10, f32[5,2,3,128,128]{4,3,2,1,0:T(8,128)S(1)} %get-tuple-element.316.refs_4_.refs_3_, ...), custom_call_target="tpu_custom_call", output_to_operand_aliasing={{}: (10, {})} | custom-call | flops 1 | bytes 1 | tf_op jit(solution)/shard_map/outer/pallas_call | solution.py:452
  126.7 1.7 %collective-permute-done.91.refs_9_ = f32[640,128]{1,0:T(8,128)S(1)} collective-permute-done((f32[640,128]{1,0:T(8,128)S(1)}, f32[640,128]{1,0:T(8,128)S(1)}, u32[]{:S(2)}, u32[]{:S(2)}) %collective-permute-start.91) | collective-permute-done | bytes 327712 | tf_op jit(solution)/shard_map/ppermute | solution.py:504
  128.4 1.8 %outer.23 = f32[5,2,4,128,128]{4,3,2,1,0:T(8,128)} custom-call(f32[16]{0:T(128)S(1)} %concatenate.7.refs_0_, f32[2,128,128]{2,1,0:T(8,128)S(1)} %get-tuple-element.260.refs_1_, f32[640,128]{1,0:T(8,128)S(1)} %copy-done.7, f32[5,2,3,128,128]{4,3,2,1,0:T(8,128)S(1)} %get-tuple-element.316.refs_4_.refs_3_, ...), custom_call_target="tpu_custom_call", output_to_operand_aliasing={{}: (10, {})} | custom-call | flops 1 | bytes 1 | tf_op jit(solution)/shard_map/outer/pallas_call | solution.py:452
  (79 shorter events, 9.5 us)
Async XLA Ops:
  0.0 1.3 %slice-start = ((f32[5,2,4,128,128]{4,3,2,1,0:T(8,128)}), f32[5,2,4,64,128]{4,3,2,1,0:T(8,128)S(1)}, s32[]{:S(2)}) async-start(f32[5,2,4,128,128]{4,3,2,1,0:T(8,128)} %refs_3_.17), calls=%async_computation | async-start | bytes 2621440 | tf_op jit(solution)/shard_map/slice | solution.py:540
  0.0 4.7 %copy-start.11 = (f32[2,4]{1,0:T(2,128)S(1)}, f32[2,4]{1,0:T(2,128)}, u32[]{:S(2)}) copy-start(f32[2,4]{1,0:T(2,128)} %param.24) | copy-start | bytes 100
  2.1 18.9 %collective-permute-start.64 = (f32[640,128]{1,0:T(8,128)}, f32[640,128]{1,0:T(8,128)}, u32[]{:S(2)}, u32[]{:S(2)}) collective-permute-start(f32[640,128]{1,0:T(8,128)} %bitcast.1), channel_id=1, source_target_pairs={{0,15},{1,2},{2,1},{3,4},{4,3},{5,6},{6,5},{7,8},{8,7},{9,10},{10,... | collective-permute-start | bytes 983048 | tf_op jit(solution)/shard_map/ppermute | solution.py:504
  4.9 1.7 %copy-start = (f32[5,2,4,128,128]{4,3,2,1,0:T(8,128)S(1)}, f32[5,2,4,128,128]{4,3,2,1,0:T(8,128)}, u32[]{:S(2)}) copy-start(f32[5,2,4,128,128]{4,3,2,1,0:T(8,128)} %refs_3_.17) | copy-start | bytes 7864324
  6.7 1.7 %copy-start.2 = (f32[5,2,4,128,128]{4,3,2,1,0:T(8,128)S(1)}, f32[5,2,4,128,128]{4,3,2,1,0:T(8,128)}, u32[]{:S(2)}) copy-start(f32[5,2,4,128,128]{4,3,2,1,0:T(8,128)} %refs_2_.13) | copy-start | bytes 7864324
  8.4 1.0 copy-start.4
  9.5 32.3 %copy-start.1 = (f32[5,2,4,128,128]{4,3,2,1,0:T(8,128)S(1)}, f32[5,2,4,128,128]{4,3,2,1,0:T(8,128)}, u32[]{:S(2)}) copy-start(f32[5,2,4,128,128]{4,3,2,1,0:T(8,128)} %refs_3_.17) | copy-start | bytes 7864324
  14.2 4.1 %collective-permute-start.65 = (f32[288,128]{1,0:T(8,128)}, f32[288,128]{1,0:T(8,128)}, u32[]{:S(2)}, u32[]{:S(2)}) collective-permute-start(f32[288,128]{1,0:T(8,128)} %get-tuple-element.265.refs_1_), channel_id=1, source_target_pairs={{0,1},{1,2},{2,3},{3,4},{4,5},{5,6},{6,7},{7,8},{8,9},{9,10},{10,1... | collective-permute-start | bytes 442376 | tf_op jit(solution)/shard_map/ppermute | solution.py:498
  14.2 4.9 %collective-permute-start.66 = (f32[288,128]{1,0:T(8,128)}, f32[288,128]{1,0:T(8,128)}, u32[]{:S(2)}, u32[]{:S(2)}) collective-permute-start(f32[288,128]{1,0:T(8,128)} %get-tuple-element.266.refs_2_), channel_id=1, source_target_pairs={{0,15},{1,0},{2,1},{3,2},{4,3},{5,4},{6,5},{7,6},{8,7},{9,8},{10,9... | collective-permute-start | bytes 442376 | tf_op jit(solution)/shard_map/ppermute | solution.py:498
  21.0 19.7 %collective-permute-start.21 = (f32[1280,128]{1,0:T(8,128)}, f32[1280,128]{1,0:T(8,128)}, u32[]{:S(2)}, u32[]{:S(2)}) collective-permute-start(f32[1280,128]{1,0:T(8,128)} %get-tuple-element.154), channel_id=1, source_target_pairs={{0,1},{1,0},{2,3},{3,2},{4,5},{5,4},{6,7},{7,6},{8,9},{9,8},{10,11... | collective-permute-start | bytes 1966088 | tf_op jit(solution)/shard_map/cond/branch_5_fun/ppermute | solution.py:509
  26.6 14.1 %collective-permute-start.20 = (f32[640,128]{1,0:T(8,128)S(1)}, f32[640,128]{1,0:T(8,128)}, u32[]{:S(2)}, u32[]{:S(2)}) collective-permute-start(f32[640,128]{1,0:T(8,128)S(1)} %get-tuple-element.153), channel_id=1, source_target_pairs={{0,15},{1,2},{2,1},{3,4},{4,3},{5,6},{6,5},{7,8},{8,7},{9,10},{10,... | collective-permute-start | bytes 983048 | tf_op jit(solution)/shard_map/cond/branch_5_fun/ppermute | solution.py:504
  26.6 12.2 %collective-permute-start.22 = (f32[320,128]{1,0:T(8,128)}, f32[320,128]{1,0:T(8,128)}, u32[]{:S(2)}, u32[]{:S(2)}) collective-permute-start(f32[320,128]{1,0:T(8,128)} %get-tuple-element.155), channel_id=1, source_target_pairs={{0,5},{1,6},{2,7},{3,8},{4,9},{5,10},{6,11},{7,12},{8,13},{9,14},{... | collective-permute-start | bytes 491528 | tf_op jit(solution)/shard_map/cond/branch_5_fun/ppermute | solution.py:498
  26.6 14.1 %collective-permute-start.23 = (f32[320,128]{1,0:T(8,128)}, f32[320,128]{1,0:T(8,128)}, u32[]{:S(2)}, u32[]{:S(2)}) collective-permute-start(f32[320,128]{1,0:T(8,128)} %get-tuple-element.156), channel_id=1, source_target_pairs={{0,11},{1,12},{2,13},{3,14},{4,15},{5,0},{6,1},{7,2},{8,3},{9,4},{... | collective-permute-start | bytes 491528 | tf_op jit(solution)/shard_map/cond/branch_5_fun/ppermute | solution.py:498
  41.8 1.0 copy-start.9
  42.7 2.3 %copy-start.7 = (f32[640,128]{1,0:T(8,128)S(1)}, f32[640,128]{1,0:T(8,128)}, u32[]{:S(2)}) copy-start(f32[640,128]{1,0:T(8,128)} %copy-done.6) | copy-start | bytes 983044
  44.4 12.1 %collective-permute-start.72 = (f32[680,128]{1,0:T(8,128)S(1)}, f32[680,128]{1,0:T(8,128)S(1)}, u32[]{:S(2)}, u32[]{:S(2)}) collective-permute-start(f32[680,128]{1,0:T(8,128)S(1)} %get-tuple-element.283.refs_10_.refs_5_.refs_6_), channel_id=1, source_target_pairs={{0,15},{1,2},{2,1},{3,4},{4,3},{5,6},{6,5},{7,8},{8,7},{9,10},{10,... | collective-permute-start | bytes 1044488 | tf_op jit(solution)/shard_map/ppermute | solution.py:504
  45.0 2.8 %copy-start.3 = (f32[5,2,4,128,128]{4,3,2,1,0:T(8,128)S(1)}, f32[5,2,4,128,128]{4,3,2,1,0:T(8,128)}, u32[]{:S(2)}) copy-start(f32[5,2,4,128,128]{4,3,2,1,0:T(8,128)} %refs_2_.13) | copy-start | bytes 7864324
  45.0 2.8 %copy-start.5 = (f32[2,4,128,128]{3,2,1,0:T(8,128)S(1)}, f32[2,4,128,128]{3,2,1,0:T(8,128)}, u32[]{:S(2)}) copy-start(f32[2,4,128,128]{3,2,1,0:T(8,128)} %refs_1_.13) | copy-start | bytes 1572868
  46.6 17.2 %collective-permute-start.71 = (f32[640,128]{1,0:T(8,128)S(1)}, f32[640,128]{1,0:T(8,128)S(1)}, u32[]{:S(2)}, u32[]{:S(2)}) collective-permute-start(f32[640,128]{1,0:T(8,128)S(1)} %outer.13.refs_16_.refs_6_.refs_7_), channel_id=1, source_target_pairs={{0,15},{1,2},{2,1},{3,4},{4,3},{5,6},{6,5},{7,8},{8,7},{9,10},{10,... | collective-permute-start | bytes 983048 | tf_op jit(solution)/shard_map/ppermute | solution.py:504
  47.9 8.7 %copy-start.10 = (f32[640,128]{1,0:T(8,128)S(1)}, f32[640,128]{1,0:T(8,128)}, u32[]{:S(2)}) copy-start(f32[640,128]{1,0:T(8,128)} %copy-done.8) | copy-start | bytes 983044
  57.7 13.2 %collective-permute-start.78 = (f32[680,128]{1,0:T(8,128)S(1)}, f32[680,128]{1,0:T(8,128)S(1)}, u32[]{:S(2)}, u32[]{:S(2)}) collective-permute-start(f32[680,128]{1,0:T(8,128)S(1)} %get-tuple-element.291.refs_10_.refs_5_.refs_6_), channel_id=1, source_target_pairs={{0,15},{1,2},{2,1},{3,4},{4,3},{5,6},{6,5},{7,8},{8,7},{9,10},{10,... | collective-permute-start | bytes 1044488 | tf_op jit(solution)/shard_map/ppermute | solution.py:504
  60.3 4.5 %collective-permute-start.67 = (f32[320,128]{1,0:T(8,128)S(1)}, f32[320,128]{1,0:T(8,128)S(1)}, u32[]{:S(2)}, u32[]{:S(2)}) collective-permute-start(f32[320,128]{1,0:T(8,128)S(1)} %get-tuple-element.286), channel_id=1, source_target_pairs={{0,1},{1,0},{2,3},{3,2},{4,5},{5,4},{6,7},{7,6},{8,9},{9,8},{10,11... | collective-permute-start | bytes 491528 | tf_op jit(solution)/shard_map/ppermute | solution.py:509
  60.3 7.0 %collective-permute-start.70 = (f32[360,128]{1,0:T(8,128)S(1)}, f32[360,128]{1,0:T(8,128)S(1)}, u32[]{:S(2)}, u32[]{:S(2)}) collective-permute-start(f32[360,128]{1,0:T(8,128)S(1)} %get-tuple-element.289), channel_id=1, source_target_pairs={{0,1},{1,0},{2,3},{3,2},{4,5},{5,4},{6,7},{7,6},{8,9},{9,8},{10,11... | collective-permute-start | bytes 552968 | tf_op jit(solution)/shard_map/ppermute | solution.py:509
  60.8 6.5 %collective-permute-start.68 = (f32[320,128]{1,0:T(8,128)S(1)}, f32[320,128]{1,0:T(8,128)S(1)}, u32[]{:S(2)}, u32[]{:S(2)}) collective-permute-start(f32[320,128]{1,0:T(8,128)S(1)} %get-tuple-element.287), channel_id=1, source_target_pairs={{0,1},{1,0},{2,3},{3,2},{4,5},{5,4},{6,7},{7,6},{8,9},{9,8},{10,11... | collective-permute-start | bytes 491528 | tf_op jit(solution)/shard_map/ppermute | solution.py:509
  63.8 3.6 %collective-permute-start.69 = (f32[320,128]{1,0:T(8,128)S(1)}, f32[320,128]{1,0:T(8,128)S(1)}, u32[]{:S(2)}, u32[]{:S(2)}) collective-permute-start(f32[320,128]{1,0:T(8,128)S(1)} %get-tuple-element.288), channel_id=1, source_target_pairs={{0,1},{1,0},{2,3},{3,2},{4,5},{5,4},{6,7},{7,6},{8,9},{9,8},{10,11... | collective-permute-start | bytes 491528 | tf_op jit(solution)/shard_map/ppermute | solution.py:509
  64.8 12.5 %collective-permute-start.77 = (f32[640,128]{1,0:T(8,128)S(1)}, f32[640,128]{1,0:T(8,128)S(1)}, u32[]{:S(2)}, u32[]{:S(2)}) collective-permute-start(f32[640,128]{1,0:T(8,128)S(1)} %outer.15.refs_18_.refs_6_.refs_7_), channel_id=1, source_target_pairs={{0,15},{1,2},{2,1},{3,4},{4,3},{5,6},{6,5},{7,8},{8,7},{9,10},{10,... | collective-permute-start | bytes 983048 | tf_op jit(solution)/shard_map/ppermute | solution.py:504
  72.2 10.2 %collective-permute-start.84 = (f32[680,128]{1,0:T(8,128)S(1)}, f32[680,128]{1,0:T(8,128)S(1)}, u32[]{:S(2)}, u32[]{:S(2)}) collective-permute-start(f32[680,128]{1,0:T(8,128)S(1)} %get-tuple-element.299.refs_10_.refs_5_.refs_8_.refs_6_), channel_id=1, source_target_pairs={{0,15},{1,2},{2,1},{3,4},{4,3},{5,6},{6,5},{7,8},{8,7},{9,10},{10,... | collective-permute-start | bytes 1044488 | tf_op jit(solution)/shard_map/ppermute | solution.py:504
  72.5 5.8 %collective-permute-start.73 = (f32[320,128]{1,0:T(8,128)S(1)}, f32[320,128]{1,0:T(8,128)S(1)}, u32[]{:S(2)}, u32[]{:S(2)}) collective-permute-start(f32[320,128]{1,0:T(8,128)S(1)} %get-tuple-element.294), channel_id=1, source_target_pairs={{0,1},{1,0},{2,3},{3,2},{4,5},{5,4},{6,7},{7,6},{8,9},{9,8},{10,11... | collective-permute-start | bytes 491528 | tf_op jit(solution)/shard_map/ppermute | solution.py:509
  76.7 1.9 %collective-permute-start.76 = (f32[360,128]{1,0:T(8,128)S(1)}, f32[360,128]{1,0:T(8,128)S(1)}, u32[]{:S(2)}, u32[]{:S(2)}) collective-permute-start(f32[360,128]{1,0:T(8,128)S(1)} %get-tuple-element.297), channel_id=1, source_target_pairs={{0,1},{1,0},{2,3},{3,2},{4,5},{5,4},{6,7},{7,6},{8,9},{9,8},{10,11... | collective-permute-start | bytes 552968 | tf_op jit(solution)/shard_map/ppermute | solution.py:509
  76.8 1.6 %collective-permute-start.74 = (f32[320,128]{1,0:T(8,128)S(1)}, f32[320,128]{1,0:T(8,128)S(1)}, u32[]{:S(2)}, u32[]{:S(2)}) collective-permute-start(f32[320,128]{1,0:T(8,128)S(1)} %get-tuple-element.295), channel_id=1, source_target_pairs={{0,1},{1,0},{2,3},{3,2},{4,5},{5,4},{6,7},{7,6},{8,9},{9,8},{10,11... | collective-permute-start | bytes 491528 | tf_op jit(solution)/shard_map/ppermute | solution.py:509
  77.2 1.4 %collective-permute-start.75 = (f32[320,128]{1,0:T(8,128)S(1)}, f32[320,128]{1,0:T(8,128)S(1)}, u32[]{:S(2)}, u32[]{:S(2)}) collective-permute-start(f32[320,128]{1,0:T(8,128)S(1)} %get-tuple-element.296), channel_id=1, source_target_pairs={{0,1},{1,0},{2,3},{3,2},{4,5},{5,4},{6,7},{7,6},{8,9},{9,8},{10,11... | collective-permute-start | bytes 491528 | tf_op jit(solution)/shard_map/ppermute | solution.py:509
  78.3 13.8 %collective-permute-start.83 = (f32[640,128]{1,0:T(8,128)S(1)}, f32[640,128]{1,0:T(8,128)S(1)}, u32[]{:S(2)}, u32[]{:S(2)}) collective-permute-start(f32[640,128]{1,0:T(8,128)S(1)} %outer.17.refs_18_.refs_6_.refs_8_.refs_7_), channel_id=1, source_target_pairs={{0,15},{1,2},{2,1},{3,4},{4,3},{5,6},{6,5},{7,8},{8,7},{9,10},{10,... | collective-permute-start | bytes 983048 | tf_op jit(solution)/shard_map/ppermute | solution.py:504
  83.7 19.9 %collective-permute-start.90 = (f32[680,128]{1,0:T(8,128)S(1)}, f32[680,128]{1,0:T(8,128)S(1)}, u32[]{:S(2)}, u32[]{:S(2)}) collective-permute-start(f32[680,128]{1,0:T(8,128)S(1)} %get-tuple-element.307.refs_10_.refs_5_.refs_6_), channel_id=1, source_target_pairs={{0,15},{1,2},{2,1},{3,4},{4,3},{5,6},{6,5},{7,8},{8,7},{9,10},{10,... | collective-permute-start | bytes 1044488 | tf_op jit(solution)/shard_map/ppermute | solution.py:504
  86.1 7.0 %collective-permute-start.79 = (f32[320,128]{1,0:T(8,128)S(1)}, f32[320,128]{1,0:T(8,128)S(1)}, u32[]{:S(2)}, u32[]{:S(2)}) collective-permute-start(f32[320,128]{1,0:T(8,128)S(1)} %get-tuple-element.302), channel_id=1, source_target_pairs={{0,1},{1,0},{2,3},{3,2},{4,5},{5,4},{6,7},{7,6},{8,9},{9,8},{10,11... | collective-permute-start | bytes 491528 | tf_op jit(solution)/shard_map/ppermute | solution.py:509
  89.9 3.6 %collective-permute-start.82 = (f32[360,128]{1,0:T(8,128)S(1)}, f32[360,128]{1,0:T(8,128)S(1)}, u32[]{:S(2)}, u32[]{:S(2)}) collective-permute-start(f32[360,128]{1,0:T(8,128)S(1)} %get-tuple-element.305), channel_id=1, source_target_pairs={{0,1},{1,0},{2,3},{3,2},{4,5},{5,4},{6,7},{7,6},{8,9},{9,8},{10,11... | collective-permute-start | bytes 552968 | tf_op jit(solution)/shard_map/ppermute | solution.py:509
  89.9 3.3 %collective-permute-start.80 = (f32[320,128]{1,0:T(8,128)S(1)}, f32[320,128]{1,0:T(8,128)S(1)}, u32[]{:S(2)}, u32[]{:S(2)}) collective-permute-start(f32[320,128]{1,0:T(8,128)S(1)} %get-tuple-element.303), channel_id=1, source_target_pairs={{0,1},{1,0},{2,3},{3,2},{4,5},{5,4},{6,7},{7,6},{8,9},{9,8},{10,11... | collective-permute-start | bytes 491528 | tf_op jit(solution)/shard_map/ppermute | solution.py:509
  92.1 1.4 %collective-permute-start.81 = (f32[320,128]{1,0:T(8,128)S(1)}, f32[320,128]{1,0:T(8,128)S(1)}, u32[]{:S(2)}, u32[]{:S(2)}) collective-permute-start(f32[320,128]{1,0:T(8,128)S(1)} %get-tuple-element.304), channel_id=1, source_target_pairs={{0,1},{1,0},{2,3},{3,2},{4,5},{5,4},{6,7},{7,6},{8,9},{9,8},{10,11... | collective-permute-start | bytes 491528 | tf_op jit(solution)/shard_map/ppermute | solution.py:509
  93.1 13.5 %collective-permute-start.89 = (f32[640,128]{1,0:T(8,128)S(1)}, f32[640,128]{1,0:T(8,128)S(1)}, u32[]{:S(2)}, u32[]{:S(2)}) collective-permute-start(f32[640,128]{1,0:T(8,128)S(1)} %outer.19.refs_18_.refs_6_.refs_7_), channel_id=1, source_target_pairs={{0,15},{1,2},{2,1},{3,4},{4,3},{5,6},{6,5},{7,8},{8,7},{9,10},{10,... | collective-permute-start | bytes 983048 | tf_op jit(solution)/shard_map/ppermute | solution.py:504
  97.1 10.6 %collective-permute-start.88 = (f32[360,128]{1,0:T(8,128)S(1)}, f32[360,128]{1,0:T(8,128)S(1)}, u32[]{:S(2)}, u32[]{:S(2)}) collective-permute-start(f32[360,128]{1,0:T(8,128)S(1)} %get-tuple-element.313), channel_id=1, source_target_pairs={{0,1},{1,0},{2,3},{3,2},{4,5},{5,4},{6,7},{7,6},{8,9},{9,8},{10,11... | collective-permute-start | bytes 552968 | tf_op jit(solution)/shard_map/ppermute | solution.py:509
  103.1 4.5 %collective-permute-start.85 = (f32[320,128]{1,0:T(8,128)S(1)}, f32[320,128]{1,0:T(8,128)S(1)}, u32[]{:S(2)}, u32[]{:S(2)}) collective-permute-start(f32[320,128]{1,0:T(8,128)S(1)} %get-tuple-element.310), channel_id=1, source_target_pairs={{0,1},{1,0},{2,3},{3,2},{4,5},{5,4},{6,7},{7,6},{8,9},{9,8},{10,11... | collective-permute-start | bytes 491528 | tf_op jit(solution)/shard_map/ppermute | solution.py:509
  103.2 4.4 %collective-permute-start.86 = (f32[320,128]{1,0:T(8,128)S(1)}, f32[320,128]{1,0:T(8,128)S(1)}, u32[]{:S(2)}, u32[]{:S(2)}) collective-permute-start(f32[320,128]{1,0:T(8,128)S(1)} %get-tuple-element.311), channel_id=1, source_target_pairs={{0,1},{1,0},{2,3},{3,2},{4,5},{5,4},{6,7},{7,6},{8,9},{9,8},{10,11... | collective-permute-start | bytes 491528 | tf_op jit(solution)/shard_map/ppermute | solution.py:509
  103.6 4.0 %collective-permute-start.87 = (f32[320,128]{1,0:T(8,128)S(1)}, f32[320,128]{1,0:T(8,128)S(1)}, u32[]{:S(2)}, u32[]{:S(2)}) collective-permute-start(f32[320,128]{1,0:T(8,128)S(1)} %get-tuple-element.312), channel_id=1, source_target_pairs={{0,1},{1,0},{2,3},{3,2},{4,5},{5,4},{6,7},{7,6},{8,9},{9,8},{10,11... | collective-permute-start | bytes 491528 | tf_op jit(solution)/shard_map/ppermute | solution.py:509
  111.2 5.0 %collective-permute-start.93 = (f32[320,128]{1,0:T(8,128)S(1)}, f32[320,128]{1,0:T(8,128)S(1)}, u32[]{:S(2)}, u32[]{:S(2)}) collective-permute-start(f32[320,128]{1,0:T(8,128)S(1)} %get-tuple-element.319), channel_id=1, source_target_pairs={{0,1},{1,0},{2,3},{3,2},{4,5},{5,4},{6,7},{7,6},{8,9},{9,8},{10,11... | collective-permute-start | bytes 491528 | tf_op jit(solution)/shard_map/ppermute | solution.py:509
  111.3 13.6 %collective-permute-start.92 = (f32[640,128]{1,0:T(8,128)S(1)}, f32[640,128]{1,0:T(8,128)S(1)}, u32[]{:S(2)}, u32[]{:S(2)}) collective-permute-start(f32[640,128]{1,0:T(8,128)S(1)} %get-tuple-element.315.refs_10_.refs_6_.refs_5_), channel_id=1, source_target_pairs={{0,15},{1,2},{2,1},{3,4},{4,3},{5,6},{6,5},{7,8},{8,7},{9,10},{10,... | collective-permute-start | bytes 983048 | tf_op jit(solution)/shard_map/ppermute | solution.py:504
  111.4 17.0 %collective-permute-start.91 = (f32[640,128]{1,0:T(8,128)S(1)}, f32[640,128]{1,0:T(8,128)S(1)}, u32[]{:S(2)}, u32[]{:S(2)}) collective-permute-start(f32[640,128]{1,0:T(8,128)S(1)} %outer.21.refs_18_.refs_7_.refs_6_), channel_id=1, source_target_pairs={{0,15},{1,2},{2,1},{3,4},{4,3},{5,6},{6,5},{7,8},{8,7},{9,10},{10,... | collective-permute-start | bytes 983048 | tf_op jit(solution)/shard_map/ppermute | solution.py:504
  113.1 4.2 %collective-permute-start.94 = (f32[320,128]{1,0:T(8,128)S(1)}, f32[320,128]{1,0:T(8,128)S(1)}, u32[]{:S(2)}, u32[]{:S(2)}) collective-permute-start(f32[320,128]{1,0:T(8,128)S(1)} %get-tuple-element.320), channel_id=1, source_target_pairs={{0,1},{1,0},{2,3},{3,2},{4,5},{5,4},{6,7},{7,6},{8,9},{9,8},{10,11... | collective-permute-start | bytes 491528 | tf_op jit(solution)/shard_map/ppermute | solution.py:509
  116.3 1.4 %collective-permute-start.95 = (f32[320,128]{1,0:T(8,128)S(1)}, f32[320,128]{1,0:T(8,128)S(1)}, u32[]{:S(2)}, u32[]{:S(2)}) collective-permute-start(f32[320,128]{1,0:T(8,128)S(1)} %get-tuple-element.321), channel_id=1, source_target_pairs={{0,1},{1,0},{2,3},{3,2},{4,5},{5,4},{6,7},{7,6},{8,9},{9,8},{10,11... | collective-permute-start | bytes 491528 | tf_op jit(solution)/shard_map/ppermute | solution.py:509
  116.3 1.6 %collective-permute-start.96 = (f32[320,128]{1,0:T(8,128)S(1)}, f32[320,128]{1,0:T(8,128)S(1)}, u32[]{:S(2)}, u32[]{:S(2)}) collective-permute-start(f32[320,128]{1,0:T(8,128)S(1)} %get-tuple-element.322), channel_id=1, source_target_pairs={{0,1},{1,0},{2,3},{3,2},{4,5},{5,4},{6,7},{7,6},{8,9},{9,8},{10,11... | collective-permute-start | bytes 491528 | tf_op jit(solution)/shard_map/ppermute | solution.py:509
  (2 other events, 1.5 us)
where the time goes:
time: 131 us; the launch traced here: 130 us
  starting transfers between devices  46.2 us (35%)
  Pallas kernels  44.3 us (34%)
  waiting for transfers between devices  29.4 us (22%)
  local copies, waits for them, and re-layouts  9.15 us (7%)
    pallas_call x21, Pallas kernels, run(): pl.pallas_call(lambda *refs: kernel(list(refs)), out_shape=outs, in_specs...  44.3 us
    ppermute x21, starting transfers between devices, within_chip(): return lax.ppermute(value, 'theta', [(i, i ^ 1) for i in range(count)])  25.4 us
    ppermute x12, waiting for transfers between devices, across_chips(): return lax.ppermute(value, 'theta', pairs)  15.9 us
    ppermute x12, starting transfers between devices, across_chips(): return lax.ppermute(value, 'theta', pairs)  14.3 us
    ppermute x4, waiting for transfers between devices, shifted(): lax.ppermute(value, 'theta', [(i, (i + steps) % count) for i in range(cou...  11.9 us
    unnamed x24, local copies, waits for them, and re-layouts  6.97 us
    ppermute x4, starting transfers between devices, shifted(): lax.ppermute(value, 'theta', [(i, (i + steps) % count) for i in range(cou...  6.42 us
  transfers between devices with their start and end apart: 37, of which 15 were waited for; matrix products, arithmetic and copies ran while one was open for 0% of the time, Pallas kernels for 28%

commit v1 on v0

--- a/solution.py
+++ b/solution.py
@@ -16,7 +16,7 @@
 NEED = 6
 HALF = 32
 PARTS = 2
-PIECES = 4
+PIECES = (4, 3, 3)
 
 
 def scalars_of(mean_flow, sign):
@@ -33,7 +33,7 @@
     return half * axial, half * swirl * sign, mass, mass * sound * sound, lift, lift * sign, sign, a
 
 
-def advance(k, f, up, down, low, high, behind, ahead, base, fixed, eddy):
+def advance(k, f, up, down, low, high, behind, ahead, kept, eddy):
     e = k[7] * eddy
     damp = 6.0 * e + (1.5 / PHYS_STEP) * k[7]
     da = [ahead[c] - behind[c] for c in range(COMPS)]
@@ -44,17 +44,24 @@
     new = []
     for c in range(COMPS):
         around = ((up[c] + down[c]) + (low[c] + high[c])) + (behind[c] + ahead[c])
-        kept = (base[c] - k[7] * fixed[c]) - damp * f[c]
-        new.append(kept + e * around - k[0] * da[c] - k[1] * dt[c] - push[c])
+        new.append((kept[c] - damp * f[c]) + e * around - k[0] * da[c] - k[1] * dt[c] - push[c])
     return new
 
 
-def fixed_part(now, prev):
-    return (prev - 4.0 * now) * (0.5 / PHYS_STEP)
+def kept_part(a, base, now, prev):
+    a = a * (0.5 / PHYS_STEP)
+    if base is None:
+        return (1.0 + 4.0 * a) * now - a * prev
+    return (base + (4.0 * a) * now) - a * prev
 
 
 def layer_rows(ref, row, size, first=0):
     return lambda c, r, n: ref[pl.ds((c * 2 + row) * size + r - first, n), :]
+
+
+def part_rows(ref, row, plan, p):
+    whole = ref.shape[0] == 2 * COMPS * plan.radial
+    return layer_rows(ref, row, plan.radial) if whole else layer_rows(ref, row, plan.size, p * plan.size)
 
 
 def joined(refs, row, size):
@@ -70,10 +77,17 @@
     return read
 
 
-def pieces(refs, row, size, piece):
+def piece_of(index):
+    for at, count in enumerate(PIECES):
+        if index < count:
+            return at, index
+        index -= count
+
+
+def pieces(refs, row, size):
     def read(c, r, n):
-        at, first = divmod((c * 2 + row) * size + r, piece)
-        return refs[at][pl.ds(first, n), :]
+        at, index = piece_of(c * 2 + row) if len(refs) > 1 else (0, c * 2 + row)
+        return refs[at][pl.ds(index * size + r, n), :]
 
     return read
 
@@ -113,7 +127,8 @@
     read = lambda source: [source(c, r0, CHUNK) for c in every]
     new = advance(
         coef[row], f, read(before), read(after), low, high, behind, ahead,
-        read(base), [fixed_part(now(c, r0, CHUNK), prev(c, r0, CHUNK)) for c in every], eddy(r0, CHUNK),
+        [kept_part(coef[row][7], base and base(c, r0, CHUNK), now(c, r0, CHUNK), prev(c, r0, CHUNK)) for c in every],
+        eddy(r0, CHUNK),
     )
     for c in every:
         store(c, r0, new[c])
@@ -156,8 +171,8 @@
         high.append(jnp.where(lane == radial - 1, wall, pltpu.roll(value, radial - 1, 1)))
         behind.append(lower)
         ahead.append(upper)
-    fixed = [fixed_part(now[c], prev[c]) for c in range(COMPS)]
-    return advance(coef[1 - side], cur, up, down, low, high, behind, ahead, base, fixed, eddy)
+    kept = [kept_part(coef[0][7], base[c], now[c], prev[c]) for c in range(COMPS)]
+    return advance(coef[1 - side], cur, up, down, low, high, behind, ahead, kept, eddy)
 
 
 def edge_of(ref, side, c, separate, offset):
@@ -179,24 +194,27 @@
         self.n, self.total = n, ITERS * len(SECTION_WEIGHTS)
         self.cells, self.radial, self.axial = shape[2:]
         self.depth, self.size = self.cells - 1, self.radial // PARTS
-        self.piece = 2 * COMPS * self.radial // PIECES
+        self.piece = PIECES[-1] * self.radial
+        self.early = n <= len(SECTION_WEIGHTS)
         self.final = n == self.total
         self.strips = n < self.total
         self.edges = n < self.total - 1
 
 
-def place_of(scalars, depth):
-    odd = scalars[10] < 0.0
+def place_of(depth):
+    odd = lax.axis_index("theta") % 2 == 1
     return jnp.where(odd, depth, 0), jnp.where(odd, -1, 1)
 
 
 def outer_kernel(plan, p, refs):
     size, radial = plan.size, plan.radial
-    scalars, eddy, prev, inner, strip = (refs.pop(0) for _ in range(5))
-    place = place_of(scalars, plan.depth)
+    scalars, eddy, prev, inner = (refs.pop(0) for _ in range(4))
+    place = place_of(plan.depth)
     coef = [coefficients(scalars, row, plan.weight) for row in range(2)]
     mine = [refs.pop(0) for _ in range(PARTS)]
-    now, base, across = refs.pop(0), refs.pop(0), refs.pop(0)
+    now = refs.pop(0)
+    base = None if plan.early else refs.pop(0)
+    across, strip = refs.pop(0), refs.pop(0)
     works = p == 0 and plan.strips
     if works:
         edges = refs.pop(0) if plan.n == 1 else across
@@ -214,6 +232,7 @@
         made, sem = refs.pop(0), refs.pop(0)
     else:
         made = out
+    copies = []
     ghost_columns(tile, columns, [(strip.at[side, c], side) for side in range(2) for c in range(COMPS)])
     for row in range(2):
         for r0 in range(p * size, (p + 1) * size, CHUNK):
@@ -221,22 +240,21 @@
             def store(c, r, value):
                 made[pl.ds((c * 2 + row) * size + r - p * size, CHUNK), :] = value
 
-            inside = plain_rows(inner, row, place[0] + place[1] if plan.n == 1 else 0)
-            part = lambda ref: layer_rows(ref, row, size, p * size)
+            part = lambda ref: part_rows(ref, row, plan, p)
+            inside = part(inner) if plan.n == 1 else plain_rows(inner, row, 0)
             update_rows(
-                row, r0, radial, lambda c: row * COMPS + c, joined(mine, row, size), part(across), inside, part(base),
-                part(now), part(prev), lambda r, n: eddy[row, pl.ds(r, n), :], columns, coef, store,
+                row, r0, radial, lambda c: row * COMPS + c, joined(mine, row, size), part(across), inside,
+                None if plan.early else part(base), part(now), part(prev), lambda r, n: eddy[row, pl.ds(r, n), :], columns,
+                coef, store,
             )
-    if plan.final:
-        copies = []
-        for c in range(COMPS):
-            for row in range(2):
+        if plan.final:
+            for c in range(COMPS):
                 source = made.at[pl.ds((c * 2 + row) * size, size), :]
                 target = out.at[c, row, place[0], pl.ds(p * size, size), :]
-                copies.append(pltpu.make_async_copy(source, target, sem.at[c * 2 + row]))
+                copies.append(pltpu.make_async_copy(source, target, sem.at[len(copies)]))
                 copies[-1].start()
-        for copy in copies:
-            copy.wait()
+    for copy in copies:
+        copy.wait()
     if works:
         lines = tile
         pack_columns(
@@ -260,12 +278,13 @@
 def inner_kernel(plan, refs):
     size, radial, depth = plan.size, plan.radial, plan.depth
     scalars, eddy, prev, now, inner, strip = (refs.pop(0) for _ in range(6))
-    place = place_of(scalars, plan.depth)
+    place = place_of(plan.depth)
     coef = [coefficients(scalars, row, plan.weight) for row in range(2)]
     if plan.n == 1:
         inner = now
     outer = [refs.pop(0) for _ in range(PARTS)]
-    partner, base = [refs.pop(0) for _ in range(1 if plan.n == 1 else PIECES)], refs.pop(0)
+    partner = [refs.pop(0) for _ in range(1 if plan.n == 1 else len(PIECES))]
+    base = None if plan.early else refs.pop(0)
     if plan.strips:
         edges = refs.pop(0) if plan.n == 1 else partner[-1]
         strip_outer, strip_now, strip_prev, strip_eddy, strip_base = (refs.pop(0) for _ in range(5))
@@ -273,7 +292,7 @@
         refs.pop(0)
     made = refs.pop(0)
     if plan.strips:
-        border, strip_out = [refs.pop(0) for _ in range(PIECES)], refs.pop(0)
+        border, strip_out = [refs.pop(0) for _ in PIECES], refs.pop(0)
     tile, columns = refs.pop(0), refs.pop(0)
     if plan.final:
         out, made, sem = made, refs.pop(0), refs.pop(0)
@@ -290,15 +309,14 @@
                 def store(c, r, value):
                     made[c, row, j, pl.ds(r, CHUNK), :] = value
                     if plan.strips and j == depth - 1:
-                        piece, at_row = divmod((c * 2 + row) * radial + r, plan.piece)
-                        border[piece][pl.ds(at_row, CHUNK), :] = value
+                        piece, index = piece_of(c * 2 + row)
+                        border[piece][pl.ds(index * radial + r, CHUNK), :] = value
 
                 before = joined(outer, row, size) if j == 0 else plain_rows(inner, row, own(j - 1))
-                after = pieces(partner, row, radial, partner[0].shape[0]) if j == depth - 1 else plain_rows(inner, row, own(j + 1))
-                first = plan.n <= len(SECTION_WEIGHTS)
+                after = pieces(partner, row, radial) if j == depth - 1 else plain_rows(inner, row, own(j + 1))
                 update_rows(
                     row, r0, radial, lambda c: (row * COMPS + c) * depth + j, plain_rows(inner, row, own(j)), before,
-                    after, plain_rows(base, row, at(j) if first else j), plain_rows(now, row, at(j)),
+                    after, None if plan.early else plain_rows(base, row, j), plain_rows(now, row, at(j)),
                     plain_rows(prev, row, at(j)), lambda r, n: eddy[row, at(j), pl.ds(r, n), :], columns, coef, store,
                 )
         if plan.final:
@@ -338,33 +356,65 @@
     return now + rest + [(2, 0, NEED - 1, COMPS * (NEED - 1))]
 
 
-def gather_kernel(scalars, now, prev, eddy, *outs):
+def border_kernel(now, out, sems):
+    _, _, cells, radial, _ = now.shape
+    first, size = place_of(cells - 1)[0], radial // PARTS
+    copies = []
+    for i in range(2 * COMPS):
+        source = now.at[i // 2, i % 2, first, pl.ds(0, size), :]
+        copies.append(pltpu.make_async_copy(source, out.at[pl.ds(i * size, size), :], sems.at[i]))
+        copies[-1].start()
+    for copy in copies:
+        copy.wait()
+
+
+def gather_kernel(now, prev, eddy, _, *outs):
     _, _, cells, radial, axial = now.shape
-    depth, size = cells - 1, radial // PARTS
-    first, step = place_of(scalars, depth)
-    border, now_outer, prev_outer, eddy_outer = outs[2], outs[3 : 3 + PARTS], outs[3 + PARTS : -1], outs[-1]
-    for c in range(COMPS):
-        for row in range(2):
-            for r0 in range(0, radial, CHUNK):
-                rows = pl.ds(r0, CHUNK)
-                border[pl.ds((c * 2 + row) * radial + r0, CHUNK), :] = now[c, row, first + step * depth, rows, :]
-                p, at_row = r0 // size, (c * 2 + row) * size + r0 % size
-                now_outer[p][pl.ds(at_row, CHUNK), :] = now[c, row, first, rows, :]
-                prev_outer[p][pl.ds(at_row, CHUNK), :] = prev[c, row, first, rows, :]
-    for row in range(2):
-        eddy_outer[row] = eddy[row, first]
+    rotor, stator, *parts = outs[: 2 + PARTS]
+    next_parts, prev_parts = outs[2 + PARTS : 2 + 2 * PARTS], outs[2 + 2 * PARTS : 2 + 3 * PARTS]
+    border, eddy_outer, now_held, prev_held, eddy_held, in_sems, out_sems = outs[2 + 3 * PARTS :]
+    size = radial // PARTS
+    _, _, cells, radial, axial = now.shape
+    depth = cells - 1
+    first, step = place_of(depth)
     per_tile = axial // STRIP
     block = lax.broadcasted_iota(jnp.int32, (radial, axial), 1) // STRIP
     items = [(item, t) for item in strip_items() for t in range(cells)]
-    outs[0][...] = jnp.zeros_like(outs[0])
-    outs[1][...] = jnp.zeros_like(outs[1])
+    arrays = ((now, now_held), (prev, prev_held), (eddy, eddy_held))
+    reads, writes = {}, []
+    order = [(row, kind, c) for row in range(2) for kind, c, _, _ in strip_items()]
+    for i, (row, kind, c) in enumerate(order):
+        at = (row,) if kind == 2 else (c, row)
+        source, held = arrays[kind]
+        reads[row, kind, c] = pltpu.make_async_copy(source.at[at], held.at[at], in_sems.at[i])
+        reads[row, kind, c].start()
+    rotor[...] = jnp.zeros_like(rotor)
+    stator[...] = jnp.zeros_like(stator)
+
+    def write(source, target):
+        writes.append(pltpu.make_async_copy(source, target, out_sems.at[len(writes)]))
+        writes[-1].start()
+
     for row in range(2):
-        mine, other = outs[row], outs[1 - row]
+        mine, other = (rotor, stator) if row == 0 else (stator, rotor)
         begin = axial - STRIP if row == 0 else 0
         for p in range(0, len(items), per_tile):
             tile = jnp.zeros((radial, axial), jnp.float32)
             for q, ((kind, c, _, _), t) in enumerate(items[p : p + per_tile]):
-                value = eddy[row, t] if kind == 2 else (now, prev)[kind][c, row, t]
+                if t == 0:
+                    reads[row, kind, c].wait()
+                    rows = pl.ds((c * 2 + row) * radial, radial)
+                    if kind == 0:
+                        write(now_held.at[c, row, first + step * depth], border.at[rows, :])
+                    if kind < 2:
+                        sources = ((now_held, first, parts), (now_held, first + step, next_parts)) if kind == 0 else ()
+                        for held, at_layer, targets in sources or ((prev_held, first, prev_parts),):
+                            for part, ref in enumerate(targets):
+                                source = held.at[c, row, at_layer, pl.ds(part * size, size), :]
+                                write(source, ref.at[pl.ds((c * 2 + row) * size, size), :])
+                    else:
+                        write(eddy_held.at[row, first], eddy_outer.at[row])
+                value = eddy_held[row, t] if kind == 2 else arrays[kind][1][c, row, t]
                 shift = (q * STRIP - begin) % axial
                 tile = jnp.where(block == q, pltpu.roll(value, shift, 1) if shift else value, tile)
             turned = tile.T
@@ -374,6 +424,8 @@
                 mine[pl.ds((2 * t + (kind > 0)) * HALF + at, count), :] = value
                 if kind == 0 and t == (0 if row == 0 else depth):
                     other[pl.ds(2 * cells * HALF + at, count), :] = value
+    for copy in writes:
+        copy.wait()
 
 
 def align_kernel(depth, within, rotor, stator, rotor_behind, stator_ahead, *outs):
@@ -401,11 +453,11 @@
                 out[pl.ds(at_row, HALF), :] = block(own, side, sidestart, far, start + k, half)
 
 
-def scatter_kernel(depth, scalars, rotor, stator, *outs):
+def scatter_kernel(depth, rotor, stator, *outs):
     cells = depth + 1
     radial = rotor.shape[-1]
     now_out, now_in, prev_out, prev_in, eddy_out, eddy_in, across, partner = outs
-    first, step = place_of(scalars, depth)
+    first, step = place_of(depth)
     for side, ref in enumerate((stator, rotor)):
         for kind, c, count, at in strip_items():
 
@@ -436,10 +488,18 @@
 ANY = pl.BlockSpec(memory_space=pl.ANY)
 
 
-def run(kernel, scalars, arrays, outs, scratch, name, final=None, out_shape=None, pinned=True):
+def in_hbm(x):
+    return pltpu.with_memory_space_constraint(x, pltpu.HBM)
+
+
+def in_vmem(x):
+    return pltpu.with_memory_space_constraint(x, pltpu.VMEM)
+
+
+def run(kernel, scalars, arrays, outs, scratch, name, final=None, out_shape=None, pinned=0):
     scalars, arrays = list(scalars), list(arrays)
-    if pinned:
-        arrays = [pltpu.with_memory_space_constraint(x, pltpu.VMEM) for x in arrays]
+    if pinned is not None:
+        arrays = [in_hbm(x) if i < pinned else in_vmem(x) for i, x in enumerate(arrays)]
     in_specs = [SMEM] * len(scalars) + [VMEM] * len(arrays)
     if out_shape is not None:
         outs, out_specs = jax.ShapeDtypeStruct(out_shape, jnp.float32), ANY
@@ -462,14 +522,41 @@
     )(*scalars, *arrays)
 
 
-def call_gather(scalars, now, prev, eddy):
+def call_border(now):
+    radial, axial = now.shape[3:]
+    return pl.pallas_call(
+        border_kernel,
+        out_shape=pltpu.VMEM((2 * COMPS * radial // PARTS, axial), jnp.float32),
+        in_specs=[ANY],
+        out_specs=VMEM,
+        scratch_shapes=[pltpu.SemaphoreType.DMA((2 * COMPS,))],
+        compiler_params=pltpu.CompilerParams(vmem_limit_bytes=16 << 20),
+        cost_estimate=pl.CostEstimate(flops=1, bytes_accessed=1, transcendentals=0),
+        name="outer_layer",
+    )(in_hbm(now))
+
+
+def call_gather(now, prev, eddy, ordered):
     cells, radial, axial = now.shape[2:]
-    plain = lambda *shape: jax.ShapeDtypeStruct(shape, jnp.float32)
-    strips = plain(2 * HALF * cells + HALF, radial)
-    part = plain(2 * COMPS * radial // PARTS, axial)
-    outs = (strips,) * 2 + (plain(2 * COMPS * radial, axial),) + (part,) * (2 * PARTS) + (plain(2, radial, axial),)
-    got = run(lambda refs: gather_kernel(*refs), [scalars], [now, prev, eddy], outs, [], "gather_strips")
-    return got[:2], got[2], got[3 : 3 + PARTS], got[3 + PARTS : -1], got[-1]
+    strips = pltpu.VMEM((2 * HALF * cells + HALF, radial), jnp.float32)
+    part = pltpu.HBM((2 * COMPS * radial // PARTS, axial), jnp.float32)
+    layer = pltpu.HBM((2 * COMPS * radial, axial), jnp.float32)
+    plane = pltpu.HBM((2, radial, axial), jnp.float32)
+    reads = pltpu.SemaphoreType.DMA((2 * (2 * COMPS + 1),))
+    writes = pltpu.SemaphoreType.DMA((2 * (COMPS + 1 + 3 * COMPS * PARTS),))
+    held = [pltpu.VMEM(x.shape, jnp.float32) for x in (now, prev, eddy)]
+    got = pl.pallas_call(
+        gather_kernel,
+        out_shape=(strips,) * 2 + (part,) * (3 * PARTS) + (layer, plane),
+        in_specs=[ANY] * 4,
+        out_specs=(VMEM,) * 2 + (ANY,) * (3 * PARTS + 2),
+        scratch_shapes=[*held, reads, writes],
+        compiler_params=pltpu.CompilerParams(vmem_limit_bytes=16 << 20),
+        cost_estimate=pl.CostEstimate(flops=1, bytes_accessed=1, transcendentals=0),
+        name="gather_strips",
+    )(*(in_hbm(x) for x in (now, prev, eddy)), ordered)
+    at = [2 + i * PARTS for i in range(4)]
+    return got[:2], *(got[i : i + PARTS] for i in at[:3]), *got[at[3] :]
 
 
 def call_align(within, strips, cells):
@@ -478,18 +565,18 @@
     rows = jax.ShapeDtypeStruct((2 * HALF * (cells + 1), rotor.shape[1]), jnp.float32)
     return run(
         lambda refs: align_kernel(cells - 1, *refs), [within.reshape(1)], [rotor, stator, *moved], (rows, rows), [],
-        "align_strips", pinned=False,
+        "align_strips",
     )
 
 
-def call_scatter(scalars, rotor, stator, cells):
+def call_scatter(rotor, stator, cells):
     radial = rotor.shape[1]
     shape = lambda *lead: pltpu.VMEM((2, *lead, STRIP, radial), jnp.float32)
     both = [shape(COMPS), shape(COMPS, cells - 1)]
     outs = (*both, *both, shape(), shape(cells - 1), shape(COMPS), shape(COMPS))
     return run(
-        lambda refs: scatter_kernel(cells - 1, *refs), [scalars], [rotor, stator], outs, [], "scatter_strips",
-        pinned=False,
+        lambda refs: scatter_kernel(cells - 1, *refs), [], [rotor, stator], outs, [], "scatter_strips",
+        pinned=None,
     )
 
 
@@ -537,16 +624,16 @@
     shift_cells = offset[0] % (cells * count)
     depth, size = cells - 1, radial // PARTS
 
-    early = lax.dynamic_index_in_dim(state_now[:, :, :, :size], core * depth, 2, keepdims=False)
-    across = [across_chips(early.reshape(2 * COMPS * size, axial))]
-    strips, border, outer, prev_outer, eddy_outer = call_gather(scalars, state_now, state_prev, eddy_visc)
+    early = call_border(state_now)
+    across = [across_chips(early)]
+    strips, outer, next_layer, prev_outer, border, eddy_outer = call_gather(state_now, state_prev, eddy_visc, early)
     rotor, stator = call_align(shift_cells % cells, strips, cells)
     sectors = lax.optimization_barrier((shift_cells // cells, across))[0]
-    late, border, rotor, stator = faced(outer[1], border, rotor, stator, sectors)
+    late, border, rotor, stator = faced(outer[-1], border, rotor, stator, sectors)
     across.append(late)
     partner = [border]
     now_out, now_in, prev_out, prev_in, eddy_out, eddy_in, edge_across, edge_within = call_scatter(
-        scalars, rotor, stator, cells
+        rotor, stator, cells
     )
 
     now_outer, inner, strip_out, strip_in = outer, state_now, now_out, now_in
@@ -560,7 +647,9 @@
             plan = Plan(n, shape)
 
             def outer_call(p, ordered):
-                arrays = [eddy_outer, prev_outer[p], inner, strip_out, *outer, now_outer[p], base_outer[p], across[p]]
+                arrays = [eddy_outer, prev_outer[p], next_layer[p] if n == 1 else inner, *outer, now_outer[p]]
+                arrays += [across[p]] if plan.early else [base_outer[p], across[p]]
+                held, arrays = len(arrays), arrays + [strip_out]
                 outs = [pltpu.VMEM((2 * COMPS * size, axial), f32)]
                 if p == 0 and plan.edges:
                     outs = [pltpu.VMEM((2 * COMPS * (size + EDGE), axial), f32)]
@@ -575,16 +664,17 @@
                     arrays.append(ordered)
                 return run(
                     lambda refs: outer_kernel(plan, p, refs), [scalars], arrays, tuple(outs), scratch, "outer",
-                    ordered if plan.final else None, shape if plan.final else None, n > 1,
+                    ordered if plan.final else None, shape if plan.final else None, held if n == 1 else 0,
                 )
 
             def inner_call(ordered):
-                arrays = [eddy_visc, state_prev, state_now, inner, strip_in, *outer, *partner, base_inner]
+                arrays = [eddy_visc, state_prev, state_now, inner, strip_in, *outer, *partner]
+                arrays += [] if plan.early else [base_inner]
                 outs = [pltpu.VMEM((COMPS, 2, depth, radial, axial), f32)]
                 if plan.strips:
                     arrays += [edge_within] if n == 1 else []
                     arrays += [strip_out, now_in, prev_in, eddy_in, base_in, ordered]
-                    outs += [pltpu.VMEM((plan.piece, axial), f32)] * (PIECES - 1)
+                    outs += [pltpu.VMEM((count * radial, axial), f32) for count in PIECES[:-1]]
                     rows = plan.piece + (2 * COMPS * EDGE if plan.edges else 0)
                     outs += [pltpu.VMEM((rows, axial), f32), pltpu.VMEM(strip_in.shape, f32)]
                 scratch = [square, square]
@@ -592,7 +682,7 @@
                     scratch += [pltpu.VMEM((COMPS, 2, depth, radial, axial), f32), pltpu.SemaphoreType.DMA((depth,))]
                 return run(
                     lambda refs: inner_kernel(plan, refs), [scalars], arrays, tuple(outs), scratch, "inner", None,
-                    shape if plan.final else None, n > 1,
+                    shape if plan.final else None, None if n == 1 else 0,
                 )
 
             if plan.final:

time: 131 us -> 123 us (0.939)
  the two profiles are of different devices: /device:TPU:1 before, /device:TPU:13 now
where the time goes in v1:
time: 123 us; the launch traced here: 125 us
  waiting for transfers between devices  56.8 us (46%)
  Pallas kernels  47.1 us (38%)
  starting transfers between devices  19.1 us (16%)
  between operations  1.25 us (1%)
    pallas_call x20, Pallas kernels, run(): pl.pallas_call(lambda *refs: kernel(list(refs)), out_shape=outs, in_specs...  40.5 us
    ppermute x12, waiting for transfers between devices, across_chips(): return lax.ppermute(value, 'theta', pairs)  35.8 us
    ppermute x4, waiting for transfers between devices, shifted(): lax.ppermute(value, 'theta', [(i, (i + steps) % count) for i in range(cou...  18.2 us
    ppermute x12, starting transfers between devices, across_chips(): return lax.ppermute(value, 'theta', pairs)  8.96 us
    ppermute x4, starting transfers between devices, shifted(): lax.ppermute(value, 'theta', [(i, (i + steps) % count) for i in range(cou...  6.19 us
    pallas_call x1, Pallas kernels, call_gather(): pl.pallas_call(gather_kernel, out_shape=(strips,) * 2 + (part,) * (3 * PA...  5.64 us
    ppermute x16, starting transfers between devices, within_chip(): return lax.ppermute(value, 'theta', [(i, i ^ 1) for i in range(count)])  4 us
    ppermute x16, waiting for transfers between devices, within_chip(): return lax.ppermute(value, 'theta', [(i, i ^ 1) for i in range(count)])  2.78 us
  transfers between devices with their start and end apart: 32, of which 15 were waited for; matrix products, arithmetic and copies ran while one was open for 0% of the time, Pallas kernels for 33%

profile of v1, /device:TPU:13, one launch (start us, length us, event | category | flops | bytes accessed | tf_op | source)
XLA Modules:
  0.0 124.6 jit_solution(13405436323790916937)
XLA Ops:
  0.0 1.0 outer_layer.1._
  1.0 1.8 %collective-permute-start.64 = (f32[640,128]{1,0:T(8,128)S(1)}, f32[640,128]{1,0:T(8,128)S(1)}, u32[]{:S(2)}, u32[]{:S(2)}) collective-permute-start(f32[640,128]{1,0:T(8,128)S(1)} %outer_layer.1._), channel_id=1, source_target_pairs={{0,15},{1,2},{2,1},{3,4},{4,3},{5,6},{6,5},{7,8},{8,7},{9,10},{10,... | collective-permute-start | bytes 983048 | tf_op jit(solution)/shard_map/ppermute | solution.py:591
  2.8 5.6 %gather_strips.1 = (f32[288,128]{1,0:T(8,128)S(1)}, f32[288,128]{1,0:T(8,128)S(1)}, f32[640,128]{1,0:T(8,128)}, f32[640,128]{1,0:T(8,128)}, f32[640,128]{1,0:T(8...) custom-call(f32[5,2,4,128,128]{4,3,2,1,0:T(8,128)} %refs_3_.11, ...), custom_call_target="tpu_custom_call" | custom-call | flops 1 | bytes 1 | tf_op jit(solution)/shard_map/gather_strips/pallas_call | solution.py:548
  10.0 2.0 %collective-permute-done.65.refs_3_ = f32[288,128]{1,0:T(8,128)S(1)} collective-permute-done((f32[288,128]{1,0:T(8,128)S(1)}, f32[288,128]{1,0:T(8,128)S(1)}, u32[]{:S(2)}, u32[]{:S(2)}) %collective-permute-start.65) | collective-permute-done | bytes 147488 | tf_op jit(solution)/shard_map/ppermute | solution.py:585
  12.0 2.7 %collective-permute-done.66.refs_4_ = f32[288,128]{1,0:T(8,128)S(1)} collective-permute-done((f32[288,128]{1,0:T(8,128)S(1)}, f32[288,128]{1,0:T(8,128)S(1)}, u32[]{:S(2)}, u32[]{:S(2)}) %collective-permute-start.66) | collective-permute-done | bytes 147488 | tf_op jit(solution)/shard_map/ppermute | solution.py:585
  14.7 21.2 %conditional.1 = (f32[640,128]{1,0:T(8,128)}, f32[1280,128]{1,0:T(8,128)}, f32[320,128]{1,0:T(8,128)}, f32[320,128]{1,0:T(8,128)}) conditional(s32[]{:T(128)} %clamp.3, (f32[640,128]{1,0:T(8,128)}, f32[1280,128]{1,0:T(8,128)}, f32[320,128]{1,0:T(8,128)S(1)}, f32[320,128]{1,0:T(8,128)S(1)}) %tuple.71, ...), branch_computations={%region_0.1_spmd, %region_1.2_spmd, %region_2.3_spmd, %region_3.4_... | conditional | bytes 5243072 | solution.py:609
  14.8 1.9 %collective-permute-start.36 = (f32[640,128]{1,0:T(8,128)}, f32[640,128]{1,0:T(8,128)}, u32[]{:S(2)}, u32[]{:S(2)}) collective-permute-start(f32[640,128]{1,0:T(8,128)} %get-tuple-element.169), channel_id=1, source_target_pairs={{0,15},{1,2},{2,1},{3,4},{4,3},{5,6},{6,5},{7,8},{8,7},{9,10},{10,... | collective-permute-start | bytes 983048 | tf_op jit(solution)/shard_map/cond/branch_9_fun/ppermute | solution.py:591
  16.7 5.6 %collective-permute-start.38 = (f32[320,128]{1,0:T(8,128)S(1)}, f32[320,128]{1,0:T(8,128)}, u32[]{:S(2)}, u32[]{:S(2)}) collective-permute-start(f32[320,128]{1,0:T(8,128)S(1)} %get-tuple-element.171), channel_id=1, source_target_pairs={{0,9},{1,10},{2,11},{3,12},{4,13},{5,14},{6,15},{7,0},{8,1},{9,2},... | collective-permute-start | bytes 491528 | tf_op jit(solution)/shard_map/cond/branch_9_fun/ppermute | solution.py:585
  22.3 10.1 %collective-permute-done.38 = f32[320,128]{1,0:T(8,128)} collective-permute-done((f32[320,128]{1,0:T(8,128)S(1)}, f32[320,128]{1,0:T(8,128)}, u32[]{:S(2)}, u32[]{:S(2)}) %collective-permute-start.38) | collective-permute-done | bytes 163872 | tf_op jit(solution)/shard_map/cond/branch_9_fun/ppermute | solution.py:585
  32.4 3.5 %collective-permute-done.39 = f32[320,128]{1,0:T(8,128)} collective-permute-done((f32[320,128]{1,0:T(8,128)S(1)}, f32[320,128]{1,0:T(8,128)}, u32[]{:S(2)}, u32[]{:S(2)}) %collective-permute-start.39) | collective-permute-done | bytes 163872 | tf_op jit(solution)/shard_map/cond/branch_9_fun/ppermute | solution.py:585
  35.9 1.1 scatter_strips.1
  37.0 2.3 %outer.12 = (f32[680,128]{1,0:T(8,128)S(1)}, f32[2,5,8,128]{3,2,1,0:T(8,128)S(1)}) custom-call(f32[16]{0:T(128)S(1)} %concatenate.7.refs_0_, f32[2,128,128]{2,1,0:T(8,128)} %get-tuple-element.257.refs_1_, f32[640,128]{1,0:T(8,128)} %get-tuple-element.277.refs_2_, f32[640,128]{1,0:T(8,128)} %get-tuple-element.278.refs_3_, ...), custom_call_target="tpu_custom_call" | custom-call | flops 1 | bytes 1 | tf_op jit(solution)/shard_map/outer/pallas_call | solution.py:512
  39.4 2.0 %outer.13.refs_15_.refs_5_.refs_7_ = f32[640,128]{1,0:T(8,128)S(1)} custom-call(f32[16]{0:T(128)S(1)} %concatenate.7.refs_0_, f32[2,128,128]{2,1,0:T(8,128)} %get-tuple-element.257.refs_1_, f32[640,128]{1,0:T(8,128)} %get-tuple-element.258.refs_2_, f32[640,128]{1,0:T(8,128)} %get-tuple-element.275.refs_3_, f32[640,128]{1,0:T(8,128)} %get-tuple-element.269.refs_4_.refs_6_, ...), custom_call_target="tpu_custom_call" | custom-call | flops 1 | bytes 1 | tf_op jit(solution)/shard_map/outer/pallas_call | solution.py:512
  41.4 1.8 %collective-permute-start.70 = (f32[640,128]{1,0:T(8,128)S(1)}, f32[640,128]{1,0:T(8,128)S(1)}, u32[]{:S(2)}, u32[]{:S(2)}) collective-permute-start(f32[640,128]{1,0:T(8,128)S(1)} %outer.13.refs_15_.refs_5_.refs_7_), channel_id=1, source_target_pairs={{0,15},{1,2},{2,1},{3,4},{4,3},{5,6},{6,5},{7,8},{8,7},{9,10},{10,... | collective-permute-start | bytes 983048 | tf_op jit(solution)/shard_map/ppermute | solution.py:591
  43.3 4.0 %inner.6 = (f32[5,2,3,128,128]{4,3,2,1,0:T(8,128)S(1)}, f32[512,128]{1,0:T(8,128)S(1)}, f32[384,128]{1,0:T(8,128)S(1)}, f32[424,128]{1,0:T(8,128)S(1)}, f32[2,5,3,8,128]{4,3,2,1,0:T(8,128)S(1)}) custom-call(f32[16]{0:T(128)S(1)} %concatenate.7.refs_0_, f32[2,4,128,128]{3,2,1,0:T(8,128)S(1)} %copy-done.4, f32[5,2,4,128,128]{4,3,2,1,0:T(8,128)S(1)} %copy-done.1, ...), custom_call_target="tpu_custom_call" | custom-call | flops 1 | bytes 1 | tf_op jit(solution)/shard_map/inner/pallas_call | solution.py:512
  47.3 10.0 %collective-permute-done.71.refs_7_ = f32[680,128]{1,0:T(8,128)S(1)} collective-permute-done((f32[680,128]{1,0:T(8,128)S(1)}, f32[680,128]{1,0:T(8,128)S(1)}, u32[]{:S(2)}, u32[]{:S(2)}) %collective-permute-start.71) | collective-permute-done | bytes 348192 | tf_op jit(solution)/shard_map/ppermute | solution.py:591
  57.3 1.3 %outer.14 = (f32[680,128]{1,0:T(8,128)S(1)}, f32[2,5,8,128]{3,2,1,0:T(8,128)S(1)}) custom-call(f32[16]{0:T(128)S(1)} %concatenate.7.refs_0_, f32[2,128,128]{2,1,0:T(8,128)S(1)} %copy-done.5, f32[640,128]{1,0:T(8,128)S(1)} %copy-done.7, f32[5,2,3,128,128]{4,3,2,1,0:T(8,128)S(1)} %get-tuple-element.283.refs_3_.refs_4_, ...), custom_call_target="tpu_custom_call" | custom-call | flops 1 | bytes 1 | tf_op jit(solution)/shard_map/outer/pallas_call | solution.py:512
  58.7 1.9 %collective-permute-done.70.refs_7_ = f32[640,128]{1,0:T(8,128)S(1)} collective-permute-done((f32[640,128]{1,0:T(8,128)S(1)}, f32[640,128]{1,0:T(8,128)S(1)}, u32[]{:S(2)}, u32[]{:S(2)}) %collective-permute-start.70) | collective-permute-done | bytes 327712 | tf_op jit(solution)/shard_map/ppermute | solution.py:591
  60.6 1.0 outer.15.refs_16_.refs_5_.refs_7_
  61.8 0.5 collective-permute-start.68
  62.3 1.2 collective-permute-done.68.refs_9_
  63.5 3.4 %inner.7 = (f32[5,2,3,128,128]{4,3,2,1,0:T(8,128)S(1)}, f32[512,128]{1,0:T(8,128)S(1)}, f32[384,128]{1,0:T(8,128)S(1)}, f32[424,128]{1,0:T(8,128)S(1)}, f32[2,5,3,8,128]{4,3,2,1,0:T(8,128)S(1)}) custom-call(f32[16]{0:T(128)S(1)} %concatenate.7.refs_0_, f32[2,4,128,128]{3,2,1,0:T(8,128)S(1)} %copy-done.4, f32[5,2,4,128,128]{4,3,2,1,0:T(8,128)S(1)} %copy-done.1, ...), custom_call_target="tpu_custom_call" | custom-call | flops 1 | bytes 1 | tf_op jit(solution)/shard_map/inner/pallas_call | solution.py:512
  67.2 1.6 %collective-permute-done.76.refs_7_ = f32[680,128]{1,0:T(8,128)S(1)} collective-permute-done((f32[680,128]{1,0:T(8,128)S(1)}, f32[680,128]{1,0:T(8,128)S(1)}, u32[]{:S(2)}, u32[]{:S(2)}) %collective-permute-start.76) | collective-permute-done | bytes 348192 | tf_op jit(solution)/shard_map/ppermute | solution.py:591
  68.9 1.2 outer.16
  70.2 1.1 collective-permute-start.74
  71.3 5.5 %collective-permute-done.75.refs_7_ = f32[640,128]{1,0:T(8,128)S(1)} collective-permute-done((f32[640,128]{1,0:T(8,128)S(1)}, f32[640,128]{1,0:T(8,128)S(1)}, u32[]{:S(2)}, u32[]{:S(2)}) %collective-permute-start.75) | collective-permute-done | bytes 327712 | tf_op jit(solution)/shard_map/ppermute | solution.py:591
  76.8 1.0 outer.17.refs_16_.refs_5_.refs_7_
  77.9 3.8 %inner.8 = (f32[5,2,3,128,128]{4,3,2,1,0:T(8,128)S(1)}, f32[512,128]{1,0:T(8,128)S(1)}, f32[384,128]{1,0:T(8,128)S(1)}, f32[424,128]{1,0:T(8,128)S(1)}, f32[2,5,3,8,128]{4,3,2,1,0:T(8,128)S(1)}) custom-call(f32[16]{0:T(128)S(1)} %concatenate.7.refs_0_, f32[2,4,128,128]{3,2,1,0:T(8,128)S(1)} %copy-done.4, f32[5,2,4,128,128]{4,3,2,1,0:T(8,128)S(1)} %copy-done.1, ...), custom_call_target="tpu_custom_call" | custom-call | flops 1 | bytes 1 | tf_op jit(solution)/shard_map/inner/pallas_call | solution.py:512
  81.8 0.5 collective-permute-start.79
  82.3 1.0 collective-permute-done.81.refs_8_
  83.3 1.3 %outer.18 = (f32[680,128]{1,0:T(8,128)S(1)}, f32[2,5,8,128]{3,2,1,0:T(8,128)S(1)}) custom-call(f32[16]{0:T(128)S(1)} %concatenate.7.refs_0_, f32[2,128,128]{2,1,0:T(8,128)S(1)} %copy-done.5, f32[640,128]{1,0:T(8,128)S(1)} %copy-done.7, f32[5,2,3,128,128]{4,3,2,1,0:T(8,128)S(1)} %get-tuple-element.297.refs_3_.refs_4_.refs_11_, ...), custom_call_target="tpu_custom_call" | custom-call | flops 1 | bytes 1 | tf_op jit(solution)/shard_map/outer/pallas_call | solution.py:512
  84.6 0.9 collective-permute-start.86
  85.5 1.4 %collective-permute-done.80.refs_8_ = f32[640,128]{1,0:T(8,128)S(1)} collective-permute-done((f32[640,128]{1,0:T(8,128)S(1)}, f32[640,128]{1,0:T(8,128)S(1)}, u32[]{:S(2)}, u32[]{:S(2)}) %collective-permute-start.80) | collective-permute-done | bytes 327712 | tf_op jit(solution)/shard_map/ppermute | solution.py:591
  86.8 1.0 outer.19.refs_17_.refs_5_.refs_7_
  87.9 0.9 collective-permute-start.85
  88.8 3.7 %inner.9 = (f32[5,2,3,128,128]{4,3,2,1,0:T(8,128)S(1)}, f32[512,128]{1,0:T(8,128)S(1)}, f32[384,128]{1,0:T(8,128)S(1)}, f32[424,128]{1,0:T(8,128)S(1)}, f32[2,5,3,8,128]{4,3,2,1,0:T(8,128)S(1)}) custom-call(f32[16]{0:T(128)S(1)} %concatenate.7.refs_0_, f32[2,4,128,128]{3,2,1,0:T(8,128)S(1)} %copy-done.4, f32[5,2,4,128,128]{4,3,2,1,0:T(8,128)S(1)} %copy-done.1, ...), custom_call_target="tpu_custom_call" | custom-call | flops 1 | bytes 1 | tf_op jit(solution)/shard_map/inner/pallas_call | solution.py:512
  92.5 0.5 collective-permute-start.84
  93.1 12.3 %collective-permute-done.86.refs_8_ = f32[680,128]{1,0:T(8,128)S(1)} collective-permute-done((f32[680,128]{1,0:T(8,128)S(1)}, f32[680,128]{1,0:T(8,128)S(1)}, u32[]{:S(2)}, u32[]{:S(2)}) %collective-permute-start.86) | collective-permute-done | bytes 348192 | tf_op jit(solution)/shard_map/ppermute | solution.py:591
  105.4 1.3 %outer.20 = (f32[640,128]{1,0:T(8,128)S(1)}, f32[2,5,8,128]{3,2,1,0:T(8,128)S(1)}) custom-call(f32[16]{0:T(128)S(1)} %concatenate.7.refs_0_, f32[2,128,128]{2,1,0:T(8,128)S(1)} %copy-done.5, f32[640,128]{1,0:T(8,128)S(1)} %copy-done.7, f32[5,2,3,128,128]{4,3,2,1,0:T(8,128)S(1)} %get-tuple-element.304.refs_3_.refs_4_, ...), custom_call_target="tpu_custom_call" | custom-call | flops 1 | bytes 1 | tf_op jit(solution)/shard_map/outer/pallas_call | solution.py:512
  106.8 2.1 %collective-permute-done.85.refs_8_ = f32[640,128]{1,0:T(8,128)S(1)} collective-permute-done((f32[640,128]{1,0:T(8,128)S(1)}, f32[640,128]{1,0:T(8,128)S(1)}, u32[]{:S(2)}, u32[]{:S(2)}) %collective-permute-start.85) | collective-permute-done | bytes 327712 | tf_op jit(solution)/shard_map/ppermute | solution.py:591
  108.8 1.0 outer.21.refs_17_.refs_7_.refs_5_
  109.8 1.2 collective-permute-start.87
  111.1 3.7 %inner.10 = (f32[5,2,3,128,128]{4,3,2,1,0:T(8,128)S(1)}, f32[512,128]{1,0:T(8,128)S(1)}, f32[384,128]{1,0:T(8,128)S(1)}, f32[384,128]{1,0:T(8,128)S(1)}, f32[2,5,3,8,128]{4,3,2,1,0:T(8,128)S(1)}) custom-call(f32[16]{0:T(128)S(1)} %concatenate.7.refs_0_, f32[2,4,128,128]{3,2,1,0:T(8,128)S(1)} %copy-done.4, f32[5,2,4,128,128]{4,3,2,1,0:T(8,128)S(1)} %copy-done.1, ...), custom_call_target="tpu_custom_call" | custom-call | flops 1 | bytes 1 | tf_op jit(solution)/shard_map/inner/pallas_call | solution.py:512
  114.8 0.5 collective-permute-start.90
  115.4 1.2 collective-permute-done.90.refs_9_
  116.9 3.9 %inner.11.refs_10_ = f32[5,2,4,128,128]{4,3,2,1,0:T(8,128)} custom-call(f32[16]{0:T(128)S(1)} %concatenate.7.refs_0_, f32[2,4,128,128]{3,2,1,0:T(8,128)S(1)} %copy-done.4, f32[5,2,4,128,128]{4,3,2,1,0:T(8,128)S(1)} %copy-done.1, f32[5,2,4,128,128]{4,3,2,1,0:T(8,128)S(1)} %copy-done, f32[5,2,3,128,128]{4,3,2,1,0:T(8,128)S(1)} %get-tuple-element.311.refs_4_.refs_3_, ...), custom_call_target="tpu_custom_call" | custom-call | flops 1 | bytes 1 | tf_op jit(solution)/shard_map/inner/pallas_call | solution.py:512
  120.9 1.8 %outer.22.refs_10_ = f32[5,2,4,128,128]{4,3,2,1,0:T(8,128)} custom-call(f32[16]{0:T(128)S(1)} %concatenate.7.refs_0_, f32[2,128,128]{2,1,0:T(8,128)S(1)} %copy-done.5, f32[640,128]{1,0:T(8,128)S(1)} %copy-done.7, f32[5,2,3,128,128]{4,3,2,1,0:T(8,128)S(1)} %get-tuple-element.311.refs_4_.refs_3_, ...), custom_call_target="tpu_custom_call", output_to_operand_aliasing={{}: (10, {})} | custom-call | flops 1 | bytes 1 | tf_op jit(solution)/shard_map/outer/pallas_call | solution.py:512
  122.7 1.8 %outer.23 = f32[5,2,4,128,128]{4,3,2,1,0:T(8,128)} custom-call(f32[16]{0:T(128)S(1)} %concatenate.7.refs_0_, f32[2,128,128]{2,1,0:T(8,128)S(1)} %copy-done.5, f32[640,128]{1,0:T(8,128)S(1)} %copy-done.6, f32[5,2,3,128,128]{4,3,2,1,0:T(8,128)S(1)} %get-tuple-element.311.refs_4_.refs_3_, ...), custom_call_target="tpu_custom_call", output_to_operand_aliasing={{}: (10, {})} | custom-call | flops 1 | bytes 1 | tf_op jit(solution)/shard_map/outer/pallas_call | solution.py:512
  (63 shorter events, 2.6 us)
Async XLA Ops:
  1.0 8.1 %copy-start.9 = (f32[2,4]{1,0:T(2,128)S(1)}, f32[2,4]{1,0:T(2,128)}, u32[]{:S(2)}) copy-start(f32[2,4]{1,0:T(2,128)} %param.24) | copy-start | bytes 100
  1.0 13.7 %collective-permute-start.64 = (f32[640,128]{1,0:T(8,128)S(1)}, f32[640,128]{1,0:T(8,128)S(1)}, u32[]{:S(2)}, u32[]{:S(2)}) collective-permute-start(f32[640,128]{1,0:T(8,128)S(1)} %outer_layer.1._), channel_id=1, source_target_pairs={{0,15},{1,2},{2,1},{3,4},{4,3},{5,6},{6,5},{7,8},{8,7},{9,10},{10,... | collective-permute-start | bytes 983048 | tf_op jit(solution)/shard_map/ppermute | solution.py:591
  2.8 40.4 %copy-start.4 = (f32[2,4,128,128]{3,2,1,0:T(8,128)S(1)}, f32[2,4,128,128]{3,2,1,0:T(8,128)}, u32[]{:S(2)}) copy-start(f32[2,4,128,128]{3,2,1,0:T(8,128)} %refs_1_.11) | copy-start | bytes 1572868
  8.5 3.5 %collective-permute-start.65 = (f32[288,128]{1,0:T(8,128)S(1)}, f32[288,128]{1,0:T(8,128)S(1)}, u32[]{:S(2)}, u32[]{:S(2)}) collective-permute-start(f32[288,128]{1,0:T(8,128)S(1)} %get-tuple-element.262.refs_1_), channel_id=1, source_target_pairs={{0,1},{1,2},{2,3},{3,4},{4,5},{5,6},{6,7},{7,8},{8,9},{9,10},{10,1... | collective-permute-start | bytes 442376 | tf_op jit(solution)/shard_map/ppermute | solution.py:585
  8.6 6.1 %collective-permute-start.66 = (f32[288,128]{1,0:T(8,128)S(1)}, f32[288,128]{1,0:T(8,128)S(1)}, u32[]{:S(2)}, u32[]{:S(2)}) collective-permute-start(f32[288,128]{1,0:T(8,128)S(1)} %get-tuple-element.263.refs_2_), channel_id=1, source_target_pairs={{0,15},{1,0},{2,1},{3,2},{4,3},{5,4},{6,5},{7,6},{8,7},{9,8},{10,9... | collective-permute-start | bytes 442376 | tf_op jit(solution)/shard_map/ppermute | solution.py:585
  14.6 28.6 %copy-start.3 = (f32[640,128]{1,0:T(8,128)S(1)}, f32[640,128]{1,0:T(8,128)}, u32[]{:S(2)}) copy-start(f32[640,128]{1,0:T(8,128)} %get-tuple-element.269.refs_4_.refs_6_) | copy-start | bytes 983044
  14.7 22.3 %copy-start.8 = (f32[640,128]{1,0:T(8,128)}, f32[640,128]{1,0:T(8,128)S(1)}, u32[]{:S(2)}) copy-start(f32[640,128]{1,0:T(8,128)S(1)} %collective-permute-done.64.refs_7_) | copy-start | bytes 983044
  14.8 21.1 %collective-permute-start.37 = (f32[1280,128]{1,0:T(8,128)}, f32[1280,128]{1,0:T(8,128)}, u32[]{:S(2)}, u32[]{:S(2)}) collective-permute-start(f32[1280,128]{1,0:T(8,128)} %get-tuple-element.170), channel_id=1, source_target_pairs={{0,1},{1,0},{2,3},{3,2},{4,5},{5,4},{6,7},{7,6},{8,9},{9,8},{10,11... | collective-permute-start | bytes 1966088 | tf_op jit(solution)/shard_map/cond/branch_9_fun/ppermute | solution.py:596
  14.8 21.1 %collective-permute-start.36 = (f32[640,128]{1,0:T(8,128)}, f32[640,128]{1,0:T(8,128)}, u32[]{:S(2)}, u32[]{:S(2)}) collective-permute-start(f32[640,128]{1,0:T(8,128)} %get-tuple-element.169), channel_id=1, source_target_pairs={{0,15},{1,2},{2,1},{3,4},{4,3},{5,6},{6,5},{7,8},{8,7},{9,10},{10,... | collective-permute-start | bytes 983048 | tf_op jit(solution)/shard_map/cond/branch_9_fun/ppermute | solution.py:591
  16.7 15.7 %collective-permute-start.38 = (f32[320,128]{1,0:T(8,128)S(1)}, f32[320,128]{1,0:T(8,128)}, u32[]{:S(2)}, u32[]{:S(2)}) collective-permute-start(f32[320,128]{1,0:T(8,128)S(1)} %get-tuple-element.171), channel_id=1, source_target_pairs={{0,9},{1,10},{2,11},{3,12},{4,13},{5,14},{6,15},{7,0},{8,1},{9,2},... | collective-permute-start | bytes 491528 | tf_op jit(solution)/shard_map/cond/branch_9_fun/ppermute | solution.py:585
  22.3 13.6 %collective-permute-start.39 = (f32[320,128]{1,0:T(8,128)S(1)}, f32[320,128]{1,0:T(8,128)}, u32[]{:S(2)}, u32[]{:S(2)}) collective-permute-start(f32[320,128]{1,0:T(8,128)S(1)} %get-tuple-element.172), channel_id=1, source_target_pairs={{0,7},{1,8},{2,9},{3,10},{4,11},{5,12},{6,13},{7,14},{8,15},{9,0},... | collective-permute-start | bytes 491528 | tf_op jit(solution)/shard_map/cond/branch_9_fun/ppermute | solution.py:585
  35.9 7.3 %copy-start.2 = (f32[640,128]{1,0:T(8,128)S(1)}, f32[640,128]{1,0:T(8,128)}, u32[]{:S(2)}) copy-start(f32[640,128]{1,0:T(8,128)} %get-tuple-element.260.refs_5_.refs_6_.refs_7_) | copy-start | bytes 983044
  37.0 6.2 %copy-start = (f32[5,2,4,128,128]{4,3,2,1,0:T(8,128)S(1)}, f32[5,2,4,128,128]{4,3,2,1,0:T(8,128)}, u32[]{:S(2)}) copy-start(f32[5,2,4,128,128]{4,3,2,1,0:T(8,128)} %refs_3_.11) | copy-start | bytes 7864324
  37.0 6.2 %copy-start.1 = (f32[5,2,4,128,128]{4,3,2,1,0:T(8,128)S(1)}, f32[5,2,4,128,128]{4,3,2,1,0:T(8,128)}, u32[]{:S(2)}) copy-start(f32[5,2,4,128,128]{4,3,2,1,0:T(8,128)} %refs_2_.11) | copy-start | bytes 7864324
  39.4 17.9 %collective-permute-start.71 = (f32[680,128]{1,0:T(8,128)S(1)}, f32[680,128]{1,0:T(8,128)S(1)}, u32[]{:S(2)}, u32[]{:S(2)}) collective-permute-start(f32[680,128]{1,0:T(8,128)S(1)} %get-tuple-element.282.refs_9_.refs_4_.refs_6_), channel_id=1, source_target_pairs={{0,15},{1,2},{2,1},{3,4},{4,3},{5,6},{6,5},{7,8},{8,7},{9,10},{10,... | collective-permute-start | bytes 1044488 | tf_op jit(solution)/shard_map/ppermute | solution.py:591
  41.4 19.2 %collective-permute-start.70 = (f32[640,128]{1,0:T(8,128)S(1)}, f32[640,128]{1,0:T(8,128)S(1)}, u32[]{:S(2)}, u32[]{:S(2)}) collective-permute-start(f32[640,128]{1,0:T(8,128)S(1)} %outer.13.refs_15_.refs_5_.refs_7_), channel_id=1, source_target_pairs={{0,15},{1,2},{2,1},{3,4},{4,3},{5,6},{6,5},{7,8},{8,7},{9,10},{10,... | collective-permute-start | bytes 983048 | tf_op jit(solution)/shard_map/ppermute | solution.py:591
  43.2 14.1 %copy-start.5 = (f32[2,128,128]{2,1,0:T(8,128)S(1)}, f32[2,128,128]{2,1,0:T(8,128)}, u32[]{:S(2)}) copy-start(f32[2,128,128]{2,1,0:T(8,128)} %get-tuple-element.257.refs_1_) | copy-start | bytes 393220
  43.2 14.0 %copy-start.7 = (f32[640,128]{1,0:T(8,128)S(1)}, f32[640,128]{1,0:T(8,128)}, u32[]{:S(2)}) copy-start(f32[640,128]{1,0:T(8,128)} %get-tuple-element.277.refs_2_) | copy-start | bytes 983044
  47.3 13.4 %copy-start.6 = (f32[640,128]{1,0:T(8,128)S(1)}, f32[640,128]{1,0:T(8,128)}, u32[]{:S(2)}) copy-start(f32[640,128]{1,0:T(8,128)} %get-tuple-element.258.refs_2_) | copy-start | bytes 983044
  58.6 10.3 %collective-permute-start.76 = (f32[680,128]{1,0:T(8,128)S(1)}, f32[680,128]{1,0:T(8,128)S(1)}, u32[]{:S(2)}, u32[]{:S(2)}) collective-permute-start(f32[680,128]{1,0:T(8,128)S(1)} %get-tuple-element.289.refs_9_.refs_4_.refs_6_), channel_id=1, source_target_pairs={{0,15},{1,2},{2,1},{3,4},{4,3},{5,6},{6,5},{7,8},{8,7},{9,10},{10,... | collective-permute-start | bytes 1044488 | tf_op jit(solution)/shard_map/ppermute | solution.py:591
  58.6 4.9 %collective-permute-start.67 = (f32[512,128]{1,0:T(8,128)S(1)}, f32[512,128]{1,0:T(8,128)S(1)}, u32[]{:S(2)}, u32[]{:S(2)}) collective-permute-start(f32[512,128]{1,0:T(8,128)S(1)} %get-tuple-element.285), channel_id=1, source_target_pairs={{0,1},{1,0},{2,3},{3,2},{4,5},{5,4},{6,7},{7,6},{8,9},{9,8},{10,11... | collective-permute-start | bytes 786440 | tf_op jit(solution)/shard_map/ppermute | solution.py:596
  61.6 15.2 %collective-permute-start.75 = (f32[640,128]{1,0:T(8,128)S(1)}, f32[640,128]{1,0:T(8,128)S(1)}, u32[]{:S(2)}, u32[]{:S(2)}) collective-permute-start(f32[640,128]{1,0:T(8,128)S(1)} %outer.15.refs_16_.refs_5_.refs_7_), channel_id=1, source_target_pairs={{0,15},{1,2},{2,1},{3,4},{4,3},{5,6},{6,5},{7,8},{8,7},{9,10},{10,... | collective-permute-start | bytes 983048 | tf_op jit(solution)/shard_map/ppermute | solution.py:591
  61.7 1.8 %collective-permute-start.69 = (f32[424,128]{1,0:T(8,128)S(1)}, f32[424,128]{1,0:T(8,128)S(1)}, u32[]{:S(2)}, u32[]{:S(2)}) collective-permute-start(f32[424,128]{1,0:T(8,128)S(1)} %get-tuple-element.287), channel_id=1, source_target_pairs={{0,1},{1,0},{2,3},{3,2},{4,5},{5,4},{6,7},{7,6},{8,9},{9,8},{10,11... | collective-permute-start | bytes 651272 | tf_op jit(solution)/shard_map/ppermute | solution.py:596
  61.8 1.7 %collective-permute-start.68 = (f32[384,128]{1,0:T(8,128)S(1)}, f32[384,128]{1,0:T(8,128)S(1)}, u32[]{:S(2)}, u32[]{:S(2)}) collective-permute-start(f32[384,128]{1,0:T(8,128)S(1)} %get-tuple-element.286), channel_id=1, source_target_pairs={{0,1},{1,0},{2,3},{3,2},{4,5},{5,4},{6,7},{7,6},{8,9},{9,8},{10,11... | collective-permute-start | bytes 589832 | tf_op jit(solution)/shard_map/ppermute | solution.py:596
  67.0 10.9 %collective-permute-start.72 = (f32[512,128]{1,0:T(8,128)S(1)}, f32[512,128]{1,0:T(8,128)S(1)}, u32[]{:S(2)}, u32[]{:S(2)}) collective-permute-start(f32[512,128]{1,0:T(8,128)S(1)} %get-tuple-element.292), channel_id=1, source_target_pairs={{0,1},{1,0},{2,3},{3,2},{4,5},{5,4},{6,7},{7,6},{8,9},{9,8},{10,11... | collective-permute-start | bytes 786440 | tf_op jit(solution)/shard_map/ppermute | solution.py:596
  70.1 13.2 %collective-permute-start.81 = (f32[680,128]{1,0:T(8,128)S(1)}, f32[680,128]{1,0:T(8,128)S(1)}, u32[]{:S(2)}, u32[]{:S(2)}) collective-permute-start(f32[680,128]{1,0:T(8,128)S(1)} %get-tuple-element.296.refs_9_.refs_4_.refs_7_.refs_6_), channel_id=1, source_target_pairs={{0,15},{1,2},{2,1},{3,4},{4,3},{5,6},{6,5},{7,8},{8,7},{9,10},{10,... | collective-permute-start | bytes 1044488 | tf_op jit(solution)/shard_map/ppermute | solution.py:591
  70.2 7.7 %collective-permute-start.74 = (f32[424,128]{1,0:T(8,128)S(1)}, f32[424,128]{1,0:T(8,128)S(1)}, u32[]{:S(2)}, u32[]{:S(2)}) collective-permute-start(f32[424,128]{1,0:T(8,128)S(1)} %get-tuple-element.294), channel_id=1, source_target_pairs={{0,1},{1,0},{2,3},{3,2},{4,5},{5,4},{6,7},{7,6},{8,9},{9,8},{10,11... | collective-permute-start | bytes 651272 | tf_op jit(solution)/shard_map/ppermute | solution.py:596
  71.3 6.6 %collective-permute-start.73 = (f32[384,128]{1,0:T(8,128)S(1)}, f32[384,128]{1,0:T(8,128)S(1)}, u32[]{:S(2)}, u32[]{:S(2)}) collective-permute-start(f32[384,128]{1,0:T(8,128)S(1)} %get-tuple-element.293), channel_id=1, source_target_pairs={{0,1},{1,0},{2,3},{3,2},{4,5},{5,4},{6,7},{7,6},{8,9},{9,8},{10,11... | collective-permute-start | bytes 589832 | tf_op jit(solution)/shard_map/ppermute | solution.py:596
  77.8 9.1 %collective-permute-start.80 = (f32[640,128]{1,0:T(8,128)S(1)}, f32[640,128]{1,0:T(8,128)S(1)}, u32[]{:S(2)}, u32[]{:S(2)}) collective-permute-start(f32[640,128]{1,0:T(8,128)S(1)} %outer.17.refs_16_.refs_5_.refs_7_), channel_id=1, source_target_pairs={{0,15},{1,2},{2,1},{3,4},{4,3},{5,6},{6,5},{7,8},{8,7},{9,10},{10,... | collective-permute-start | bytes 983048 | tf_op jit(solution)/shard_map/ppermute | solution.py:591
  81.7 7.1 %collective-permute-start.77 = (f32[512,128]{1,0:T(8,128)S(1)}, f32[512,128]{1,0:T(8,128)S(1)}, u32[]{:S(2)}, u32[]{:S(2)}) collective-permute-start(f32[512,128]{1,0:T(8,128)S(1)} %get-tuple-element.299), channel_id=1, source_target_pairs={{0,1},{1,0},{2,3},{3,2},{4,5},{5,4},{6,7},{7,6},{8,9},{9,8},{10,11... | collective-permute-start | bytes 786440 | tf_op jit(solution)/shard_map/ppermute | solution.py:596
  81.8 7.0 %collective-permute-start.79 = (f32[424,128]{1,0:T(8,128)S(1)}, f32[424,128]{1,0:T(8,128)S(1)}, u32[]{:S(2)}, u32[]{:S(2)}) collective-permute-start(f32[424,128]{1,0:T(8,128)S(1)} %get-tuple-element.301), channel_id=1, source_target_pairs={{0,1},{1,0},{2,3},{3,2},{4,5},{5,4},{6,7},{7,6},{8,9},{9,8},{10,11... | collective-permute-start | bytes 651272 | tf_op jit(solution)/shard_map/ppermute | solution.py:596
  82.3 6.5 %collective-permute-start.78 = (f32[384,128]{1,0:T(8,128)S(1)}, f32[384,128]{1,0:T(8,128)S(1)}, u32[]{:S(2)}, u32[]{:S(2)}) collective-permute-start(f32[384,128]{1,0:T(8,128)S(1)} %get-tuple-element.300), channel_id=1, source_target_pairs={{0,1},{1,0},{2,3},{3,2},{4,5},{5,4},{6,7},{7,6},{8,9},{9,8},{10,11... | collective-permute-start | bytes 589832 | tf_op jit(solution)/shard_map/ppermute | solution.py:596
  84.6 20.8 %collective-permute-start.86 = (f32[680,128]{1,0:T(8,128)S(1)}, f32[680,128]{1,0:T(8,128)S(1)}, u32[]{:S(2)}, u32[]{:S(2)}) collective-permute-start(f32[680,128]{1,0:T(8,128)S(1)} %get-tuple-element.303.refs_10_.refs_4_.refs_6_), channel_id=1, source_target_pairs={{0,15},{1,2},{2,1},{3,4},{4,3},{5,6},{6,5},{7,8},{8,7},{9,10},{10,... | collective-permute-start | bytes 1044488 | tf_op jit(solution)/shard_map/ppermute | solution.py:591
  87.9 21.0 %collective-permute-start.85 = (f32[640,128]{1,0:T(8,128)S(1)}, f32[640,128]{1,0:T(8,128)S(1)}, u32[]{:S(2)}, u32[]{:S(2)}) collective-permute-start(f32[640,128]{1,0:T(8,128)S(1)} %outer.19.refs_17_.refs_5_.refs_7_), channel_id=1, source_target_pairs={{0,15},{1,2},{2,1},{3,4},{4,3},{5,6},{6,5},{7,8},{8,7},{9,10},{10,... | collective-permute-start | bytes 983048 | tf_op jit(solution)/shard_map/ppermute | solution.py:591
  92.4 18.7 %collective-permute-start.82 = (f32[512,128]{1,0:T(8,128)S(1)}, f32[512,128]{1,0:T(8,128)S(1)}, u32[]{:S(2)}, u32[]{:S(2)}) collective-permute-start(f32[512,128]{1,0:T(8,128)S(1)} %get-tuple-element.306), channel_id=1, source_target_pairs={{0,1},{1,0},{2,3},{3,2},{4,5},{5,4},{6,7},{7,6},{8,9},{9,8},{10,11... | collective-permute-start | bytes 786440 | tf_op jit(solution)/shard_map/ppermute | solution.py:596
  92.5 18.6 %collective-permute-start.84 = (f32[424,128]{1,0:T(8,128)S(1)}, f32[424,128]{1,0:T(8,128)S(1)}, u32[]{:S(2)}, u32[]{:S(2)}) collective-permute-start(f32[424,128]{1,0:T(8,128)S(1)} %get-tuple-element.308), channel_id=1, source_target_pairs={{0,1},{1,0},{2,3},{3,2},{4,5},{5,4},{6,7},{7,6},{8,9},{9,8},{10,11... | collective-permute-start | bytes 651272 | tf_op jit(solution)/shard_map/ppermute | solution.py:596
  93.0 18.1 %collective-permute-start.83 = (f32[384,128]{1,0:T(8,128)S(1)}, f32[384,128]{1,0:T(8,128)S(1)}, u32[]{:S(2)}, u32[]{:S(2)}) collective-permute-start(f32[384,128]{1,0:T(8,128)S(1)} %get-tuple-element.307), channel_id=1, source_target_pairs={{0,1},{1,0},{2,3},{3,2},{4,5},{5,4},{6,7},{7,6},{8,9},{9,8},{10,11... | collective-permute-start | bytes 589832 | tf_op jit(solution)/shard_map/ppermute | solution.py:596
  106.7 14.2 %collective-permute-start.88 = (f32[640,128]{1,0:T(8,128)S(1)}, f32[640,128]{1,0:T(8,128)S(1)}, u32[]{:S(2)}, u32[]{:S(2)}) collective-permute-start(f32[640,128]{1,0:T(8,128)S(1)} %get-tuple-element.310.refs_10_.refs_6_.refs_4_), channel_id=1, source_target_pairs={{0,15},{1,2},{2,1},{3,4},{4,3},{5,6},{6,5},{7,8},{8,7},{9,10},{10,... | collective-permute-start | bytes 983048 | tf_op jit(solution)/shard_map/ppermute | solution.py:591
  109.8 12.8 %collective-permute-start.87 = (f32[640,128]{1,0:T(8,128)S(1)}, f32[640,128]{1,0:T(8,128)S(1)}, u32[]{:S(2)}, u32[]{:S(2)}) collective-permute-start(f32[640,128]{1,0:T(8,128)S(1)} %outer.21.refs_17_.refs_7_.refs_5_), channel_id=1, source_target_pairs={{0,15},{1,2},{2,1},{3,4},{4,3},{5,6},{6,5},{7,8},{8,7},{9,10},{10,... | collective-permute-start | bytes 983048 | tf_op jit(solution)/shard_map/ppermute | solution.py:591
  114.8 2.2 %collective-permute-start.89 = (f32[512,128]{1,0:T(8,128)S(1)}, f32[512,128]{1,0:T(8,128)S(1)}, u32[]{:S(2)}, u32[]{:S(2)}) collective-permute-start(f32[512,128]{1,0:T(8,128)S(1)} %get-tuple-element.314), channel_id=1, source_target_pairs={{0,1},{1,0},{2,3},{3,2},{4,5},{5,4},{6,7},{7,6},{8,9},{9,8},{10,11... | collective-permute-start | bytes 786440 | tf_op jit(solution)/shard_map/ppermute | solution.py:596
  114.8 1.8 %collective-permute-start.90 = (f32[384,128]{1,0:T(8,128)S(1)}, f32[384,128]{1,0:T(8,128)S(1)}, u32[]{:S(2)}, u32[]{:S(2)}) collective-permute-start(f32[384,128]{1,0:T(8,128)S(1)} %get-tuple-element.315), channel_id=1, source_target_pairs={{0,1},{1,0},{2,3},{3,2},{4,5},{5,4},{6,7},{7,6},{8,9},{9,8},{10,11... | collective-permute-start | bytes 589832 | tf_op jit(solution)/shard_map/ppermute | solution.py:596
  115.3 1.6 %collective-permute-start.91 = (f32[384,128]{1,0:T(8,128)S(1)}, f32[384,128]{1,0:T(8,128)S(1)}, u32[]{:S(2)}, u32[]{:S(2)}) collective-permute-start(f32[384,128]{1,0:T(8,128)S(1)} %get-tuple-element.316), channel_id=1, source_target_pairs={{0,1},{1,0},{2,3},{3,2},{4,5},{5,4},{6,7},{7,6},{8,9},{9,8},{10,11... | collective-permute-start | bytes 589832 | tf_op jit(solution)/shard_map/ppermute | solution.py:596

commit v2 on v1

--- a/solution.py
+++ b/solution.py
@@ -12,7 +12,6 @@
 COMPS = 5
 CHUNK = 32
 STRIP = 8
-EDGE = 4
 NEED = 6
 HALF = 32
 PARTS = 2
@@ -84,10 +83,10 @@
         index -= count
 
 
-def pieces(refs, row, size):
+def pieces(refs, row, size, first=0):
     def read(c, r, n):
-        at, index = piece_of(c * 2 + row) if len(refs) > 1 else (0, c * 2 + row)
-        return refs[at][pl.ds(index * size + r, n), :]
+        at, index = piece_of(c * 2 + row)
+        return refs[at][pl.ds(index * size + r - first, n), :]
 
     return read
 
@@ -175,17 +174,17 @@
     return advance(coef[1 - side], cur, up, down, low, high, behind, ahead, kept, eddy)
 
 
-def edge_of(ref, side, c, separate, offset):
-    if separate:
+def edge_of(ref, side, c, plan, offset):
+    if plan.n == 1:
         return ref[side, c]
-    got = ref[pl.ds(offset + EDGE * (side * COMPS + c), EDGE), :]
-    rest = jnp.zeros((STRIP - EDGE, got.shape[1]), jnp.float32)
+    got = ref[pl.ds(offset + (plan.edge + 1) * (side * COMPS + c), plan.edge + 1), :]
+    rest = jnp.zeros((STRIP - got.shape[0], got.shape[1]), jnp.float32)
     return jnp.concatenate([got, rest] if side == 0 else [rest, got], axis=0)
 
 
-def put_edge(ref, side, c, value, offset):
-    start = 0 if side == 0 else STRIP - EDGE
-    ref[pl.ds(offset + EDGE * (side * COMPS + c), EDGE), :] = value[start : start + EDGE]
+def put_edge(ref, side, c, value, plan, offset):
+    start = 0 if side == 0 else STRIP - plan.edge
+    ref[pl.ds(offset + plan.edge * (side * COMPS + c), plan.edge), :] = value[start : start + plan.edge]
 
 
 class Plan:
@@ -198,7 +197,8 @@
         self.early = n <= len(SECTION_WEIGHTS)
         self.final = n == self.total
         self.strips = n < self.total
-        self.edges = n < self.total - 1
+        self.edge = self.total - 1 - n
+        self.edges = self.edge > 0
 
 
 def place_of(depth):
@@ -214,7 +214,9 @@
     mine = [refs.pop(0) for _ in range(PARTS)]
     now = refs.pop(0)
     base = None if plan.early else refs.pop(0)
-    across, strip = refs.pop(0), refs.pop(0)
+    split = plan.n == 1 and p == PARTS - 1
+    across = [refs.pop(0) for _ in PIECES] if split else refs.pop(0)
+    strip = refs.pop(0)
     works = p == 0 and plan.strips
     if works:
         edges = refs.pop(0) if plan.n == 1 else across
@@ -243,7 +245,8 @@
             part = lambda ref: part_rows(ref, row, plan, p)
             inside = part(inner) if plan.n == 1 else plain_rows(inner, row, 0)
             update_rows(
-                row, r0, radial, lambda c: row * COMPS + c, joined(mine, row, size), part(across), inside,
+                row, r0, radial, lambda c: row * COMPS + c, joined(mine, row, size),
+                pieces(across, row, size, p * size) if split else part(across), inside,
                 None if plan.early else part(base), part(now), part(prev), lambda r, n: eddy[row, pl.ds(r, n), :], columns,
                 coef, store,
             )
@@ -264,7 +267,7 @@
         for side in range(2):
             result = strip_layer(
                 coef, side, [strip[side, c] for c in every],
-                [edge_of(edges, side, c, plan.n == 1, 2 * COMPS * size) for c in every],
+                [edge_of(edges, side, c, plan, 2 * COMPS * size) for c in every],
                 [strip_inner[side, c, 0] for c in every], [lines[pl.ds(side * COMPS + c, 1), :] for c in every],
                 [strip_base[side, c] for c in every], [strip_now[side, c] for c in every],
                 [strip_prev[side, c] for c in every], strip_eddy[side],
@@ -272,7 +275,7 @@
             for c in every:
                 strip_out[side, c] = result[c]
                 if plan.edges:
-                    put_edge(out, side, c, result[c], 2 * COMPS * size)
+                    put_edge(out, side, c, result[c], plan, 2 * COMPS * size)
 
 
 def inner_kernel(plan, refs):
@@ -283,7 +286,7 @@
     if plan.n == 1:
         inner = now
     outer = [refs.pop(0) for _ in range(PARTS)]
-    partner = [refs.pop(0) for _ in range(1 if plan.n == 1 else len(PIECES))]
+    partner = [refs.pop(0) for _ in PIECES]
     base = None if plan.early else refs.pop(0)
     if plan.strips:
         edges = refs.pop(0) if plan.n == 1 else partner[-1]
@@ -336,7 +339,7 @@
                 if j < depth - 1:
                     down = [strip[side, c, j + 1] for c in every]
                 else:
-                    down = [edge_of(edges, side, c, plan.n == 1, plan.piece) for c in every]
+                    down = [edge_of(edges, side, c, plan, plan.piece) for c in every]
                 result = strip_layer(
                     coef, side, [strip[side, c, j] for c in every],
                     [strip_outer[side, c] if j == 0 else strip[side, c, j - 1] for c in every], down,
@@ -347,7 +350,7 @@
                 for c in every:
                     strip_out[side, c, j] = result[c]
                     if j == depth - 1 and plan.edges:
-                        put_edge(border[-1], side, c, result[c], plan.piece)
+                        put_edge(border[-1], side, c, result[c], plan, plan.piece)
 
 
 def strip_items():
@@ -372,7 +375,8 @@
     _, _, cells, radial, axial = now.shape
     rotor, stator, *parts = outs[: 2 + PARTS]
     next_parts, prev_parts = outs[2 + PARTS : 2 + 2 * PARTS], outs[2 + 2 * PARTS : 2 + 3 * PARTS]
-    border, eddy_outer, now_held, prev_held, eddy_held, in_sems, out_sems = outs[2 + 3 * PARTS :]
+    border, rest = outs[2 + 3 * PARTS :][: len(PIECES)], outs[2 + 3 * PARTS + len(PIECES) :]
+    late, (eddy_outer, now_held, prev_held, eddy_held, in_sems, out_sems) = rest[: len(PIECES)], rest[len(PIECES) :]
     size = radial // PARTS
     _, _, cells, radial, axial = now.shape
     depth = cells - 1
@@ -403,9 +407,12 @@
             for q, ((kind, c, _, _), t) in enumerate(items[p : p + per_tile]):
                 if t == 0:
                     reads[row, kind, c].wait()
-                    rows = pl.ds((c * 2 + row) * radial, radial)
                     if kind == 0:
-                        write(now_held.at[c, row, first + step * depth], border.at[rows, :])
+                        at_piece, index = piece_of(c * 2 + row)
+                        target = border[at_piece].at[pl.ds(index * radial, radial), :]
+                        write(now_held.at[c, row, first + step * depth], target)
+                        target = late[at_piece].at[pl.ds(index * size, size), :]
+                        write(now_held.at[c, row, first, pl.ds(radial - size, size), :], target)
                     if kind < 2:
                         sources = ((now_held, first, parts), (now_held, first + step, next_parts)) if kind == 0 else ()
                         for held, at_layer, targets in sources or ((prev_held, first, prev_parts),):
@@ -540,23 +547,25 @@
     cells, radial, axial = now.shape[2:]
     strips = pltpu.VMEM((2 * HALF * cells + HALF, radial), jnp.float32)
     part = pltpu.HBM((2 * COMPS * radial // PARTS, axial), jnp.float32)
-    layer = pltpu.HBM((2 * COMPS * radial, axial), jnp.float32)
+    border = [pltpu.HBM((count * radial, axial), jnp.float32) for count in PIECES]
+    late = [pltpu.HBM((count * radial // PARTS, axial), jnp.float32) for count in PIECES]
     plane = pltpu.HBM((2, radial, axial), jnp.float32)
     reads = pltpu.SemaphoreType.DMA((2 * (2 * COMPS + 1),))
-    writes = pltpu.SemaphoreType.DMA((2 * (COMPS + 1 + 3 * COMPS * PARTS),))
+    writes = pltpu.SemaphoreType.DMA((2 * (2 * COMPS + 1 + 3 * COMPS * PARTS),))
     held = [pltpu.VMEM(x.shape, jnp.float32) for x in (now, prev, eddy)]
     got = pl.pallas_call(
         gather_kernel,
-        out_shape=(strips,) * 2 + (part,) * (3 * PARTS) + (layer, plane),
+        out_shape=(strips,) * 2 + (part,) * (3 * PARTS) + (*border, *late, plane),
         in_specs=[ANY] * 4,
-        out_specs=(VMEM,) * 2 + (ANY,) * (3 * PARTS + 2),
+        out_specs=(VMEM,) * 2 + (ANY,) * (3 * PARTS + 1 + 2 * len(PIECES)),
         scratch_shapes=[*held, reads, writes],
         compiler_params=pltpu.CompilerParams(vmem_limit_bytes=16 << 20),
         cost_estimate=pl.CostEstimate(flops=1, bytes_accessed=1, transcendentals=0),
         name="gather_strips",
     )(*(in_hbm(x) for x in (now, prev, eddy)), ordered)
     at = [2 + i * PARTS for i in range(4)]
-    return got[:2], *(got[i : i + PARTS] for i in at[:3]), *got[at[3] :]
+    ends = at[3] + len(PIECES)
+    return got[:2], *(got[i : i + PARTS] for i in at[:3]), got[at[3] : ends], got[ends:-1], got[-1]
 
 
 def call_align(within, strips, cells):
@@ -596,23 +605,23 @@
     return lax.ppermute(value, "theta", [(i, i ^ 1) for i in range(count)])
 
 
-def faced(outer, border, rotor, stator, sectors):
+def faced(outer, rotor, stator, sectors):
     count = lax.axis_size("theta")
     if count <= 16:
 
         def branch(steps):
-            def exchange(outer, border, rotor, stator):
-                return across_chips(outer), within_chip(border), shifted(rotor, steps), shifted(stator, -steps)
+            def exchange(outer, rotor, stator):
+                return [across_chips(x) for x in outer], shifted(rotor, steps), shifted(stator, -steps)
 
             return exchange
 
-        return lax.switch(sectors, [branch(i) for i in range(count)], outer, border, rotor, stator)
+        return lax.switch(sectors, [branch(i) for i in range(count)], outer, rotor, stator)
     amounts = jnp.stack([sectors, count - sectors]) % count
     stacked = jnp.stack([rotor, stator])
     for level in range((count - 1).bit_length()):
         taken = ((amounts >> level) & 1) == 1
         stacked = jnp.where(taken[:, None, None], shifted(stacked, 1 << level), stacked)
-    return across_chips(outer), within_chip(border), stacked[0], stacked[1]
+    return [across_chips(x) for x in outer], stacked[0], stacked[1]
 
 
 def per_device(state_now, state_prev, eddy_visc, mean_flow, offset):
@@ -626,12 +635,14 @@
 
     early = call_border(state_now)
     across = [across_chips(early)]
-    strips, outer, next_layer, prev_outer, border, eddy_outer = call_gather(state_now, state_prev, eddy_visc, early)
+    strips, outer, next_layer, prev_outer, border, late, eddy_outer = call_gather(
+        state_now, state_prev, eddy_visc, early
+    )
     rotor, stator = call_align(shift_cells % cells, strips, cells)
     sectors = lax.optimization_barrier((shift_cells // cells, across))[0]
-    late, border, rotor, stator = faced(outer[-1], border, rotor, stator, sectors)
+    late, rotor, stator = faced(late, rotor, stator, sectors)
     across.append(late)
-    partner = [border]
+    partner = [within_chip(x) for x in border]
     now_out, now_in, prev_out, prev_in, eddy_out, eddy_in, edge_across, edge_within = call_scatter(
         rotor, stator, cells
     )
@@ -648,11 +659,12 @@
 
             def outer_call(p, ordered):
                 arrays = [eddy_outer, prev_outer[p], next_layer[p] if n == 1 else inner, *outer, now_outer[p]]
-                arrays += [across[p]] if plan.early else [base_outer[p], across[p]]
+                arrays += [] if plan.early else [base_outer[p]]
+                arrays += across[p] if n == 1 and p == PARTS - 1 else [across[p]]
                 held, arrays = len(arrays), arrays + [strip_out]
                 outs = [pltpu.VMEM((2 * COMPS * size, axial), f32)]
                 if p == 0 and plan.edges:
-                    outs = [pltpu.VMEM((2 * COMPS * (size + EDGE), axial), f32)]
+                    outs = [pltpu.VMEM((2 * COMPS * (size + plan.edge), axial), f32)]
                 if p == 0 and plan.strips:
                     arrays += [edge_across] if n == 1 else []
                     arrays += [strip_in, now_out, prev_out, eddy_out, base_out]
@@ -675,7 +687,7 @@
                     arrays += [edge_within] if n == 1 else []
                     arrays += [strip_out, now_in, prev_in, eddy_in, base_in, ordered]
                     outs += [pltpu.VMEM((count * radial, axial), f32) for count in PIECES[:-1]]
-                    rows = plan.piece + (2 * COMPS * EDGE if plan.edges else 0)
+                    rows = plan.piece + 2 * COMPS * plan.edge
                     outs += [pltpu.VMEM((rows, axial), f32), pltpu.VMEM(strip_in.shape, f32)]
                 scratch = [square, square]
                 if plan.final:
@@ -690,13 +702,14 @@
                 for p in range(PARTS):
                     made = outer_call(p, made)
                 return made
-            new_outer = []
-            for p in range(PARTS):
-                got = outer_call(p, new_outer[-1] if p else None)
-                new_outer.append(got[0])
-                if p == 0:
-                    new_strip_out = got[1]
-            made = inner_call(new_outer[-1])
+            got, new_strip_out = outer_call(0, None)
+            new_outer = [got]
+            if n > 1:
+                made = inner_call(got)
+            for p in range(1, PARTS):
+                new_outer.append(outer_call(p, made[1] if n > 1 else new_outer[-1])[0])
+            if n == 1:
+                made = inner_call(new_outer[-1])
             across = [across_chips(x) for x in new_outer]
             partner = [within_chip(x) for x in made[1:-1]]
             inner, strip_in = made[0], made[-1]

time: 123 us -> 118 us (0.959)
  the two profiles are of different devices: /device:TPU:13 before, /device:TPU:1 now
where the time goes in v2:
time: 118 us
  Pallas kernels  46.5 us (39%)
  starting transfers between devices  46 us (39%)
  waiting for transfers between devices  24.2 us (21%)
  between operations  1.43 us (1%)
    pallas_call x20, Pallas kernels, run(): pl.pallas_call(lambda *refs: kernel(list(refs)), out_shape=outs, in_specs...  39.9 us
    ppermute x14, starting transfers between devices, across_chips(): return lax.ppermute(value, 'theta', pairs)  23.5 us
    ppermute x14, waiting for transfers between devices, across_chips(): return lax.ppermute(value, 'theta', pairs)  19.6 us
    ppermute x18, starting transfers between devices, within_chip(): return lax.ppermute(value, 'theta', [(i, i ^ 1) for i in range(count)])  15.9 us
    ppermute x4, starting transfers between devices, shifted(): lax.ppermute(value, 'theta', [(i, (i + steps) % count) for i in range(cou...  6.59 us
    pallas_call x1, Pallas kernels, call_gather(): pl.pallas_call(gather_kernel, out_shape=(strips,) * 2 + (part,) * (3 * PA...  5.66 us
    ppermute x4, waiting for transfers between devices, shifted(): lax.ppermute(value, 'theta', [(i, (i + steps) % count) for i in range(cou...  3.36 us
  transfers between devices with their start and end apart: 36, of which 12 were waited for; matrix products, arithmetic and copies ran while one was open for 0% of the time, Pallas kernels for 37%

profile of v2, /device:TPU:1, one launch (start us, length us, event | category | flops | bytes accessed | tf_op | source)
XLA Modules:
  0.0 118.5 jit_solution(7875564786874201962)
XLA Ops:
  0.0 1.0 outer_layer.1._
  1.0 2.7 %collective-permute-start.80 = (f32[640,128]{1,0:T(8,128)S(1)}, f32[640,128]{1,0:T(8,128)S(1)}, u32[]{:S(2)}, u32[]{:S(2)}) collective-permute-start(f32[640,128]{1,0:T(8,128)S(1)} %outer_layer.1._), channel_id=1, source_target_pairs={{0,15},{1,2},{2,1},{3,4},{4,3},{5,6},{6,5},{7,8},{8,7},{9,10},{10,... | collective-permute-start | bytes 983048 | tf_op jit(solution)/shard_map/ppermute | solution.py:600
  3.7 5.7 %gather_strips.1 = (f32[288,128]{1,0:T(8,128)S(1)}, f32[288,128]{1,0:T(8,128)S(1)}, f32[640,128]{1,0:T(8,128)}, f32[640,128]{1,0:T(8,128)}, f32[640,128]{1,0:T(8...) custom-call(f32[5,2,4,128,128]{4,3,2,1,0:T(8,128)} %refs_3_.11, ...), custom_call_target="tpu_custom_call" | custom-call | flops 1 | bytes 1 | tf_op jit(solution)/shard_map/gather_strips/pallas_call | solution.py:556
  9.4 2.9 %collective-permute-start.82 = (f32[288,128]{1,0:T(8,128)S(1)}, f32[288,128]{1,0:T(8,128)S(1)}, u32[]{:S(2)}, u32[]{:S(2)}) collective-permute-start(f32[288,128]{1,0:T(8,128)S(1)} %get-tuple-element.318.refs_2_), channel_id=1, source_target_pairs={{0,15},{1,0},{2,1},{3,2},{4,3},{5,4},{6,5},{7,6},{8,7},{9,8},{10,9... | collective-permute-start | bytes 442376 | tf_op jit(solution)/shard_map/ppermute | solution.py:594
  13.1 0.9 collective-permute-done.82.refs_4_
  14.1 16.7 %conditional.1 = (f32[256,128]{1,0:T(8,128)}, f32[192,128]{1,0:T(8,128)}, f32[192,128]{1,0:T(8,128)}, f32[320,128]{1,0:T(8,128)}, f32[320,128]{1,0:T(8,128)}) conditional(s32[]{:T(128)} %clamp.3, (f32[256,128]{1,0:T(8,128)}, f32[192,128]{1,0:T(8,128)}, f32[192,128]{1,0:T(8,128)}, f32[320,128]{1,0:T(8,128)S(1)}, ...), branch_computations={%region_0.1_spmd, %region_1.2_spmd, %region_2.3_spmd, %region_3.4_... | conditional | bytes 2621680 | solution.py:618
  14.2 2.9 %collective-permute-start.38 = (f32[320,128]{1,0:T(8,128)S(1)}, f32[320,128]{1,0:T(8,128)}, u32[]{:S(2)}, u32[]{:S(2)}) collective-permute-start(f32[320,128]{1,0:T(8,128)S(1)} %get-tuple-element.203), channel_id=1, source_target_pairs={{0,7},{1,8},{2,9},{3,10},{4,11},{5,12},{6,13},{7,14},{8,15},{9,0},... | collective-permute-start | bytes 491528 | tf_op jit(solution)/shard_map/cond/branch_7_fun/ppermute | solution.py:594
  17.1 0.7 collective-permute-start.39
  17.8 2.0 %collective-permute-start.35 = (f32[256,128]{1,0:T(8,128)}, f32[256,128]{1,0:T(8,128)}, u32[]{:S(2)}, u32[]{:S(2)}) collective-permute-start(f32[256,128]{1,0:T(8,128)} %get-tuple-element.200), channel_id=1, source_target_pairs={{0,15},{1,2},{2,1},{3,4},{4,3},{5,6},{6,5},{7,8},{8,7},{9,10},{10,... | collective-permute-start | bytes 393224 | tf_op jit(solution)/shard_map/cond/branch_7_fun/ppermute | solution.py:600
  19.8 1.7 %collective-permute-start.37 = (f32[192,128]{1,0:T(8,128)}, f32[192,128]{1,0:T(8,128)}, u32[]{:S(2)}, u32[]{:S(2)}) collective-permute-start(f32[192,128]{1,0:T(8,128)} %get-tuple-element.202), channel_id=1, source_target_pairs={{0,15},{1,2},{2,1},{3,4},{4,3},{5,6},{6,5},{7,8},{8,7},{9,10},{10,... | collective-permute-start | bytes 294920 | tf_op jit(solution)/shard_map/cond/branch_7_fun/ppermute | solution.py:600
  21.5 5.8 %collective-permute-done.36 = f32[192,128]{1,0:T(8,128)} collective-permute-done((f32[192,128]{1,0:T(8,128)}, f32[192,128]{1,0:T(8,128)}, u32[]{:S(2)}, u32[]{:S(2)}) %collective-permute-start.36) | collective-permute-done | bytes 98336 | tf_op jit(solution)/shard_map/cond/branch_7_fun/ppermute | solution.py:600
  27.4 1.1 collective-permute-done.37
  28.4 2.4 %collective-permute-done.39 = f32[320,128]{1,0:T(8,128)} collective-permute-done((f32[320,128]{1,0:T(8,128)S(1)}, f32[320,128]{1,0:T(8,128)}, u32[]{:S(2)}, u32[]{:S(2)}) %collective-permute-start.39) | collective-permute-done | bytes 163872 | tf_op jit(solution)/shard_map/cond/branch_7_fun/ppermute | solution.py:594
  30.8 5.9 %collective-permute-start.83 = (f32[512,128]{1,0:T(8,128)}, f32[512,128]{1,0:T(8,128)S(1)}, u32[]{:S(2)}, u32[]{:S(2)}) collective-permute-start(f32[512,128]{1,0:T(8,128)} %get-tuple-element.326), channel_id=1, source_target_pairs={{0,1},{1,0},{2,3},{3,2},{4,5},{5,4},{6,7},{7,6},{8,9},{9,8},{10,11... | collective-permute-start | bytes 786440 | tf_op jit(solution)/shard_map/ppermute | solution.py:605
  37.4 1.1 scatter_strips.1
  38.6 2.3 %outer.12 = (f32[680,128]{1,0:T(8,128)S(1)}, f32[2,5,8,128]{3,2,1,0:T(8,128)S(1)}) custom-call(f32[16]{0:T(128)S(1)} %concatenate.7.refs_0_, f32[2,128,128]{2,1,0:T(8,128)} %get-tuple-element.311.refs_1_, f32[640,128]{1,0:T(8,128)} %get-tuple-element.337.refs_2_, f32[640,128]{1,0:T(8,128)} %get-tuple-element.338.refs_3_, ...), custom_call_target="tpu_custom_call" | custom-call | flops 1 | bytes 1 | tf_op jit(solution)/shard_map/outer/pallas_call | solution.py:519
  41.0 1.9 %outer.13.refs_17_.refs_5_.refs_7_ = f32[640,128]{1,0:T(8,128)S(1)} custom-call(f32[16]{0:T(128)S(1)} %concatenate.7.refs_0_, f32[2,128,128]{2,1,0:T(8,128)} %get-tuple-element.311.refs_1_, f32[640,128]{1,0:T(8,128)} %get-tuple-element.312.refs_2_, f32[640,128]{1,0:T(8,128)} %get-tuple-element.333.refs_3_, f32[640,128]{1,0:T(8,128)} %get-tuple-element.324.refs_4_.refs_6_, ...), custom_call_target="tpu_custom_call" | custom-call | flops 1 | bytes 1 | tf_op jit(solution)/shard_map/outer/pallas_call | solution.py:519
  42.9 1.8 %collective-permute-start.90 = (f32[640,128]{1,0:T(8,128)S(1)}, f32[640,128]{1,0:T(8,128)S(1)}, u32[]{:S(2)}, u32[]{:S(2)}) collective-permute-start(f32[640,128]{1,0:T(8,128)S(1)} %outer.13.refs_17_.refs_5_.refs_7_), channel_id=1, source_target_pairs={{0,15},{1,2},{2,1},{3,4},{4,3},{5,6},{6,5},{7,8},{8,7},{9,10},{10,... | collective-permute-start | bytes 983048 | tf_op jit(solution)/shard_map/ppermute | solution.py:600
  44.8 3.4 %inner.6 = (f32[5,2,3,128,128]{4,3,2,1,0:T(8,128)S(1)}, f32[512,128]{1,0:T(8,128)S(1)}, f32[384,128]{1,0:T(8,128)S(1)}, f32[424,128]{1,0:T(8,128)S(1)}, f32[2,5,3,8,128]{4,3,2,1,0:T(8,128)S(1)}) custom-call(f32[16]{0:T(128)S(1)} %concatenate.7.refs_0_, f32[2,4,128,128]{3,2,1,0:T(8,128)S(1)} %copy-done.4, f32[5,2,4,128,128]{4,3,2,1,0:T(8,128)S(1)} %copy-done.1, ...), custom_call_target="tpu_custom_call" | custom-call | flops 1 | bytes 1 | tf_op jit(solution)/shard_map/inner/pallas_call | solution.py:519
  48.2 2.8 %collective-permute-start.86 = (f32[512,128]{1,0:T(8,128)S(1)}, f32[512,128]{1,0:T(8,128)S(1)}, u32[]{:S(2)}, u32[]{:S(2)}) collective-permute-start(f32[512,128]{1,0:T(8,128)S(1)} %get-tuple-element.345), channel_id=1, source_target_pairs={{0,1},{1,0},{2,3},{3,2},{4,5},{5,4},{6,7},{7,6},{8,9},{9,8},{10,11... | collective-permute-start | bytes 786440 | tf_op jit(solution)/shard_map/ppermute | solution.py:605
  51.6 0.9 collective-permute-done.89.refs_7_
  52.4 1.3 %outer.14 = (f32[670,128]{1,0:T(8,128)S(1)}, f32[2,5,8,128]{3,2,1,0:T(8,128)S(1)}) custom-call(f32[16]{0:T(128)S(1)} %concatenate.7.refs_0_, f32[2,128,128]{2,1,0:T(8,128)S(1)} %copy-done.5, f32[640,128]{1,0:T(8,128)S(1)} %copy-done.7, f32[5,2,3,128,128]{4,3,2,1,0:T(8,128)S(1)} %get-tuple-element.343.refs_3_.refs_4_, ...), custom_call_target="tpu_custom_call" | custom-call | flops 1 | bytes 1 | tf_op jit(solution)/shard_map/outer/pallas_call | solution.py:519
  53.7 6.2 %collective-permute-start.94 = (f32[670,128]{1,0:T(8,128)S(1)}, f32[670,128]{1,0:T(8,128)S(1)}, u32[]{:S(2)}, u32[]{:S(2)}) collective-permute-start(f32[670,128]{1,0:T(8,128)S(1)} %get-tuple-element.349.refs_16_.refs_4_.refs_6_), channel_id=1, source_target_pairs={{0,15},{1,2},{2,1},{3,4},{4,3},{5,6},{6,5},{7,8},{8,7},{9,10},{10,... | collective-permute-start | bytes 1029128 | tf_op jit(solution)/shard_map/ppermute | solution.py:600
  60.0 3.6 %inner.7 = (f32[5,2,3,128,128]{4,3,2,1,0:T(8,128)S(1)}, f32[512,128]{1,0:T(8,128)S(1)}, f32[384,128]{1,0:T(8,128)S(1)}, f32[414,128]{1,0:T(8,128)S(1)}, f32[2,5,3,8,128]{4,3,2,1,0:T(8,128)S(1)}) custom-call(f32[16]{0:T(128)S(1)} %concatenate.7.refs_0_, f32[2,4,128,128]{3,2,1,0:T(8,128)S(1)} %copy-done.4, f32[5,2,4,128,128]{4,3,2,1,0:T(8,128)S(1)} %copy-done.1, ...), custom_call_target="tpu_custom_call" | custom-call | flops 1 | bytes 1 | tf_op jit(solution)/shard_map/inner/pallas_call | solution.py:519
  63.6 1.0 outer.15.refs_5_.refs_7_
  64.6 2.1 %collective-permute-start.95 = (f32[640,128]{1,0:T(8,128)S(1)}, f32[640,128]{1,0:T(8,128)S(1)}, u32[]{:S(2)}, u32[]{:S(2)}) collective-permute-start(f32[640,128]{1,0:T(8,128)S(1)} %outer.15.refs_5_.refs_7_), channel_id=1, source_target_pairs={{0,15},{1,2},{2,1},{3,4},{4,3},{5,6},{6,5},{7,8},{8,7},{9,10},{10,... | collective-permute-start | bytes 983048 | tf_op jit(solution)/shard_map/ppermute | solution.py:600
  67.2 1.2 %outer.16 = (f32[660,128]{1,0:T(8,128)S(1)}, f32[2,5,8,128]{3,2,1,0:T(8,128)S(1)}) custom-call(f32[16]{0:T(128)S(1)} %concatenate.7.refs_0_, f32[2,128,128]{2,1,0:T(8,128)S(1)} %copy-done.5, f32[640,128]{1,0:T(8,128)S(1)} %copy-done.7, f32[5,2,3,128,128]{4,3,2,1,0:T(8,128)S(1)} %get-tuple-element.350.refs_3_.refs_4_, ...), custom_call_target="tpu_custom_call" | custom-call | flops 1 | bytes 1 | tf_op jit(solution)/shard_map/outer/pallas_call | solution.py:519
  68.5 2.2 %collective-permute-start.99 = (f32[660,128]{1,0:T(8,128)S(1)}, f32[660,128]{1,0:T(8,128)S(1)}, u32[]{:S(2)}, u32[]{:S(2)}) collective-permute-start(f32[660,128]{1,0:T(8,128)S(1)} %get-tuple-element.356.refs_16_.refs_4_.refs_7_.refs_6_), channel_id=1, source_target_pairs={{0,15},{1,2},{2,1},{3,4},{4,3},{5,6},{6,5},{7,8},{8,7},{9,10},{10,... | collective-permute-start | bytes 1013768 | tf_op jit(solution)/shard_map/ppermute | solution.py:600
  70.6 3.6 %inner.8 = (f32[5,2,3,128,128]{4,3,2,1,0:T(8,128)S(1)}, f32[512,128]{1,0:T(8,128)S(1)}, f32[384,128]{1,0:T(8,128)S(1)}, f32[404,128]{1,0:T(8,128)S(1)}, f32[2,5,3,8,128]{4,3,2,1,0:T(8,128)S(1)}) custom-call(f32[16]{0:T(128)S(1)} %concatenate.7.refs_0_, f32[2,4,128,128]{3,2,1,0:T(8,128)S(1)} %copy-done.4, f32[5,2,4,128,128]{4,3,2,1,0:T(8,128)S(1)} %copy-done.1, ...), custom_call_target="tpu_custom_call" | custom-call | flops 1 | bytes 1 | tf_op jit(solution)/shard_map/inner/pallas_call | solution.py:519
  74.5 1.0 outer.17.refs_5_.refs_7_
  75.6 2.8 %collective-permute-start.96 = (f32[512,128]{1,0:T(8,128)S(1)}, f32[512,128]{1,0:T(8,128)S(1)}, u32[]{:S(2)}, u32[]{:S(2)}) collective-permute-start(f32[512,128]{1,0:T(8,128)S(1)} %get-tuple-element.359.refs_9_), channel_id=1, source_target_pairs={{0,1},{1,0},{2,3},{3,2},{4,5},{5,4},{6,7},{7,6},{8,9},{9,8},{10,11... | collective-permute-start | bytes 786440 | tf_op jit(solution)/shard_map/ppermute | solution.py:605
  78.9 1.5 %collective-permute-done.99.refs_8_ = f32[660,128]{1,0:T(8,128)S(1)} collective-permute-done((f32[660,128]{1,0:T(8,128)S(1)}, f32[660,128]{1,0:T(8,128)S(1)}, u32[]{:S(2)}, u32[]{:S(2)}) %collective-permute-start.99) | collective-permute-done | bytes 337952 | tf_op jit(solution)/shard_map/ppermute | solution.py:600
  80.5 1.3 %outer.18 = (f32[650,128]{1,0:T(8,128)S(1)}, f32[2,5,8,128]{3,2,1,0:T(8,128)S(1)}) custom-call(f32[16]{0:T(128)S(1)} %concatenate.7.refs_0_, f32[2,128,128]{2,1,0:T(8,128)S(1)} %copy-done.5, f32[640,128]{1,0:T(8,128)S(1)} %copy-done.7, f32[5,2,3,128,128]{4,3,2,1,0:T(8,128)S(1)} %get-tuple-element.357.refs_3_.refs_4_.refs_11_, ...), custom_call_target="tpu_custom_call" | custom-call | flops 1 | bytes 1 | tf_op jit(solution)/shard_map/outer/pallas_call | solution.py:519
  81.9 3.7 %inner.9 = (f32[5,2,3,128,128]{4,3,2,1,0:T(8,128)S(1)}, f32[512,128]{1,0:T(8,128)S(1)}, f32[384,128]{1,0:T(8,128)S(1)}, f32[394,128]{1,0:T(8,128)S(1)}, f32[2,5,3,8,128]{4,3,2,1,0:T(8,128)S(1)}) custom-call(f32[16]{0:T(128)S(1)} %concatenate.7.refs_0_, f32[2,4,128,128]{3,2,1,0:T(8,128)S(1)} %copy-done.4, f32[5,2,4,128,128]{4,3,2,1,0:T(8,128)S(1)} %copy-done.1, ...), custom_call_target="tpu_custom_call" | custom-call | flops 1 | bytes 1 | tf_op jit(solution)/shard_map/inner/pallas_call | solution.py:519
  85.6 6.6 %collective-permute-done.100.refs_8_ = f32[640,128]{1,0:T(8,128)S(1)} collective-permute-done((f32[640,128]{1,0:T(8,128)S(1)}, f32[640,128]{1,0:T(8,128)S(1)}, u32[]{:S(2)}, u32[]{:S(2)}) %collective-permute-start.100) | collective-permute-done | bytes 327712 | tf_op jit(solution)/shard_map/ppermute | solution.py:600
  92.2 1.0 outer.19.refs_5_.refs_7_
  93.2 2.5 %collective-permute-start.105 = (f32[640,128]{1,0:T(8,128)S(1)}, f32[640,128]{1,0:T(8,128)S(1)}, u32[]{:S(2)}, u32[]{:S(2)}) collective-permute-start(f32[640,128]{1,0:T(8,128)S(1)} %outer.19.refs_5_.refs_7_), channel_id=1, source_target_pairs={{0,15},{1,2},{2,1},{3,4},{4,3},{5,6},{6,5},{7,8},{8,7},{9,10},{10,... | collective-permute-start | bytes 983048 | tf_op jit(solution)/shard_map/ppermute | solution.py:600
  96.3 1.9 %collective-permute-done.104.refs_8_ = f32[650,128]{1,0:T(8,128)S(1)} collective-permute-done((f32[650,128]{1,0:T(8,128)S(1)}, f32[650,128]{1,0:T(8,128)S(1)}, u32[]{:S(2)}, u32[]{:S(2)}) %collective-permute-start.104) | collective-permute-done | bytes 332832 | tf_op jit(solution)/shard_map/ppermute | solution.py:600
  98.2 1.2 %outer.20 = (f32[640,128]{1,0:T(8,128)S(1)}, f32[2,5,8,128]{3,2,1,0:T(8,128)S(1)}) custom-call(f32[16]{0:T(128)S(1)} %concatenate.7.refs_0_, f32[2,128,128]{2,1,0:T(8,128)S(1)} %copy-done.5, f32[640,128]{1,0:T(8,128)S(1)} %copy-done.7, f32[5,2,3,128,128]{4,3,2,1,0:T(8,128)S(1)} %get-tuple-element.364.refs_3_.refs_4_, ...), custom_call_target="tpu_custom_call" | custom-call | flops 1 | bytes 1 | tf_op jit(solution)/shard_map/outer/pallas_call | solution.py:519
  99.6 3.7 %inner.10 = (f32[5,2,3,128,128]{4,3,2,1,0:T(8,128)S(1)}, f32[512,128]{1,0:T(8,128)S(1)}, f32[384,128]{1,0:T(8,128)S(1)}, f32[384,128]{1,0:T(8,128)S(1)}, f32[2,5,3,8,128]{4,3,2,1,0:T(8,128)S(1)}) custom-call(f32[16]{0:T(128)S(1)} %concatenate.7.refs_0_, f32[2,4,128,128]{3,2,1,0:T(8,128)S(1)} %copy-done.4, f32[5,2,4,128,128]{4,3,2,1,0:T(8,128)S(1)} %copy-done.1, ...), custom_call_target="tpu_custom_call" | custom-call | flops 1 | bytes 1 | tf_op jit(solution)/shard_map/inner/pallas_call | solution.py:519
  103.3 1.0 outer.21.refs_7_.refs_5_
  104.3 1.7 %collective-permute-start.106 = (f32[640,128]{1,0:T(8,128)S(1)}, f32[640,128]{1,0:T(8,128)S(1)}, u32[]{:S(2)}, u32[]{:S(2)}) collective-permute-start(f32[640,128]{1,0:T(8,128)S(1)} %outer.21.refs_7_.refs_5_), channel_id=1, source_target_pairs={{0,15},{1,2},{2,1},{3,4},{4,3},{5,6},{6,5},{7,8},{8,7},{9,10},{10,... | collective-permute-start | bytes 983048 | tf_op jit(solution)/shard_map/ppermute | solution.py:600
  106.0 1.3 %collective-permute-start.108 = (f32[512,128]{1,0:T(8,128)S(1)}, f32[512,128]{1,0:T(8,128)S(1)}, u32[]{:S(2)}, u32[]{:S(2)}) collective-permute-start(f32[512,128]{1,0:T(8,128)S(1)} %get-tuple-element.372.refs_10_), channel_id=1, source_target_pairs={{0,1},{1,0},{2,3},{3,2},{4,5},{5,4},{6,7},{7,6},{8,9},{9,8},{10,11... | collective-permute-start | bytes 786440 | tf_op jit(solution)/shard_map/ppermute | solution.py:605
  107.9 0.9 collective-permute-done.109.refs_9_
  109.1 3.9 %inner.11.refs_10_ = f32[5,2,4,128,128]{4,3,2,1,0:T(8,128)} custom-call(f32[16]{0:T(128)S(1)} %concatenate.7.refs_0_, f32[2,4,128,128]{3,2,1,0:T(8,128)S(1)} %copy-done.4, f32[5,2,4,128,128]{4,3,2,1,0:T(8,128)S(1)} %copy-done.1, f32[5,2,4,128,128]{4,3,2,1,0:T(8,128)S(1)} %copy-done, f32[5,2,3,128,128]{4,3,2,1,0:T(8,128)S(1)} %get-tuple-element.371.refs_4_.refs_3_, ...), custom_call_target="tpu_custom_call" | custom-call | flops 1 | bytes 1 | tf_op jit(solution)/shard_map/inner/pallas_call | solution.py:519
  113.0 1.8 %outer.22.refs_10_ = f32[5,2,4,128,128]{4,3,2,1,0:T(8,128)} custom-call(f32[16]{0:T(128)S(1)} %concatenate.7.refs_0_, f32[2,128,128]{2,1,0:T(8,128)S(1)} %copy-done.5, f32[640,128]{1,0:T(8,128)S(1)} %copy-done.7, f32[5,2,3,128,128]{4,3,2,1,0:T(8,128)S(1)} %get-tuple-element.371.refs_4_.refs_3_, ...), custom_call_target="tpu_custom_call", output_to_operand_aliasing={{}: (10, {})} | custom-call | flops 1 | bytes 1 | tf_op jit(solution)/shard_map/outer/pallas_call | solution.py:519
  114.8 1.8 %collective-permute-done.106.refs_8_ = f32[640,128]{1,0:T(8,128)S(1)} collective-permute-done((f32[640,128]{1,0:T(8,128)S(1)}, f32[640,128]{1,0:T(8,128)S(1)}, u32[]{:S(2)}, u32[]{:S(2)}) %collective-permute-start.106) | collective-permute-done | bytes 327712 | tf_op jit(solution)/shard_map/ppermute | solution.py:600
  116.5 1.8 %outer.23 = f32[5,2,4,128,128]{4,3,2,1,0:T(8,128)} custom-call(f32[16]{0:T(128)S(1)} %concatenate.7.refs_0_, f32[2,128,128]{2,1,0:T(8,128)S(1)} %copy-done.5, f32[640,128]{1,0:T(8,128)S(1)} %copy-done.6, f32[5,2,3,128,128]{4,3,2,1,0:T(8,128)S(1)} %get-tuple-element.371.refs_4_.refs_3_, ...), custom_call_target="tpu_custom_call", output_to_operand_aliasing={{}: (10, {})} | custom-call | flops 1 | bytes 1 | tf_op jit(solution)/shard_map/outer/pallas_call | solution.py:519
  (71 shorter events, 4.4 us)
Async XLA Ops:
  1.0 36.2 %copy-start.9 = (f32[2,4]{1,0:T(2,128)S(1)}, f32[2,4]{1,0:T(2,128)}, u32[]{:S(2)}) copy-start(f32[2,4]{1,0:T(2,128)} %param.24) | copy-start | bytes 100
  1.0 13.1 %collective-permute-start.80 = (f32[640,128]{1,0:T(8,128)S(1)}, f32[640,128]{1,0:T(8,128)S(1)}, u32[]{:S(2)}, u32[]{:S(2)}) collective-permute-start(f32[640,128]{1,0:T(8,128)S(1)} %outer_layer.1._), channel_id=1, source_target_pairs={{0,15},{1,2},{2,1},{3,4},{4,3},{5,6},{6,5},{7,8},{8,7},{9,10},{10,... | collective-permute-start | bytes 983048 | tf_op jit(solution)/shard_map/ppermute | solution.py:600
  9.3 3.8 %collective-permute-start.81 = (f32[288,128]{1,0:T(8,128)S(1)}, f32[288,128]{1,0:T(8,128)S(1)}, u32[]{:S(2)}, u32[]{:S(2)}) collective-permute-start(f32[288,128]{1,0:T(8,128)S(1)} %get-tuple-element.317.refs_1_), channel_id=1, source_target_pairs={{0,1},{1,2},{2,3},{3,4},{4,5},{5,6},{6,7},{7,8},{8,9},{9,10},{10,1... | collective-permute-start | bytes 442376 | tf_op jit(solution)/shard_map/ppermute | solution.py:594
  9.4 4.6 %collective-permute-start.82 = (f32[288,128]{1,0:T(8,128)S(1)}, f32[288,128]{1,0:T(8,128)S(1)}, u32[]{:S(2)}, u32[]{:S(2)}) collective-permute-start(f32[288,128]{1,0:T(8,128)S(1)} %get-tuple-element.318.refs_2_), channel_id=1, source_target_pairs={{0,15},{1,0},{2,1},{3,2},{4,3},{5,4},{6,5},{7,6},{8,7},{9,8},{10,9... | collective-permute-start | bytes 442376 | tf_op jit(solution)/shard_map/ppermute | solution.py:594
  14.0 30.7 %copy-start.3 = (f32[640,128]{1,0:T(8,128)S(1)}, f32[640,128]{1,0:T(8,128)}, u32[]{:S(2)}) copy-start(f32[640,128]{1,0:T(8,128)} %get-tuple-element.324.refs_4_.refs_6_) | copy-start | bytes 983044
  14.0 30.7 %copy-start.4 = (f32[2,4,128,128]{3,2,1,0:T(8,128)S(1)}, f32[2,4,128,128]{3,2,1,0:T(8,128)}, u32[]{:S(2)}) copy-start(f32[2,4,128,128]{3,2,1,0:T(8,128)} %refs_1_.11) | copy-start | bytes 1572868
  14.1 24.4 %copy-start.8 = (f32[640,128]{1,0:T(8,128)}, f32[640,128]{1,0:T(8,128)S(1)}, u32[]{:S(2)}) copy-start(f32[640,128]{1,0:T(8,128)S(1)} %collective-permute-done.80.refs_7_) | copy-start | bytes 983044
  14.2 14.3 %collective-permute-start.38 = (f32[320,128]{1,0:T(8,128)S(1)}, f32[320,128]{1,0:T(8,128)}, u32[]{:S(2)}, u32[]{:S(2)}) collective-permute-start(f32[320,128]{1,0:T(8,128)S(1)} %get-tuple-element.203), channel_id=1, source_target_pairs={{0,7},{1,8},{2,9},{3,10},{4,11},{5,12},{6,13},{7,14},{8,15},{9,0},... | collective-permute-start | bytes 491528 | tf_op jit(solution)/shard_map/cond/branch_7_fun/ppermute | solution.py:594
  17.1 13.7 %collective-permute-start.39 = (f32[320,128]{1,0:T(8,128)S(1)}, f32[320,128]{1,0:T(8,128)}, u32[]{:S(2)}, u32[]{:S(2)}) collective-permute-start(f32[320,128]{1,0:T(8,128)S(1)} %get-tuple-element.204), channel_id=1, source_target_pairs={{0,9},{1,10},{2,11},{3,12},{4,13},{5,14},{6,15},{7,0},{8,1},{9,2},... | collective-permute-start | bytes 491528 | tf_op jit(solution)/shard_map/cond/branch_7_fun/ppermute | solution.py:594
  17.8 10.7 %collective-permute-start.35 = (f32[256,128]{1,0:T(8,128)}, f32[256,128]{1,0:T(8,128)}, u32[]{:S(2)}, u32[]{:S(2)}) collective-permute-start(f32[256,128]{1,0:T(8,128)} %get-tuple-element.200), channel_id=1, source_target_pairs={{0,15},{1,2},{2,1},{3,4},{4,3},{5,6},{6,5},{7,8},{8,7},{9,10},{10,... | collective-permute-start | bytes 393224 | tf_op jit(solution)/shard_map/cond/branch_7_fun/ppermute | solution.py:600
  19.8 7.6 %collective-permute-start.36 = (f32[192,128]{1,0:T(8,128)}, f32[192,128]{1,0:T(8,128)}, u32[]{:S(2)}, u32[]{:S(2)}) collective-permute-start(f32[192,128]{1,0:T(8,128)} %get-tuple-element.201), channel_id=1, source_target_pairs={{0,15},{1,2},{2,1},{3,4},{4,3},{5,6},{6,5},{7,8},{8,7},{9,10},{10,... | collective-permute-start | bytes 294920 | tf_op jit(solution)/shard_map/cond/branch_7_fun/ppermute | solution.py:600
  19.8 8.6 %collective-permute-start.37 = (f32[192,128]{1,0:T(8,128)}, f32[192,128]{1,0:T(8,128)}, u32[]{:S(2)}, u32[]{:S(2)}) collective-permute-start(f32[192,128]{1,0:T(8,128)} %get-tuple-element.202), channel_id=1, source_target_pairs={{0,15},{1,2},{2,1},{3,4},{4,3},{5,6},{6,5},{7,8},{8,7},{9,10},{10,... | collective-permute-start | bytes 294920 | tf_op jit(solution)/shard_map/cond/branch_7_fun/ppermute | solution.py:600
  30.8 13.9 %collective-permute-start.83 = (f32[512,128]{1,0:T(8,128)}, f32[512,128]{1,0:T(8,128)S(1)}, u32[]{:S(2)}, u32[]{:S(2)}) collective-permute-start(f32[512,128]{1,0:T(8,128)} %get-tuple-element.326), channel_id=1, source_target_pairs={{0,1},{1,0},{2,3},{3,2},{4,5},{5,4},{6,7},{7,6},{8,9},{9,8},{10,11... | collective-permute-start | bytes 786440 | tf_op jit(solution)/shard_map/ppermute | solution.py:605
  36.7 8.0 %collective-permute-start.84 = (f32[384,128]{1,0:T(8,128)}, f32[384,128]{1,0:T(8,128)S(1)}, u32[]{:S(2)}, u32[]{:S(2)}) collective-permute-start(f32[384,128]{1,0:T(8,128)} %get-tuple-element.327), channel_id=1, source_target_pairs={{0,1},{1,0},{2,3},{3,2},{4,5},{5,4},{6,7},{7,6},{8,9},{9,8},{10,11... | collective-permute-start | bytes 589832 | tf_op jit(solution)/shard_map/ppermute | solution.py:605
  36.8 7.9 %collective-permute-start.85 = (f32[384,128]{1,0:T(8,128)}, f32[384,128]{1,0:T(8,128)S(1)}, u32[]{:S(2)}, u32[]{:S(2)}) collective-permute-start(f32[384,128]{1,0:T(8,128)} %get-tuple-element.328), channel_id=1, source_target_pairs={{0,1},{1,0},{2,3},{3,2},{4,5},{5,4},{6,7},{7,6},{8,9},{9,8},{10,11... | collective-permute-start | bytes 589832 | tf_op jit(solution)/shard_map/ppermute | solution.py:605
  37.4 7.3 %copy-start.2 = (f32[640,128]{1,0:T(8,128)S(1)}, f32[640,128]{1,0:T(8,128)}, u32[]{:S(2)}) copy-start(f32[640,128]{1,0:T(8,128)} %get-tuple-element.325.refs_5_.refs_6_.refs_7_) | copy-start | bytes 983044
  38.5 6.2 %copy-start = (f32[5,2,4,128,128]{4,3,2,1,0:T(8,128)S(1)}, f32[5,2,4,128,128]{4,3,2,1,0:T(8,128)}, u32[]{:S(2)}) copy-start(f32[5,2,4,128,128]{4,3,2,1,0:T(8,128)} %refs_3_.11) | copy-start | bytes 7864324
  38.6 6.2 %copy-start.1 = (f32[5,2,4,128,128]{4,3,2,1,0:T(8,128)S(1)}, f32[5,2,4,128,128]{4,3,2,1,0:T(8,128)}, u32[]{:S(2)}) copy-start(f32[5,2,4,128,128]{4,3,2,1,0:T(8,128)} %refs_2_.11) | copy-start | bytes 7864324
  40.9 11.6 %collective-permute-start.89 = (f32[680,128]{1,0:T(8,128)S(1)}, f32[680,128]{1,0:T(8,128)S(1)}, u32[]{:S(2)}, u32[]{:S(2)}) collective-permute-start(f32[680,128]{1,0:T(8,128)S(1)} %get-tuple-element.342.refs_11_.refs_4_.refs_6_), channel_id=1, source_target_pairs={{0,15},{1,2},{2,1},{3,4},{4,3},{5,6},{6,5},{7,8},{8,7},{9,10},{10,... | collective-permute-start | bytes 1044488 | tf_op jit(solution)/shard_map/ppermute | solution.py:600
  42.9 20.7 %collective-permute-start.90 = (f32[640,128]{1,0:T(8,128)S(1)}, f32[640,128]{1,0:T(8,128)S(1)}, u32[]{:S(2)}, u32[]{:S(2)}) collective-permute-start(f32[640,128]{1,0:T(8,128)S(1)} %outer.13.refs_17_.refs_5_.refs_7_), channel_id=1, source_target_pairs={{0,15},{1,2},{2,1},{3,4},{4,3},{5,6},{6,5},{7,8},{8,7},{9,10},{10,... | collective-permute-start | bytes 983048 | tf_op jit(solution)/shard_map/ppermute | solution.py:600
  44.8 7.7 %copy-start.5 = (f32[2,128,128]{2,1,0:T(8,128)S(1)}, f32[2,128,128]{2,1,0:T(8,128)}, u32[]{:S(2)}) copy-start(f32[2,128,128]{2,1,0:T(8,128)} %get-tuple-element.311.refs_1_) | copy-start | bytes 393220
  44.8 7.7 %copy-start.7 = (f32[640,128]{1,0:T(8,128)S(1)}, f32[640,128]{1,0:T(8,128)}, u32[]{:S(2)}) copy-start(f32[640,128]{1,0:T(8,128)} %get-tuple-element.337.refs_2_) | copy-start | bytes 983044
  48.2 11.8 %collective-permute-start.86 = (f32[512,128]{1,0:T(8,128)S(1)}, f32[512,128]{1,0:T(8,128)S(1)}, u32[]{:S(2)}, u32[]{:S(2)}) collective-permute-start(f32[512,128]{1,0:T(8,128)S(1)} %get-tuple-element.345), channel_id=1, source_target_pairs={{0,1},{1,0},{2,3},{3,2},{4,5},{5,4},{6,7},{7,6},{8,9},{9,8},{10,11... | collective-permute-start | bytes 786440 | tf_op jit(solution)/shard_map/ppermute | solution.py:605
  51.1 8.9 %collective-permute-start.88 = (f32[424,128]{1,0:T(8,128)S(1)}, f32[424,128]{1,0:T(8,128)S(1)}, u32[]{:S(2)}, u32[]{:S(2)}) collective-permute-start(f32[424,128]{1,0:T(8,128)S(1)} %get-tuple-element.347), channel_id=1, source_target_pairs={{0,1},{1,0},{2,3},{3,2},{4,5},{5,4},{6,7},{7,6},{8,9},{9,8},{10,11... | collective-permute-start | bytes 651272 | tf_op jit(solution)/shard_map/ppermute | solution.py:605
  51.1 8.8 %collective-permute-start.87 = (f32[384,128]{1,0:T(8,128)S(1)}, f32[384,128]{1,0:T(8,128)S(1)}, u32[]{:S(2)}, u32[]{:S(2)}) collective-permute-start(f32[384,128]{1,0:T(8,128)S(1)} %get-tuple-element.346), channel_id=1, source_target_pairs={{0,1},{1,0},{2,3},{3,2},{4,5},{5,4},{6,7},{7,6},{8,9},{9,8},{10,11... | collective-permute-start | bytes 589832 | tf_op jit(solution)/shard_map/ppermute | solution.py:605
  53.7 9.9 %copy-start.6 = (f32[640,128]{1,0:T(8,128)S(1)}, f32[640,128]{1,0:T(8,128)}, u32[]{:S(2)}) copy-start(f32[640,128]{1,0:T(8,128)} %get-tuple-element.312.refs_2_) | copy-start | bytes 983044
  53.7 13.5 %collective-permute-start.94 = (f32[670,128]{1,0:T(8,128)S(1)}, f32[670,128]{1,0:T(8,128)S(1)}, u32[]{:S(2)}, u32[]{:S(2)}) collective-permute-start(f32[670,128]{1,0:T(8,128)S(1)} %get-tuple-element.349.refs_16_.refs_4_.refs_6_), channel_id=1, source_target_pairs={{0,15},{1,2},{2,1},{3,4},{4,3},{5,6},{6,5},{7,8},{8,7},{9,10},{10,... | collective-permute-start | bytes 1029128 | tf_op jit(solution)/shard_map/ppermute | solution.py:600
  64.6 9.7 %collective-permute-start.95 = (f32[640,128]{1,0:T(8,128)S(1)}, f32[640,128]{1,0:T(8,128)S(1)}, u32[]{:S(2)}, u32[]{:S(2)}) collective-permute-start(f32[640,128]{1,0:T(8,128)S(1)} %outer.15.refs_5_.refs_7_), channel_id=1, source_target_pairs={{0,15},{1,2},{2,1},{3,4},{4,3},{5,6},{6,5},{7,8},{8,7},{9,10},{10,... | collective-permute-start | bytes 983048 | tf_op jit(solution)/shard_map/ppermute | solution.py:600
  66.7 3.9 %collective-permute-start.91 = (f32[512,128]{1,0:T(8,128)S(1)}, f32[512,128]{1,0:T(8,128)S(1)}, u32[]{:S(2)}, u32[]{:S(2)}) collective-permute-start(f32[512,128]{1,0:T(8,128)S(1)} %get-tuple-element.352.refs_9_), channel_id=1, source_target_pairs={{0,1},{1,0},{2,3},{3,2},{4,5},{5,4},{6,7},{7,6},{8,9},{9,8},{10,11... | collective-permute-start | bytes 786440 | tf_op jit(solution)/shard_map/ppermute | solution.py:605
  66.7 3.9 %collective-permute-start.93 = (f32[414,128]{1,0:T(8,128)S(1)}, f32[414,128]{1,0:T(8,128)S(1)}, u32[]{:S(2)}, u32[]{:S(2)}) collective-permute-start(f32[414,128]{1,0:T(8,128)S(1)} %get-tuple-element.354), channel_id=1, source_target_pairs={{0,1},{1,0},{2,3},{3,2},{4,5},{5,4},{6,7},{7,6},{8,9},{9,8},{10,11... | collective-permute-start | bytes 635912 | tf_op jit(solution)/shard_map/ppermute | solution.py:605
  67.2 3.4 %collective-permute-start.92 = (f32[384,128]{1,0:T(8,128)S(1)}, f32[384,128]{1,0:T(8,128)S(1)}, u32[]{:S(2)}, u32[]{:S(2)}) collective-permute-start(f32[384,128]{1,0:T(8,128)S(1)} %get-tuple-element.353), channel_id=1, source_target_pairs={{0,1},{1,0},{2,3},{3,2},{4,5},{5,4},{6,7},{7,6},{8,9},{9,8},{10,11... | collective-permute-start | bytes 589832 | tf_op jit(solution)/shard_map/ppermute | solution.py:605
  68.5 12.0 %collective-permute-start.99 = (f32[660,128]{1,0:T(8,128)S(1)}, f32[660,128]{1,0:T(8,128)S(1)}, u32[]{:S(2)}, u32[]{:S(2)}) collective-permute-start(f32[660,128]{1,0:T(8,128)S(1)} %get-tuple-element.356.refs_16_.refs_4_.refs_7_.refs_6_), channel_id=1, source_target_pairs={{0,15},{1,2},{2,1},{3,4},{4,3},{5,6},{6,5},{7,8},{8,7},{9,10},{10,... | collective-permute-start | bytes 1013768 | tf_op jit(solution)/shard_map/ppermute | solution.py:600
  75.5 16.7 %collective-permute-start.100 = (f32[640,128]{1,0:T(8,128)S(1)}, f32[640,128]{1,0:T(8,128)S(1)}, u32[]{:S(2)}, u32[]{:S(2)}) collective-permute-start(f32[640,128]{1,0:T(8,128)S(1)} %outer.17.refs_5_.refs_7_), channel_id=1, source_target_pairs={{0,15},{1,2},{2,1},{3,4},{4,3},{5,6},{6,5},{7,8},{8,7},{9,10},{10,... | collective-permute-start | bytes 983048 | tf_op jit(solution)/shard_map/ppermute | solution.py:600
  75.6 6.3 %collective-permute-start.96 = (f32[512,128]{1,0:T(8,128)S(1)}, f32[512,128]{1,0:T(8,128)S(1)}, u32[]{:S(2)}, u32[]{:S(2)}) collective-permute-start(f32[512,128]{1,0:T(8,128)S(1)} %get-tuple-element.359.refs_9_), channel_id=1, source_target_pairs={{0,1},{1,0},{2,3},{3,2},{4,5},{5,4},{6,7},{7,6},{8,9},{9,8},{10,11... | collective-permute-start | bytes 786440 | tf_op jit(solution)/shard_map/ppermute | solution.py:605
  78.4 3.5 %collective-permute-start.98 = (f32[404,128]{1,0:T(8,128)S(1)}, f32[404,128]{1,0:T(8,128)S(1)}, u32[]{:S(2)}, u32[]{:S(2)}) collective-permute-start(f32[404,128]{1,0:T(8,128)S(1)} %get-tuple-element.361), channel_id=1, source_target_pairs={{0,1},{1,0},{2,3},{3,2},{4,5},{5,4},{6,7},{7,6},{8,9},{9,8},{10,11... | collective-permute-start | bytes 620552 | tf_op jit(solution)/shard_map/ppermute | solution.py:605
  78.4 3.5 %collective-permute-start.97 = (f32[384,128]{1,0:T(8,128)S(1)}, f32[384,128]{1,0:T(8,128)S(1)}, u32[]{:S(2)}, u32[]{:S(2)}) collective-permute-start(f32[384,128]{1,0:T(8,128)S(1)} %get-tuple-element.360), channel_id=1, source_target_pairs={{0,1},{1,0},{2,3},{3,2},{4,5},{5,4},{6,7},{7,6},{8,9},{9,8},{10,11... | collective-permute-start | bytes 589832 | tf_op jit(solution)/shard_map/ppermute | solution.py:605
  81.8 16.5 %collective-permute-start.104 = (f32[650,128]{1,0:T(8,128)S(1)}, f32[650,128]{1,0:T(8,128)S(1)}, u32[]{:S(2)}, u32[]{:S(2)}) collective-permute-start(f32[650,128]{1,0:T(8,128)S(1)} %get-tuple-element.363.refs_17_.refs_4_.refs_6_), channel_id=1, source_target_pairs={{0,15},{1,2},{2,1},{3,4},{4,3},{5,6},{6,5},{7,8},{8,7},{9,10},{10,... | collective-permute-start | bytes 998408 | tf_op jit(solution)/shard_map/ppermute | solution.py:600
  93.2 10.0 %collective-permute-start.105 = (f32[640,128]{1,0:T(8,128)S(1)}, f32[640,128]{1,0:T(8,128)S(1)}, u32[]{:S(2)}, u32[]{:S(2)}) collective-permute-start(f32[640,128]{1,0:T(8,128)S(1)} %outer.19.refs_5_.refs_7_), channel_id=1, source_target_pairs={{0,15},{1,2},{2,1},{3,4},{4,3},{5,6},{6,5},{7,8},{8,7},{9,10},{10,... | collective-permute-start | bytes 983048 | tf_op jit(solution)/shard_map/ppermute | solution.py:600
  95.8 3.8 %collective-permute-start.101 = (f32[512,128]{1,0:T(8,128)S(1)}, f32[512,128]{1,0:T(8,128)S(1)}, u32[]{:S(2)}, u32[]{:S(2)}) collective-permute-start(f32[512,128]{1,0:T(8,128)S(1)} %get-tuple-element.366.refs_10_), channel_id=1, source_target_pairs={{0,1},{1,0},{2,3},{3,2},{4,5},{5,4},{6,7},{7,6},{8,9},{9,8},{10,11... | collective-permute-start | bytes 786440 | tf_op jit(solution)/shard_map/ppermute | solution.py:605
  95.8 3.8 %collective-permute-start.103 = (f32[394,128]{1,0:T(8,128)S(1)}, f32[394,128]{1,0:T(8,128)S(1)}, u32[]{:S(2)}, u32[]{:S(2)}) collective-permute-start(f32[394,128]{1,0:T(8,128)S(1)} %get-tuple-element.368), channel_id=1, source_target_pairs={{0,1},{1,0},{2,3},{3,2},{4,5},{5,4},{6,7},{7,6},{8,9},{9,8},{10,11... | collective-permute-start | bytes 605192 | tf_op jit(solution)/shard_map/ppermute | solution.py:605
  96.3 3.3 %collective-permute-start.102 = (f32[384,128]{1,0:T(8,128)S(1)}, f32[384,128]{1,0:T(8,128)S(1)}, u32[]{:S(2)}, u32[]{:S(2)}) collective-permute-start(f32[384,128]{1,0:T(8,128)S(1)} %get-tuple-element.367), channel_id=1, source_target_pairs={{0,1},{1,0},{2,3},{3,2},{4,5},{5,4},{6,7},{7,6},{8,9},{9,8},{10,11... | collective-permute-start | bytes 589832 | tf_op jit(solution)/shard_map/ppermute | solution.py:605
  99.4 13.5 %collective-permute-start.107 = (f32[640,128]{1,0:T(8,128)S(1)}, f32[640,128]{1,0:T(8,128)S(1)}, u32[]{:S(2)}, u32[]{:S(2)}) collective-permute-start(f32[640,128]{1,0:T(8,128)S(1)} %get-tuple-element.370.refs_17_.refs_6_.refs_4_), channel_id=1, source_target_pairs={{0,15},{1,2},{2,1},{3,4},{4,3},{5,6},{6,5},{7,8},{8,7},{9,10},{10,... | collective-permute-start | bytes 983048 | tf_op jit(solution)/shard_map/ppermute | solution.py:600
  104.3 12.2 %collective-permute-start.106 = (f32[640,128]{1,0:T(8,128)S(1)}, f32[640,128]{1,0:T(8,128)S(1)}, u32[]{:S(2)}, u32[]{:S(2)}) collective-permute-start(f32[640,128]{1,0:T(8,128)S(1)} %outer.21.refs_7_.refs_5_), channel_id=1, source_target_pairs={{0,15},{1,2},{2,1},{3,4},{4,3},{5,6},{6,5},{7,8},{8,7},{9,10},{10,... | collective-permute-start | bytes 983048 | tf_op jit(solution)/shard_map/ppermute | solution.py:600
  106.0 3.0 %collective-permute-start.108 = (f32[512,128]{1,0:T(8,128)S(1)}, f32[512,128]{1,0:T(8,128)S(1)}, u32[]{:S(2)}, u32[]{:S(2)}) collective-permute-start(f32[512,128]{1,0:T(8,128)S(1)} %get-tuple-element.372.refs_10_), channel_id=1, source_target_pairs={{0,1},{1,0},{2,3},{3,2},{4,5},{5,4},{6,7},{7,6},{8,9},{9,8},{10,11... | collective-permute-start | bytes 786440 | tf_op jit(solution)/shard_map/ppermute | solution.py:605
  107.4 1.4 %collective-permute-start.109 = (f32[384,128]{1,0:T(8,128)S(1)}, f32[384,128]{1,0:T(8,128)S(1)}, u32[]{:S(2)}, u32[]{:S(2)}) collective-permute-start(f32[384,128]{1,0:T(8,128)S(1)} %get-tuple-element.375), channel_id=1, source_target_pairs={{0,1},{1,0},{2,3},{3,2},{4,5},{5,4},{6,7},{7,6},{8,9},{9,8},{10,11... | collective-permute-start | bytes 589832 | tf_op jit(solution)/shard_map/ppermute | solution.py:605
  107.4 1.7 %collective-permute-start.110 = (f32[384,128]{1,0:T(8,128)S(1)}, f32[384,128]{1,0:T(8,128)S(1)}, u32[]{:S(2)}, u32[]{:S(2)}) collective-permute-start(f32[384,128]{1,0:T(8,128)S(1)} %get-tuple-element.376), channel_id=1, source_target_pairs={{0,1},{1,0},{2,3},{3,2},{4,5},{5,4},{6,7},{7,6},{8,9},{9,8},{10,11... | collective-permute-start | bytes 589832 | tf_op jit(solution)/shard_map/ppermute | solution.py:605

commit v3 on v2

--- a/solution.py
+++ b/solution.py
@@ -10,7 +10,7 @@
 PHYS_STEP = 1.0
 SECTION_WEIGHTS = (0.6, 0.6, 1.0)
 COMPS = 5
-CHUNK = 32
+CHUNK = 16
 STRIP = 8
 NEED = 6
 HALF = 32
@@ -18,15 +18,15 @@
 PIECES = (4, 3, 3)
 
 
-def scalars_of(mean_flow, sign):
+def scalars_of(mean_flow, sign, lanes):
     flow = jnp.concatenate([mean_flow, 1.0 / mean_flow[:, 2:3]], axis=1).reshape(-1)
-    return jnp.concatenate([flow, jnp.broadcast_to(sign, (6,))])
+    return jnp.broadcast_to(jnp.concatenate([flow, jnp.broadcast_to(sign, (6,))])[:, None], (16, lanes))
 
 
 def coefficients(scalars, row, weight):
     a = weight * PSEUDO_STEP
-    axial, swirl, density, sound, inverse = (scalars[row * 5 + i] for i in range(5))
-    sign = scalars[10]
+    axial, swirl, density, sound, inverse = (scalars[pl.ds(row * 5 + i, 1), :] for i in range(5))
+    sign = scalars[pl.ds(10, 1), :]
     half = 0.5 * a
     mass, lift = half * density, half * inverse
     return half * axial, half * swirl * sign, mass, mass * sound * sound, lift, lift * sign, sign, a
@@ -35,15 +35,17 @@
 def advance(k, f, up, down, low, high, behind, ahead, kept, eddy):
     e = k[7] * eddy
     damp = 6.0 * e + (1.5 / PHYS_STEP) * k[7]
-    da = [ahead[c] - behind[c] for c in range(COMPS)]
-    dt = [down[c] - up[c] for c in range(COMPS)]
-    dr = [high[c] - low[c] if c >= 3 else None for c in range(COMPS)]
-    div = da[1] + k[6] * dt[2] + dr[3]
-    push = (k[2] * div, k[4] * da[4], k[5] * dt[4], k[4] * dr[4], k[3] * div)
+    to_ahead, to_behind, to_down, to_up = e - k[0], e + k[0], e - k[1], e + k[1]
+    div = (ahead[1] - behind[1]) + k[6] * (down[2] - up[2]) + (high[3] - low[3])
+    push = (
+        k[2] * div, k[4] * (ahead[4] - behind[4]), k[5] * (down[4] - up[4]), k[4] * (high[4] - low[4]), k[3] * div,
+    )
     new = []
     for c in range(COMPS):
-        around = ((up[c] + down[c]) + (low[c] + high[c])) + (behind[c] + ahead[c])
-        new.append((kept[c] - damp * f[c]) + e * around - k[0] * da[c] - k[1] * dt[c] - push[c])
+        axial = to_ahead * ahead[c] + to_behind * behind[c]
+        theta = to_down * down[c] + to_up * up[c]
+        own = (kept[c] - push[c]) - damp * f[c]
+        new.append((own + e * (low[c] + high[c])) + (axial + theta))
     return new
 
 
@@ -506,8 +508,9 @@
 def run(kernel, scalars, arrays, outs, scratch, name, final=None, out_shape=None, pinned=0):
     scalars, arrays = list(scalars), list(arrays)
     if pinned is not None:
+        scalars = [x if x.dtype == jnp.int32 else in_vmem(x) for x in scalars]
         arrays = [in_hbm(x) if i < pinned else in_vmem(x) for i, x in enumerate(arrays)]
-    in_specs = [SMEM] * len(scalars) + [VMEM] * len(arrays)
+    in_specs = [SMEM if x.dtype == jnp.int32 else VMEM for x in scalars] + [VMEM] * len(arrays)
     if out_shape is not None:
         outs, out_specs = jax.ShapeDtypeStruct(out_shape, jnp.float32), ANY
     else:
@@ -629,7 +632,7 @@
     cells, radial, axial = shape[2:]
     count = lax.axis_size("theta")
     core = lax.axis_index("theta") % 2
-    scalars = scalars_of(mean_flow, jnp.where(core == 1, -1.0, 1.0).astype(jnp.float32))
+    scalars = scalars_of(mean_flow, jnp.where(core == 1, -1.0, 1.0).astype(jnp.float32), axial)
     shift_cells = offset[0] % (cells * count)
     depth, size = cells - 1, radial // PARTS
 

time: 118 us -> 117 us (level)
  waiting for transfers between devices: 24.2 us -> 44.7 us
  Pallas kernels: 46.5 us -> 35.6 us
  starting transfers between devices: 46 us -> 36.1 us
    ppermute x14, waiting for transfers between devices: 19.6 us -> 40.1 us  [across_chips(): return lax.ppermute(value, 'theta', pairs)]
    pallas_call x20, Pallas kernels: 39.9 us -> 28.9 us  [run(): pl.pallas_call(lambda *refs: kernel(list(refs)), out_shape=outs, in_specs...]
    ppermute x14, starting transfers between devices: 23.5 us -> 16.7 us  [across_chips(): return lax.ppermute(value, 'theta', pairs)]
    ppermute x18, starting transfers between devices: 15.9 us -> 12.8 us  [within_chip(): return lax.ppermute(value, 'theta', [(i, i ^ 1) for i in range(count)])]
  transfers between devices with their start and end apart: 36 -> 36, of which waited for: 12 -> 15; matrix products, arithmetic and copies ran while one was open for 0% -> 0% of each run, Pallas kernels for 37% -> 28%
where the time goes in v3:
time: 117 us; the launch traced here: 118 us
  waiting for transfers between devices  44.7 us (38%)
  starting transfers between devices  36.1 us (31%)
  Pallas kernels  35.6 us (30%)
  between operations  1.29 us (1%)
    ppermute x14, waiting for transfers between devices, across_chips(): return lax.ppermute(value, 'theta', pairs)  40.1 us
    pallas_call x20, Pallas kernels, run(): pl.pallas_call(lambda *refs: kernel(list(refs)), out_shape=outs, in_specs...  28.9 us
    ppermute x14, starting transfers between devices, across_chips(): return lax.ppermute(value, 'theta', pairs)  16.7 us
    ppermute x18, starting transfers between devices, within_chip(): return lax.ppermute(value, 'theta', [(i, i ^ 1) for i in range(count)])  12.8 us
    ppermute x4, starting transfers between devices, shifted(): lax.ppermute(value, 'theta', [(i, (i + steps) % count) for i in range(cou...  6.59 us
    pallas_call x1, Pallas kernels, call_gather(): pl.pallas_call(gather_kernel, out_shape=(strips,) * 2 + (part,) * (3 * PA...  5.66 us
    ppermute x4, waiting for transfers between devices, shifted(): lax.ppermute(value, 'theta', [(i, (i + steps) % count) for i in range(cou...  3.36 us
  transfers between devices with their start and end apart: 36, of which 15 were waited for; matrix products, arithmetic and copies ran while one was open for 0% of the time, Pallas kernels for 28%

profile of v3, /device:TPU:1, one launch (start us, length us, event | category | flops | bytes accessed | tf_op | source)
XLA Modules:
  0.0 118.1 jit_solution(8286452009554735014)
XLA Ops:
  0.0 1.0 outer_layer.1._
  1.0 2.7 %collective-permute-start.80 = (f32[640,128]{1,0:T(8,128)S(1)}, f32[640,128]{1,0:T(8,128)S(1)}, u32[]{:S(2)}, u32[]{:S(2)}) collective-permute-start(f32[640,128]{1,0:T(8,128)S(1)} %outer_layer.1._), channel_id=1, source_target_pairs={{0,15},{1,2},{2,1},{3,4},{4,3},{5,6},{6,5},{7,8},{8,7},{9,10},{10,... | collective-permute-start | bytes 983048 | tf_op jit(solution)/shard_map/ppermute | solution.py:603
  3.7 5.7 %gather_strips.1 = (f32[288,128]{1,0:T(8,128)S(1)}, f32[288,128]{1,0:T(8,128)S(1)}, f32[640,128]{1,0:T(8,128)}, f32[640,128]{1,0:T(8,128)}, f32[640,128]{1,0:T(8...) custom-call(f32[5,2,4,128,128]{4,3,2,1,0:T(8,128)} %refs_3_.11, ...), custom_call_target="tpu_custom_call" | custom-call | flops 1 | bytes 1 | tf_op jit(solution)/shard_map/gather_strips/pallas_call | solution.py:559
  9.4 2.9 %collective-permute-start.82 = (f32[288,128]{1,0:T(8,128)S(1)}, f32[288,128]{1,0:T(8,128)S(1)}, u32[]{:S(2)}, u32[]{:S(2)}) collective-permute-start(f32[288,128]{1,0:T(8,128)S(1)} %get-tuple-element.318.refs_2_), channel_id=1, source_target_pairs={{0,15},{1,0},{2,1},{3,2},{4,3},{5,4},{6,5},{7,6},{8,7},{9,8},{10,9... | collective-permute-start | bytes 442376 | tf_op jit(solution)/shard_map/ppermute | solution.py:597
  13.1 0.9 collective-permute-done.82.refs_4_
  14.1 16.7 %conditional.1 = (f32[256,128]{1,0:T(8,128)}, f32[192,128]{1,0:T(8,128)}, f32[192,128]{1,0:T(8,128)}, f32[320,128]{1,0:T(8,128)}, f32[320,128]{1,0:T(8,128)}) conditional(s32[]{:T(128)} %clamp.3, (f32[256,128]{1,0:T(8,128)}, f32[192,128]{1,0:T(8,128)}, f32[192,128]{1,0:T(8,128)}, f32[320,128]{1,0:T(8,128)S(1)}, ...), branch_computations={%region_0.1_spmd, %region_1.2_spmd, %region_2.3_spmd, %region_3.4_... | conditional | bytes 2621680 | solution.py:621
  14.2 2.9 %collective-permute-start.38 = (f32[320,128]{1,0:T(8,128)S(1)}, f32[320,128]{1,0:T(8,128)}, u32[]{:S(2)}, u32[]{:S(2)}) collective-permute-start(f32[320,128]{1,0:T(8,128)S(1)} %get-tuple-element.203), channel_id=1, source_target_pairs={{0,7},{1,8},{2,9},{3,10},{4,11},{5,12},{6,13},{7,14},{8,15},{9,0},... | collective-permute-start | bytes 491528 | tf_op jit(solution)/shard_map/cond/branch_7_fun/ppermute | solution.py:597
  17.1 0.7 collective-permute-start.39
  17.8 2.0 %collective-permute-start.35 = (f32[256,128]{1,0:T(8,128)}, f32[256,128]{1,0:T(8,128)}, u32[]{:S(2)}, u32[]{:S(2)}) collective-permute-start(f32[256,128]{1,0:T(8,128)} %get-tuple-element.200), channel_id=1, source_target_pairs={{0,15},{1,2},{2,1},{3,4},{4,3},{5,6},{6,5},{7,8},{8,7},{9,10},{10,... | collective-permute-start | bytes 393224 | tf_op jit(solution)/shard_map/cond/branch_7_fun/ppermute | solution.py:603
  19.8 1.7 %collective-permute-start.37 = (f32[192,128]{1,0:T(8,128)}, f32[192,128]{1,0:T(8,128)}, u32[]{:S(2)}, u32[]{:S(2)}) collective-permute-start(f32[192,128]{1,0:T(8,128)} %get-tuple-element.202), channel_id=1, source_target_pairs={{0,15},{1,2},{2,1},{3,4},{4,3},{5,6},{6,5},{7,8},{8,7},{9,10},{10,... | collective-permute-start | bytes 294920 | tf_op jit(solution)/shard_map/cond/branch_7_fun/ppermute | solution.py:603
  21.5 5.8 %collective-permute-done.36 = f32[192,128]{1,0:T(8,128)} collective-permute-done((f32[192,128]{1,0:T(8,128)}, f32[192,128]{1,0:T(8,128)}, u32[]{:S(2)}, u32[]{:S(2)}) %collective-permute-start.36) | collective-permute-done | bytes 98336 | tf_op jit(solution)/shard_map/cond/branch_7_fun/ppermute | solution.py:603
  27.4 1.1 collective-permute-done.37
  28.4 2.4 %collective-permute-done.39 = f32[320,128]{1,0:T(8,128)} collective-permute-done((f32[320,128]{1,0:T(8,128)S(1)}, f32[320,128]{1,0:T(8,128)}, u32[]{:S(2)}, u32[]{:S(2)}) %collective-permute-start.39) | collective-permute-done | bytes 163872 | tf_op jit(solution)/shard_map/cond/branch_7_fun/ppermute | solution.py:597
  30.8 5.9 %collective-permute-start.83 = (f32[512,128]{1,0:T(8,128)}, f32[512,128]{1,0:T(8,128)S(1)}, u32[]{:S(2)}, u32[]{:S(2)}) collective-permute-start(f32[512,128]{1,0:T(8,128)} %get-tuple-element.326), channel_id=1, source_target_pairs={{0,1},{1,0},{2,3},{3,2},{4,5},{5,4},{6,7},{7,6},{8,9},{9,8},{10,11... | collective-permute-start | bytes 786440 | tf_op jit(solution)/shard_map/ppermute | solution.py:608
  37.4 1.1 scatter_strips.1
  38.6 2.3 %outer.12 = (f32[680,128]{1,0:T(8,128)S(1)}, f32[2,5,8,128]{3,2,1,0:T(8,128)S(1)}) custom-call(f32[16,128]{1,0:T(8,128)S(1)} %broadcast_in_dim.2.refs_0_, f32[2,128,128]{2,1,0:T(8,128)} %get-tuple-element.311.refs_1_, f32[640,128]{1,0:T(8,128)} %get-tuple-element.337.refs_2_, f32[640,128]{1,0:T(8,128)} %get-tuple-element.338.refs_3_, ...), custom_call_target="tpu_custom_call" | custom-call | flops 1 | bytes 1 | tf_op jit(solution)/shard_map/outer/pallas_call | solution.py:522
  41.0 1.9 %outer.13.refs_17_.refs_5_.refs_7_ = f32[640,128]{1,0:T(8,128)S(1)} custom-call(f32[16,128]{1,0:T(8,128)S(1)} %broadcast_in_dim.2.refs_0_, f32[2,128,128]{2,1,0:T(8,128)} %get-tuple-element.311.refs_1_, f32[640,128]{1,0:T(8,128)} %get-tuple-element.312.refs_2_, f32[640,128]{1,0:T(8,128)} %get-tuple-element.333.refs_3_, ...), custom_call_target="tpu_custom_call" | custom-call | flops 1 | bytes 1 | tf_op jit(solution)/shard_map/outer/pallas_call | solution.py:522
  42.9 1.8 %collective-permute-start.90 = (f32[640,128]{1,0:T(8,128)S(1)}, f32[640,128]{1,0:T(8,128)S(1)}, u32[]{:S(2)}, u32[]{:S(2)}) collective-permute-start(f32[640,128]{1,0:T(8,128)S(1)} %outer.13.refs_17_.refs_5_.refs_7_), channel_id=1, source_target_pairs={{0,15},{1,2},{2,1},{3,4},{4,3},{5,6},{6,5},{7,8},{8,7},{9,10},{10,... | collective-permute-start | bytes 983048 | tf_op jit(solution)/shard_map/ppermute | solution.py:603
  44.8 2.5 %inner.6 = (f32[5,2,3,128,128]{4,3,2,1,0:T(8,128)S(1)}, f32[512,128]{1,0:T(8,128)S(1)}, f32[384,128]{1,0:T(8,128)S(1)}, f32[424,128]{1,0:T(8,128)S(1)}, f32[2,5,3,8,128]{4,3,2,1,0:T(8,128)S(1)}) custom-call(f32[16,128]{1,0:T(8,128)S(1)} %broadcast_in_dim.2.refs_0_, f32[2,4,128,128]{3,2,1,0:T(8,128)S(1)} %copy-done.4, f32[5,2,4,128,128]{4,3,2,1,0:T(8,128)S(1)} %copy-done.1, ...), custom_call_target="tpu_custom_call" | custom-call | flops 1 | bytes 1 | tf_op jit(solution)/shard_map/inner/pallas_call | solution.py:522
  47.3 2.8 %collective-permute-start.86 = (f32[512,128]{1,0:T(8,128)S(1)}, f32[512,128]{1,0:T(8,128)S(1)}, u32[]{:S(2)}, u32[]{:S(2)}) collective-permute-start(f32[512,128]{1,0:T(8,128)S(1)} %get-tuple-element.345), channel_id=1, source_target_pairs={{0,1},{1,0},{2,3},{3,2},{4,5},{5,4},{6,7},{7,6},{8,9},{9,8},{10,11... | collective-permute-start | bytes 786440 | tf_op jit(solution)/shard_map/ppermute | solution.py:608
  50.7 5.5 %collective-permute-done.89.refs_7_ = f32[680,128]{1,0:T(8,128)S(1)} collective-permute-done((f32[680,128]{1,0:T(8,128)S(1)}, f32[680,128]{1,0:T(8,128)S(1)}, u32[]{:S(2)}, u32[]{:S(2)}) %collective-permute-start.89) | collective-permute-done | bytes 348192 | tf_op jit(solution)/shard_map/ppermute | solution.py:603
  56.2 0.7 outer.14
  56.9 6.0 %collective-permute-start.94 = (f32[670,128]{1,0:T(8,128)S(1)}, f32[670,128]{1,0:T(8,128)S(1)}, u32[]{:S(2)}, u32[]{:S(2)}) collective-permute-start(f32[670,128]{1,0:T(8,128)S(1)} %get-tuple-element.349.refs_16_.refs_4_.refs_6_), channel_id=1, source_target_pairs={{0,15},{1,2},{2,1},{3,4},{4,3},{5,6},{6,5},{7,8},{8,7},{9,10},{10,... | collective-permute-start | bytes 1029128 | tf_op jit(solution)/shard_map/ppermute | solution.py:603
  63.0 2.5 %inner.7 = (f32[5,2,3,128,128]{4,3,2,1,0:T(8,128)S(1)}, f32[512,128]{1,0:T(8,128)S(1)}, f32[384,128]{1,0:T(8,128)S(1)}, f32[414,128]{1,0:T(8,128)S(1)}, f32[2,5,3,8,128]{4,3,2,1,0:T(8,128)S(1)}) custom-call(f32[16,128]{1,0:T(8,128)S(1)} %broadcast_in_dim.2.refs_0_, f32[2,4,128,128]{3,2,1,0:T(8,128)S(1)} %copy-done.4, f32[5,2,4,128,128]{4,3,2,1,0:T(8,128)S(1)} %copy-done.1, ...), custom_call_target="tpu_custom_call" | custom-call | flops 1 | bytes 1 | tf_op jit(solution)/shard_map/inner/pallas_call | solution.py:522
  66.2 0.5 collective-permute-start.93
  66.7 3.6 %collective-permute-done.94.refs_7_ = f32[670,128]{1,0:T(8,128)S(1)} collective-permute-done((f32[670,128]{1,0:T(8,128)S(1)}, f32[670,128]{1,0:T(8,128)S(1)}, u32[]{:S(2)}, u32[]{:S(2)}) %collective-permute-start.94) | collective-permute-done | bytes 343072 | tf_op jit(solution)/shard_map/ppermute | solution.py:603
  70.3 0.7 outer.16
  71.1 2.6 %inner.8 = (f32[5,2,3,128,128]{4,3,2,1,0:T(8,128)S(1)}, f32[512,128]{1,0:T(8,128)S(1)}, f32[384,128]{1,0:T(8,128)S(1)}, f32[404,128]{1,0:T(8,128)S(1)}, f32[2,5,3,8,128]{4,3,2,1,0:T(8,128)S(1)}) custom-call(f32[16,128]{1,0:T(8,128)S(1)} %broadcast_in_dim.2.refs_0_, f32[2,4,128,128]{3,2,1,0:T(8,128)S(1)} %copy-done.4, f32[5,2,4,128,128]{4,3,2,1,0:T(8,128)S(1)} %copy-done.1, ...), custom_call_target="tpu_custom_call" | custom-call | flops 1 | bytes 1 | tf_op jit(solution)/shard_map/inner/pallas_call | solution.py:522
  73.7 3.8 %collective-permute-done.95.refs_7_ = f32[640,128]{1,0:T(8,128)S(1)} collective-permute-done((f32[640,128]{1,0:T(8,128)S(1)}, f32[640,128]{1,0:T(8,128)S(1)}, u32[]{:S(2)}, u32[]{:S(2)}) %collective-permute-start.95) | collective-permute-done | bytes 327712 | tf_op jit(solution)/shard_map/ppermute | solution.py:603
  78.1 0.5 collective-permute-start.98
  78.7 5.9 %collective-permute-done.99.refs_8_ = f32[660,128]{1,0:T(8,128)S(1)} collective-permute-done((f32[660,128]{1,0:T(8,128)S(1)}, f32[660,128]{1,0:T(8,128)S(1)}, u32[]{:S(2)}, u32[]{:S(2)}) %collective-permute-start.99) | collective-permute-done | bytes 337952 | tf_op jit(solution)/shard_map/ppermute | solution.py:603
  84.6 0.7 outer.18
  85.4 2.7 %inner.9 = (f32[5,2,3,128,128]{4,3,2,1,0:T(8,128)S(1)}, f32[512,128]{1,0:T(8,128)S(1)}, f32[384,128]{1,0:T(8,128)S(1)}, f32[394,128]{1,0:T(8,128)S(1)}, f32[2,5,3,8,128]{4,3,2,1,0:T(8,128)S(1)}) custom-call(f32[16,128]{1,0:T(8,128)S(1)} %broadcast_in_dim.2.refs_0_, f32[2,4,128,128]{3,2,1,0:T(8,128)S(1)} %copy-done.4, f32[5,2,4,128,128]{4,3,2,1,0:T(8,128)S(1)} %copy-done.1, ...), custom_call_target="tpu_custom_call" | custom-call | flops 1 | bytes 1 | tf_op jit(solution)/shard_map/inner/pallas_call | solution.py:522
  88.2 7.1 %collective-permute-done.100.refs_8_ = f32[640,128]{1,0:T(8,128)S(1)} collective-permute-done((f32[640,128]{1,0:T(8,128)S(1)}, f32[640,128]{1,0:T(8,128)S(1)}, u32[]{:S(2)}, u32[]{:S(2)}) %collective-permute-start.100) | collective-permute-done | bytes 327712 | tf_op jit(solution)/shard_map/ppermute | solution.py:603
  95.9 0.5 collective-permute-start.103
  96.5 2.4 %collective-permute-done.104.refs_8_ = f32[650,128]{1,0:T(8,128)S(1)} collective-permute-done((f32[650,128]{1,0:T(8,128)S(1)}, f32[650,128]{1,0:T(8,128)S(1)}, u32[]{:S(2)}, u32[]{:S(2)}) %collective-permute-start.104) | collective-permute-done | bytes 332832 | tf_op jit(solution)/shard_map/ppermute | solution.py:603
  98.8 0.7 outer.20
  99.7 2.7 %inner.10 = (f32[5,2,3,128,128]{4,3,2,1,0:T(8,128)S(1)}, f32[512,128]{1,0:T(8,128)S(1)}, f32[384,128]{1,0:T(8,128)S(1)}, f32[384,128]{1,0:T(8,128)S(1)}, f32[2,5,3,8,128]{4,3,2,1,0:T(8,128)S(1)}) custom-call(f32[16,128]{1,0:T(8,128)S(1)} %broadcast_in_dim.2.refs_0_, f32[2,4,128,128]{3,2,1,0:T(8,128)S(1)} %copy-done.4, f32[5,2,4,128,128]{4,3,2,1,0:T(8,128)S(1)} %copy-done.1, ...), custom_call_target="tpu_custom_call" | custom-call | flops 1 | bytes 1 | tf_op jit(solution)/shard_map/inner/pallas_call | solution.py:522
  102.4 0.5 outer.21.refs_7_.refs_5_
  102.9 1.8 %collective-permute-start.106 = (f32[640,128]{1,0:T(8,128)S(1)}, f32[640,128]{1,0:T(8,128)S(1)}, u32[]{:S(2)}, u32[]{:S(2)}) collective-permute-start(f32[640,128]{1,0:T(8,128)S(1)} %outer.21.refs_7_.refs_5_), channel_id=1, source_target_pairs={{0,15},{1,2},{2,1},{3,4},{4,3},{5,6},{6,5},{7,8},{8,7},{9,10},{10,... | collective-permute-start | bytes 983048 | tf_op jit(solution)/shard_map/ppermute | solution.py:603
  104.7 0.8 collective-permute-start.108
  105.4 0.5 collective-permute-start.110
  106.0 0.9 collective-permute-done.109.refs_9_
  107.2 3.3 %inner.11.refs_10_ = f32[5,2,4,128,128]{4,3,2,1,0:T(8,128)} custom-call(f32[16,128]{1,0:T(8,128)S(1)} %broadcast_in_dim.2.refs_0_, f32[2,4,128,128]{3,2,1,0:T(8,128)S(1)} %copy-done.4, f32[5,2,4,128,128]{4,3,2,1,0:T(8,128)S(1)} %copy-done.1, f32[5,2,4,128,128]{4,3,2,1,0:T(8,128)S(1)} %copy-done, ...), custom_call_target="tpu_custom_call" | custom-call | flops 1 | bytes 1 | tf_op jit(solution)/shard_map/inner/pallas_call | solution.py:522
  110.4 2.7 %collective-permute-done.107.refs_8_ = f32[640,128]{1,0:T(8,128)S(1)} collective-permute-done((f32[640,128]{1,0:T(8,128)S(1)}, f32[640,128]{1,0:T(8,128)S(1)}, u32[]{:S(2)}, u32[]{:S(2)}) %collective-permute-start.107) | collective-permute-done | bytes 327712 | tf_op jit(solution)/shard_map/ppermute | solution.py:603
  113.1 1.2 %outer.22.refs_10_ = f32[5,2,4,128,128]{4,3,2,1,0:T(8,128)} custom-call(f32[16,128]{1,0:T(8,128)S(1)} %broadcast_in_dim.2.refs_0_, f32[2,128,128]{2,1,0:T(8,128)S(1)} %copy-done.5, f32[640,128]{1,0:T(8,128)S(1)} %copy-done.7, f32[5,2,3,128,128]{4,3,2,1,0:T(8,128)S(1)} %get-tuple-element.371.refs_4_.refs_3_, ...), custom_call_target="tpu_custom_call", output_to_operand_aliasing={{}: (10, {})} | custom-call | flops 1 | bytes 1 | tf_op jit(solution)/shard_map/outer/pallas_call | solution.py:522
  114.3 2.3 %collective-permute-done.106.refs_8_ = f32[640,128]{1,0:T(8,128)S(1)} collective-permute-done((f32[640,128]{1,0:T(8,128)S(1)}, f32[640,128]{1,0:T(8,128)S(1)}, u32[]{:S(2)}, u32[]{:S(2)}) %collective-permute-start.106) | collective-permute-done | bytes 327712 | tf_op jit(solution)/shard_map/ppermute | solution.py:603
  116.6 1.2 %outer.23 = f32[5,2,4,128,128]{4,3,2,1,0:T(8,128)} custom-call(f32[16,128]{1,0:T(8,128)S(1)} %broadcast_in_dim.2.refs_0_, f32[2,128,128]{2,1,0:T(8,128)S(1)} %copy-done.5, f32[640,128]{1,0:T(8,128)S(1)} %copy-done.6, f32[5,2,3,128,128]{4,3,2,1,0:T(8,128)S(1)} %get-tuple-element.371.refs_4_.refs_3_, ...), custom_call_target="tpu_custom_call", output_to_operand_aliasing={{}: (10, {})} | custom-call | flops 1 | bytes 1 | tf_op jit(solution)/shard_map/outer/pallas_call | solution.py:522
  (72 shorter events, 4.4 us)
Async XLA Ops:
  1.0 36.2 %copy-start.9 = (f32[2,4]{1,0:T(2,128)S(1)}, f32[2,4]{1,0:T(2,128)}, u32[]{:S(2)}) copy-start(f32[2,4]{1,0:T(2,128)} %param.24) | copy-start | bytes 100
  1.0 13.1 %collective-permute-start.80 = (f32[640,128]{1,0:T(8,128)S(1)}, f32[640,128]{1,0:T(8,128)S(1)}, u32[]{:S(2)}, u32[]{:S(2)}) collective-permute-start(f32[640,128]{1,0:T(8,128)S(1)} %outer_layer.1._), channel_id=1, source_target_pairs={{0,15},{1,2},{2,1},{3,4},{4,3},{5,6},{6,5},{7,8},{8,7},{9,10},{10,... | collective-permute-start | bytes 983048 | tf_op jit(solution)/shard_map/ppermute | solution.py:603
  9.3 3.8 %collective-permute-start.81 = (f32[288,128]{1,0:T(8,128)S(1)}, f32[288,128]{1,0:T(8,128)S(1)}, u32[]{:S(2)}, u32[]{:S(2)}) collective-permute-start(f32[288,128]{1,0:T(8,128)S(1)} %get-tuple-element.317.refs_1_), channel_id=1, source_target_pairs={{0,1},{1,2},{2,3},{3,4},{4,5},{5,6},{6,7},{7,8},{8,9},{9,10},{10,1... | collective-permute-start | bytes 442376 | tf_op jit(solution)/shard_map/ppermute | solution.py:597
  9.4 4.6 %collective-permute-start.82 = (f32[288,128]{1,0:T(8,128)S(1)}, f32[288,128]{1,0:T(8,128)S(1)}, u32[]{:S(2)}, u32[]{:S(2)}) collective-permute-start(f32[288,128]{1,0:T(8,128)S(1)} %get-tuple-element.318.refs_2_), channel_id=1, source_target_pairs={{0,15},{1,0},{2,1},{3,2},{4,3},{5,4},{6,5},{7,6},{8,7},{9,8},{10,9... | collective-permute-start | bytes 442376 | tf_op jit(solution)/shard_map/ppermute | solution.py:597
  14.0 30.7 %copy-start.3 = (f32[640,128]{1,0:T(8,128)S(1)}, f32[640,128]{1,0:T(8,128)}, u32[]{:S(2)}) copy-start(f32[640,128]{1,0:T(8,128)} %get-tuple-element.324.refs_4_.refs_6_) | copy-start | bytes 983044
  14.0 30.7 %copy-start.4 = (f32[2,4,128,128]{3,2,1,0:T(8,128)S(1)}, f32[2,4,128,128]{3,2,1,0:T(8,128)}, u32[]{:S(2)}) copy-start(f32[2,4,128,128]{3,2,1,0:T(8,128)} %refs_1_.11) | copy-start | bytes 1572868
  14.1 24.5 %copy-start.8 = (f32[640,128]{1,0:T(8,128)}, f32[640,128]{1,0:T(8,128)S(1)}, u32[]{:S(2)}) copy-start(f32[640,128]{1,0:T(8,128)S(1)} %collective-permute-done.80.refs_7_) | copy-start | bytes 983044
  14.2 14.3 %collective-permute-start.38 = (f32[320,128]{1,0:T(8,128)S(1)}, f32[320,128]{1,0:T(8,128)}, u32[]{:S(2)}, u32[]{:S(2)}) collective-permute-start(f32[320,128]{1,0:T(8,128)S(1)} %get-tuple-element.203), channel_id=1, source_target_pairs={{0,7},{1,8},{2,9},{3,10},{4,11},{5,12},{6,13},{7,14},{8,15},{9,0},... | collective-permute-start | bytes 491528 | tf_op jit(solution)/shard_map/cond/branch_7_fun/ppermute | solution.py:597
  17.1 13.7 %collective-permute-start.39 = (f32[320,128]{1,0:T(8,128)S(1)}, f32[320,128]{1,0:T(8,128)}, u32[]{:S(2)}, u32[]{:S(2)}) collective-permute-start(f32[320,128]{1,0:T(8,128)S(1)} %get-tuple-element.204), channel_id=1, source_target_pairs={{0,9},{1,10},{2,11},{3,12},{4,13},{5,14},{6,15},{7,0},{8,1},{9,2},... | collective-permute-start | bytes 491528 | tf_op jit(solution)/shard_map/cond/branch_7_fun/ppermute | solution.py:597
  17.8 10.7 %collective-permute-start.35 = (f32[256,128]{1,0:T(8,128)}, f32[256,128]{1,0:T(8,128)}, u32[]{:S(2)}, u32[]{:S(2)}) collective-permute-start(f32[256,128]{1,0:T(8,128)} %get-tuple-element.200), channel_id=1, source_target_pairs={{0,15},{1,2},{2,1},{3,4},{4,3},{5,6},{6,5},{7,8},{8,7},{9,10},{10,... | collective-permute-start | bytes 393224 | tf_op jit(solution)/shard_map/cond/branch_7_fun/ppermute | solution.py:603
  19.8 7.6 %collective-permute-start.36 = (f32[192,128]{1,0:T(8,128)}, f32[192,128]{1,0:T(8,128)}, u32[]{:S(2)}, u32[]{:S(2)}) collective-permute-start(f32[192,128]{1,0:T(8,128)} %get-tuple-element.201), channel_id=1, source_target_pairs={{0,15},{1,2},{2,1},{3,4},{4,3},{5,6},{6,5},{7,8},{8,7},{9,10},{10,... | collective-permute-start | bytes 294920 | tf_op jit(solution)/shard_map/cond/branch_7_fun/ppermute | solution.py:603
  19.8 8.6 %collective-permute-start.37 = (f32[192,128]{1,0:T(8,128)}, f32[192,128]{1,0:T(8,128)}, u32[]{:S(2)}, u32[]{:S(2)}) collective-permute-start(f32[192,128]{1,0:T(8,128)} %get-tuple-element.202), channel_id=1, source_target_pairs={{0,15},{1,2},{2,1},{3,4},{4,3},{5,6},{6,5},{7,8},{8,7},{9,10},{10,... | collective-permute-start | bytes 294920 | tf_op jit(solution)/shard_map/cond/branch_7_fun/ppermute | solution.py:603
  30.8 13.9 %collective-permute-start.83 = (f32[512,128]{1,0:T(8,128)}, f32[512,128]{1,0:T(8,128)S(1)}, u32[]{:S(2)}, u32[]{:S(2)}) collective-permute-start(f32[512,128]{1,0:T(8,128)} %get-tuple-element.326), channel_id=1, source_target_pairs={{0,1},{1,0},{2,3},{3,2},{4,5},{5,4},{6,7},{7,6},{8,9},{9,8},{10,11... | collective-permute-start | bytes 786440 | tf_op jit(solution)/shard_map/ppermute | solution.py:608
  36.7 8.0 %collective-permute-start.84 = (f32[384,128]{1,0:T(8,128)}, f32[384,128]{1,0:T(8,128)S(1)}, u32[]{:S(2)}, u32[]{:S(2)}) collective-permute-start(f32[384,128]{1,0:T(8,128)} %get-tuple-element.327), channel_id=1, source_target_pairs={{0,1},{1,0},{2,3},{3,2},{4,5},{5,4},{6,7},{7,6},{8,9},{9,8},{10,11... | collective-permute-start | bytes 589832 | tf_op jit(solution)/shard_map/ppermute | solution.py:608
  36.8 8.0 %collective-permute-start.85 = (f32[384,128]{1,0:T(8,128)}, f32[384,128]{1,0:T(8,128)S(1)}, u32[]{:S(2)}, u32[]{:S(2)}) collective-permute-start(f32[384,128]{1,0:T(8,128)} %get-tuple-element.328), channel_id=1, source_target_pairs={{0,1},{1,0},{2,3},{3,2},{4,5},{5,4},{6,7},{7,6},{8,9},{9,8},{10,11... | collective-permute-start | bytes 589832 | tf_op jit(solution)/shard_map/ppermute | solution.py:608
  37.4 7.3 %copy-start.2 = (f32[640,128]{1,0:T(8,128)S(1)}, f32[640,128]{1,0:T(8,128)}, u32[]{:S(2)}) copy-start(f32[640,128]{1,0:T(8,128)} %get-tuple-element.325.refs_5_.refs_6_.refs_7_) | copy-start | bytes 983044
  38.6 6.1 %copy-start = (f32[5,2,4,128,128]{4,3,2,1,0:T(8,128)S(1)}, f32[5,2,4,128,128]{4,3,2,1,0:T(8,128)}, u32[]{:S(2)}) copy-start(f32[5,2,4,128,128]{4,3,2,1,0:T(8,128)} %refs_3_.11) | copy-start | bytes 7864324
  38.6 6.2 %copy-start.1 = (f32[5,2,4,128,128]{4,3,2,1,0:T(8,128)S(1)}, f32[5,2,4,128,128]{4,3,2,1,0:T(8,128)}, u32[]{:S(2)}) copy-start(f32[5,2,4,128,128]{4,3,2,1,0:T(8,128)} %refs_2_.11) | copy-start | bytes 7864324
  40.9 15.2 %collective-permute-start.89 = (f32[680,128]{1,0:T(8,128)S(1)}, f32[680,128]{1,0:T(8,128)S(1)}, u32[]{:S(2)}, u32[]{:S(2)}) collective-permute-start(f32[680,128]{1,0:T(8,128)S(1)} %get-tuple-element.342.refs_11_.refs_4_.refs_6_), channel_id=1, source_target_pairs={{0,15},{1,2},{2,1},{3,4},{4,3},{5,6},{6,5},{7,8},{8,7},{9,10},{10,... | collective-permute-start | bytes 1044488 | tf_op jit(solution)/shard_map/ppermute | solution.py:603
  42.9 22.6 %collective-permute-start.90 = (f32[640,128]{1,0:T(8,128)S(1)}, f32[640,128]{1,0:T(8,128)S(1)}, u32[]{:S(2)}, u32[]{:S(2)}) collective-permute-start(f32[640,128]{1,0:T(8,128)S(1)} %outer.13.refs_17_.refs_5_.refs_7_), channel_id=1, source_target_pairs={{0,15},{1,2},{2,1},{3,4},{4,3},{5,6},{6,5},{7,8},{8,7},{9,10},{10,... | collective-permute-start | bytes 983048 | tf_op jit(solution)/shard_map/ppermute | solution.py:603
  44.8 11.4 %copy-start.5 = (f32[2,128,128]{2,1,0:T(8,128)S(1)}, f32[2,128,128]{2,1,0:T(8,128)}, u32[]{:S(2)}) copy-start(f32[2,128,128]{2,1,0:T(8,128)} %get-tuple-element.311.refs_1_) | copy-start | bytes 393220
  44.8 11.4 %copy-start.7 = (f32[640,128]{1,0:T(8,128)S(1)}, f32[640,128]{1,0:T(8,128)}, u32[]{:S(2)}) copy-start(f32[640,128]{1,0:T(8,128)} %get-tuple-element.337.refs_2_) | copy-start | bytes 983044
  47.3 15.6 %collective-permute-start.86 = (f32[512,128]{1,0:T(8,128)S(1)}, f32[512,128]{1,0:T(8,128)S(1)}, u32[]{:S(2)}, u32[]{:S(2)}) collective-permute-start(f32[512,128]{1,0:T(8,128)S(1)} %get-tuple-element.345), channel_id=1, source_target_pairs={{0,1},{1,0},{2,3},{3,2},{4,5},{5,4},{6,7},{7,6},{8,9},{9,8},{10,11... | collective-permute-start | bytes 786440 | tf_op jit(solution)/shard_map/ppermute | solution.py:608
  50.2 12.8 %collective-permute-start.88 = (f32[424,128]{1,0:T(8,128)S(1)}, f32[424,128]{1,0:T(8,128)S(1)}, u32[]{:S(2)}, u32[]{:S(2)}) collective-permute-start(f32[424,128]{1,0:T(8,128)S(1)} %get-tuple-element.347), channel_id=1, source_target_pairs={{0,1},{1,0},{2,3},{3,2},{4,5},{5,4},{6,7},{7,6},{8,9},{9,8},{10,11... | collective-permute-start | bytes 651272 | tf_op jit(solution)/shard_map/ppermute | solution.py:608
  50.2 12.7 %collective-permute-start.87 = (f32[384,128]{1,0:T(8,128)S(1)}, f32[384,128]{1,0:T(8,128)S(1)}, u32[]{:S(2)}, u32[]{:S(2)}) collective-permute-start(f32[384,128]{1,0:T(8,128)S(1)} %get-tuple-element.346), channel_id=1, source_target_pairs={{0,1},{1,0},{2,3},{3,2},{4,5},{5,4},{6,7},{7,6},{8,9},{9,8},{10,11... | collective-permute-start | bytes 589832 | tf_op jit(solution)/shard_map/ppermute | solution.py:608
  56.9 8.6 %copy-start.6 = (f32[640,128]{1,0:T(8,128)S(1)}, f32[640,128]{1,0:T(8,128)}, u32[]{:S(2)}) copy-start(f32[640,128]{1,0:T(8,128)} %get-tuple-element.312.refs_2_) | copy-start | bytes 983044
  56.9 13.4 %collective-permute-start.94 = (f32[670,128]{1,0:T(8,128)S(1)}, f32[670,128]{1,0:T(8,128)S(1)}, u32[]{:S(2)}, u32[]{:S(2)}) collective-permute-start(f32[670,128]{1,0:T(8,128)S(1)} %get-tuple-element.349.refs_16_.refs_4_.refs_6_), channel_id=1, source_target_pairs={{0,15},{1,2},{2,1},{3,4},{4,3},{5,6},{6,5},{7,8},{8,7},{9,10},{10,... | collective-permute-start | bytes 1029128 | tf_op jit(solution)/shard_map/ppermute | solution.py:603
  66.0 11.5 %collective-permute-start.95 = (f32[640,128]{1,0:T(8,128)S(1)}, f32[640,128]{1,0:T(8,128)S(1)}, u32[]{:S(2)}, u32[]{:S(2)}) collective-permute-start(f32[640,128]{1,0:T(8,128)S(1)} %outer.15.refs_5_.refs_7_), channel_id=1, source_target_pairs={{0,15},{1,2},{2,1},{3,4},{4,3},{5,6},{6,5},{7,8},{8,7},{9,10},{10,... | collective-permute-start | bytes 983048 | tf_op jit(solution)/shard_map/ppermute | solution.py:603
  66.2 4.9 %collective-permute-start.91 = (f32[512,128]{1,0:T(8,128)S(1)}, f32[512,128]{1,0:T(8,128)S(1)}, u32[]{:S(2)}, u32[]{:S(2)}) collective-permute-start(f32[512,128]{1,0:T(8,128)S(1)} %get-tuple-element.352.refs_9_), channel_id=1, source_target_pairs={{0,1},{1,0},{2,3},{3,2},{4,5},{5,4},{6,7},{7,6},{8,9},{9,8},{10,11... | collective-permute-start | bytes 786440 | tf_op jit(solution)/shard_map/ppermute | solution.py:608
  66.2 4.9 %collective-permute-start.93 = (f32[414,128]{1,0:T(8,128)S(1)}, f32[414,128]{1,0:T(8,128)S(1)}, u32[]{:S(2)}, u32[]{:S(2)}) collective-permute-start(f32[414,128]{1,0:T(8,128)S(1)} %get-tuple-element.354), channel_id=1, source_target_pairs={{0,1},{1,0},{2,3},{3,2},{4,5},{5,4},{6,7},{7,6},{8,9},{9,8},{10,11... | collective-permute-start | bytes 635912 | tf_op jit(solution)/shard_map/ppermute | solution.py:608
  66.7 4.4 %collective-permute-start.92 = (f32[384,128]{1,0:T(8,128)S(1)}, f32[384,128]{1,0:T(8,128)S(1)}, u32[]{:S(2)}, u32[]{:S(2)}) collective-permute-start(f32[384,128]{1,0:T(8,128)S(1)} %get-tuple-element.353), channel_id=1, source_target_pairs={{0,1},{1,0},{2,3},{3,2},{4,5},{5,4},{6,7},{7,6},{8,9},{9,8},{10,11... | collective-permute-start | bytes 589832 | tf_op jit(solution)/shard_map/ppermute | solution.py:608
  71.0 13.6 %collective-permute-start.99 = (f32[660,128]{1,0:T(8,128)S(1)}, f32[660,128]{1,0:T(8,128)S(1)}, u32[]{:S(2)}, u32[]{:S(2)}) collective-permute-start(f32[660,128]{1,0:T(8,128)S(1)} %get-tuple-element.356.refs_16_.refs_4_.refs_7_.refs_6_), channel_id=1, source_target_pairs={{0,15},{1,2},{2,1},{3,4},{4,3},{5,6},{6,5},{7,8},{8,7},{9,10},{10,... | collective-permute-start | bytes 1013768 | tf_op jit(solution)/shard_map/ppermute | solution.py:603
  77.9 17.3 %collective-permute-start.100 = (f32[640,128]{1,0:T(8,128)S(1)}, f32[640,128]{1,0:T(8,128)S(1)}, u32[]{:S(2)}, u32[]{:S(2)}) collective-permute-start(f32[640,128]{1,0:T(8,128)S(1)} %outer.17.refs_5_.refs_7_), channel_id=1, source_target_pairs={{0,15},{1,2},{2,1},{3,4},{4,3},{5,6},{6,5},{7,8},{8,7},{9,10},{10,... | collective-permute-start | bytes 983048 | tf_op jit(solution)/shard_map/ppermute | solution.py:603
  78.0 7.4 %collective-permute-start.96 = (f32[512,128]{1,0:T(8,128)S(1)}, f32[512,128]{1,0:T(8,128)S(1)}, u32[]{:S(2)}, u32[]{:S(2)}) collective-permute-start(f32[512,128]{1,0:T(8,128)S(1)} %get-tuple-element.359.refs_9_), channel_id=1, source_target_pairs={{0,1},{1,0},{2,3},{3,2},{4,5},{5,4},{6,7},{7,6},{8,9},{9,8},{10,11... | collective-permute-start | bytes 786440 | tf_op jit(solution)/shard_map/ppermute | solution.py:608
  78.1 7.3 %collective-permute-start.98 = (f32[404,128]{1,0:T(8,128)S(1)}, f32[404,128]{1,0:T(8,128)S(1)}, u32[]{:S(2)}, u32[]{:S(2)}) collective-permute-start(f32[404,128]{1,0:T(8,128)S(1)} %get-tuple-element.361), channel_id=1, source_target_pairs={{0,1},{1,0},{2,3},{3,2},{4,5},{5,4},{6,7},{7,6},{8,9},{9,8},{10,11... | collective-permute-start | bytes 620552 | tf_op jit(solution)/shard_map/ppermute | solution.py:608
  78.6 6.8 %collective-permute-start.97 = (f32[384,128]{1,0:T(8,128)S(1)}, f32[384,128]{1,0:T(8,128)S(1)}, u32[]{:S(2)}, u32[]{:S(2)}) collective-permute-start(f32[384,128]{1,0:T(8,128)S(1)} %get-tuple-element.360), channel_id=1, source_target_pairs={{0,1},{1,0},{2,3},{3,2},{4,5},{5,4},{6,7},{7,6},{8,9},{9,8},{10,11... | collective-permute-start | bytes 589832 | tf_op jit(solution)/shard_map/ppermute | solution.py:608
  85.3 13.5 %collective-permute-start.104 = (f32[650,128]{1,0:T(8,128)S(1)}, f32[650,128]{1,0:T(8,128)S(1)}, u32[]{:S(2)}, u32[]{:S(2)}) collective-permute-start(f32[650,128]{1,0:T(8,128)S(1)} %get-tuple-element.363.refs_17_.refs_4_.refs_6_), channel_id=1, source_target_pairs={{0,15},{1,2},{2,1},{3,4},{4,3},{5,6},{6,5},{7,8},{8,7},{9,10},{10,... | collective-permute-start | bytes 998408 | tf_op jit(solution)/shard_map/ppermute | solution.py:603
  95.7 6.7 %collective-permute-start.105 = (f32[640,128]{1,0:T(8,128)S(1)}, f32[640,128]{1,0:T(8,128)S(1)}, u32[]{:S(2)}, u32[]{:S(2)}) collective-permute-start(f32[640,128]{1,0:T(8,128)S(1)} %outer.19.refs_5_.refs_7_), channel_id=1, source_target_pairs={{0,15},{1,2},{2,1},{3,4},{4,3},{5,6},{6,5},{7,8},{8,7},{9,10},{10,... | collective-permute-start | bytes 983048 | tf_op jit(solution)/shard_map/ppermute | solution.py:603
  95.8 3.8 %collective-permute-start.101 = (f32[512,128]{1,0:T(8,128)S(1)}, f32[512,128]{1,0:T(8,128)S(1)}, u32[]{:S(2)}, u32[]{:S(2)}) collective-permute-start(f32[512,128]{1,0:T(8,128)S(1)} %get-tuple-element.366.refs_10_), channel_id=1, source_target_pairs={{0,1},{1,0},{2,3},{3,2},{4,5},{5,4},{6,7},{7,6},{8,9},{9,8},{10,11... | collective-permute-start | bytes 786440 | tf_op jit(solution)/shard_map/ppermute | solution.py:608
  95.9 3.8 %collective-permute-start.103 = (f32[394,128]{1,0:T(8,128)S(1)}, f32[394,128]{1,0:T(8,128)S(1)}, u32[]{:S(2)}, u32[]{:S(2)}) collective-permute-start(f32[394,128]{1,0:T(8,128)S(1)} %get-tuple-element.368), channel_id=1, source_target_pairs={{0,1},{1,0},{2,3},{3,2},{4,5},{5,4},{6,7},{7,6},{8,9},{9,8},{10,11... | collective-permute-start | bytes 605192 | tf_op jit(solution)/shard_map/ppermute | solution.py:608
  96.4 3.2 %collective-permute-start.102 = (f32[384,128]{1,0:T(8,128)S(1)}, f32[384,128]{1,0:T(8,128)S(1)}, u32[]{:S(2)}, u32[]{:S(2)}) collective-permute-start(f32[384,128]{1,0:T(8,128)S(1)} %get-tuple-element.367), channel_id=1, source_target_pairs={{0,1},{1,0},{2,3},{3,2},{4,5},{5,4},{6,7},{7,6},{8,9},{9,8},{10,11... | collective-permute-start | bytes 589832 | tf_op jit(solution)/shard_map/ppermute | solution.py:608
  99.5 13.6 %collective-permute-start.107 = (f32[640,128]{1,0:T(8,128)S(1)}, f32[640,128]{1,0:T(8,128)S(1)}, u32[]{:S(2)}, u32[]{:S(2)}) collective-permute-start(f32[640,128]{1,0:T(8,128)S(1)} %get-tuple-element.370.refs_17_.refs_6_.refs_4_), channel_id=1, source_target_pairs={{0,15},{1,2},{2,1},{3,4},{4,3},{5,6},{6,5},{7,8},{8,7},{9,10},{10,... | collective-permute-start | bytes 983048 | tf_op jit(solution)/shard_map/ppermute | solution.py:603
  102.9 13.7 %collective-permute-start.106 = (f32[640,128]{1,0:T(8,128)S(1)}, f32[640,128]{1,0:T(8,128)S(1)}, u32[]{:S(2)}, u32[]{:S(2)}) collective-permute-start(f32[640,128]{1,0:T(8,128)S(1)} %outer.21.refs_7_.refs_5_), channel_id=1, source_target_pairs={{0,15},{1,2},{2,1},{3,4},{4,3},{5,6},{6,5},{7,8},{8,7},{9,10},{10,... | collective-permute-start | bytes 983048 | tf_op jit(solution)/shard_map/ppermute | solution.py:603
  104.7 2.5 %collective-permute-start.108 = (f32[512,128]{1,0:T(8,128)S(1)}, f32[512,128]{1,0:T(8,128)S(1)}, u32[]{:S(2)}, u32[]{:S(2)}) collective-permute-start(f32[512,128]{1,0:T(8,128)S(1)} %get-tuple-element.372.refs_10_), channel_id=1, source_target_pairs={{0,1},{1,0},{2,3},{3,2},{4,5},{5,4},{6,7},{7,6},{8,9},{9,8},{10,11... | collective-permute-start | bytes 786440 | tf_op jit(solution)/shard_map/ppermute | solution.py:608
  105.4 1.4 %collective-permute-start.109 = (f32[384,128]{1,0:T(8,128)S(1)}, f32[384,128]{1,0:T(8,128)S(1)}, u32[]{:S(2)}, u32[]{:S(2)}) collective-permute-start(f32[384,128]{1,0:T(8,128)S(1)} %get-tuple-element.375), channel_id=1, source_target_pairs={{0,1},{1,0},{2,3},{3,2},{4,5},{5,4},{6,7},{7,6},{8,9},{9,8},{10,11... | collective-permute-start | bytes 589832 | tf_op jit(solution)/shard_map/ppermute | solution.py:608
  105.4 1.7 %collective-permute-start.110 = (f32[384,128]{1,0:T(8,128)S(1)}, f32[384,128]{1,0:T(8,128)S(1)}, u32[]{:S(2)}, u32[]{:S(2)}) collective-permute-start(f32[384,128]{1,0:T(8,128)S(1)} %get-tuple-element.376), channel_id=1, source_target_pairs={{0,1},{1,0},{2,3},{3,2},{4,5},{5,4},{6,7},{7,6},{8,9},{9,8},{10,11... | collective-permute-start | bytes 589832 | tf_op jit(solution)/shard_map/ppermute | solution.py:608

commit v4 on v3

--- a/solution.py
+++ b/solution.py
@@ -13,7 +13,7 @@
 CHUNK = 16
 STRIP = 8
 NEED = 6
-HALF = 32
+HALF = 30
 PARTS = 2
 PIECES = (4, 3, 3)
 

time: 117 us -> 117 us (level)
  starting transfers between devices: 36.1 us -> 33.4 us
  waiting for transfers between devices: 44.7 us -> 47.2 us
    ppermute x4, starting transfers between devices: 6.59 us -> 12.7 us  [shifted(): lax.ppermute(value, 'theta', [(i, (i + steps) % count) for i in range(cou...]
    ppermute x14, starting transfers between devices: 16.7 us -> 11.2 us  [across_chips(): return lax.ppermute(value, 'theta', pairs)]
    ppermute x14, waiting for transfers between devices: 40.1 us -> 45 us  [across_chips(): return lax.ppermute(value, 'theta', pairs)]
    ppermute x18, starting transfers between devices: 12.8 us -> 9.49 us  [within_chip(): return lax.ppermute(value, 'theta', [(i, i ^ 1) for i in range(count)])]
    ppermute x4, waiting for transfers between devices: 3.36 us -> 0.92 us  [shifted(): lax.ppermute(value, 'theta', [(i, (i + steps) % count) for i in range(cou...]
  transfers between devices with their start and end apart: 36 -> 36, of which waited for: 15 -> 14; matrix products, arithmetic and copies ran while one was open for 0% -> 0% of each run, Pallas kernels for 28% -> 28%
where the time goes in v4:
time: 117 us; the launch traced here: 118 us
  waiting for transfers between devices  47.2 us (40%)
  Pallas kernels  35.6 us (30%)
  starting transfers between devices  33.4 us (29%)
  between operations  1.3 us (1%)
    ppermute x14, waiting for transfers between devices, across_chips(): return lax.ppermute(value, 'theta', pairs)  45 us
    pallas_call x20, Pallas kernels, run(): pl.pallas_call(lambda *refs: kernel(list(refs)), out_shape=outs, in_specs...  28.9 us
    ppermute x4, starting transfers between devices, shifted(): lax.ppermute(value, 'theta', [(i, (i + steps) % count) for i in range(cou...  12.7 us
    ppermute x14, starting transfers between devices, across_chips(): return lax.ppermute(value, 'theta', pairs)  11.2 us
    ppermute x18, starting transfers between devices, within_chip(): return lax.ppermute(value, 'theta', [(i, i ^ 1) for i in range(count)])  9.49 us
    pallas_call x1, Pallas kernels, call_gather(): pl.pallas_call(gather_kernel, out_shape=(strips,) * 2 + (part,) * (3 * PA...  5.66 us
  transfers between devices with their start and end apart: 36, of which 14 were waited for; matrix products, arithmetic and copies ran while one was open for 0% of the time, Pallas kernels for 28%

profile of v4, /device:TPU:1, one launch (start us, length us, event | category | flops | bytes accessed | tf_op | source)
XLA Modules:
  0.0 118.0 jit_solution(3248010398311884506)
XLA Ops:
  0.0 1.0 outer_layer.1._
  1.0 2.7 %collective-permute-start.80 = (f32[640,128]{1,0:T(8,128)S(1)}, f32[640,128]{1,0:T(8,128)S(1)}, u32[]{:S(2)}, u32[]{:S(2)}) collective-permute-start(f32[640,128]{1,0:T(8,128)S(1)} %outer_layer.1._), channel_id=1, source_target_pairs={{0,15},{1,2},{2,1},{3,4},{4,3},{5,6},{6,5},{7,8},{8,7},{9,10},{10,... | collective-permute-start | bytes 983048 | tf_op jit(solution)/shard_map/ppermute | solution.py:603
  3.7 5.7 %gather_strips.1 = (f32[270,128]{1,0:T(8,128)S(1)}, f32[270,128]{1,0:T(8,128)S(1)}, f32[640,128]{1,0:T(8,128)}, f32[640,128]{1,0:T(8,128)}, f32[640,128]{1,0:T(8...) custom-call(f32[5,2,4,128,128]{4,3,2,1,0:T(8,128)} %refs_3_.11, ...), custom_call_target="tpu_custom_call" | custom-call | flops 1 | bytes 1 | tf_op jit(solution)/shard_map/gather_strips/pallas_call | solution.py:559
  9.4 2.9 %collective-permute-start.82 = (f32[270,128]{1,0:T(8,128)S(1)}, f32[270,128]{1,0:T(8,128)S(1)}, u32[]{:S(2)}, u32[]{:S(2)}) collective-permute-start(f32[270,128]{1,0:T(8,128)S(1)} %get-tuple-element.318.refs_2_), channel_id=1, source_target_pairs={{0,15},{1,0},{2,1},{3,2},{4,3},{5,4},{6,5},{7,6},{8,7},{9,8},{10,9... | collective-permute-start | bytes 414728 | tf_op jit(solution)/shard_map/ppermute | solution.py:597
  13.1 0.8 collective-permute-done.82.refs_4_
  14.0 20.2 %conditional.1 = (f32[256,128]{1,0:T(8,128)}, f32[192,128]{1,0:T(8,128)}, f32[192,128]{1,0:T(8,128)}, f32[300,128]{1,0:T(8,128)}, f32[300,128]{1,0:T(8,128)}) conditional(s32[]{:T(128)} %clamp.3, (f32[256,128]{1,0:T(8,128)}, f32[192,128]{1,0:T(8,128)}, f32[192,128]{1,0:T(8,128)}, f32[300,128]{1,0:T(8,128)S(1)}, ...), branch_computations={%region_0.1_spmd, %region_1.2_spmd, %region_2.3_spmd, %region_3.4_... | conditional | bytes 2539760 | solution.py:621
  14.1 9.7 %collective-permute-start.73 = (f32[300,128]{1,0:T(8,128)S(1)}, f32[300,128]{1,0:T(8,128)}, u32[]{:S(2)}, u32[]{:S(2)}) collective-permute-start(f32[300,128]{1,0:T(8,128)S(1)} %get-tuple-element.238), channel_id=1, source_target_pairs={{0,14},{1,15},{2,0},{3,1},{4,2},{5,3},{6,4},{7,5},{8,6},{9,7},{10,... | collective-permute-start | bytes 460808 | tf_op jit(solution)/shard_map/cond/branch_14_fun/ppermute | solution.py:597
  23.8 1.7 %collective-permute-start.71 = (f32[192,128]{1,0:T(8,128)}, f32[192,128]{1,0:T(8,128)}, u32[]{:S(2)}, u32[]{:S(2)}) collective-permute-start(f32[192,128]{1,0:T(8,128)} %get-tuple-element.236), channel_id=1, source_target_pairs={{0,15},{1,2},{2,1},{3,4},{4,3},{5,6},{6,5},{7,8},{8,7},{9,10},{10,... | collective-permute-start | bytes 294920 | tf_op jit(solution)/shard_map/cond/branch_14_fun/ppermute | solution.py:603
  25.6 7.1 %collective-permute-done.71 = f32[192,128]{1,0:T(8,128)} collective-permute-done((f32[192,128]{1,0:T(8,128)}, f32[192,128]{1,0:T(8,128)}, u32[]{:S(2)}, u32[]{:S(2)}) %collective-permute-start.71) | collective-permute-done | bytes 98336 | tf_op jit(solution)/shard_map/cond/branch_14_fun/ppermute | solution.py:603
  32.7 1.4 %collective-permute-done.72 = f32[192,128]{1,0:T(8,128)} collective-permute-done((f32[192,128]{1,0:T(8,128)}, f32[192,128]{1,0:T(8,128)}, u32[]{:S(2)}, u32[]{:S(2)}) %collective-permute-start.72) | collective-permute-done | bytes 98336 | tf_op jit(solution)/shard_map/cond/branch_14_fun/ppermute | solution.py:603
  34.2 2.6 %collective-permute-start.83 = (f32[512,128]{1,0:T(8,128)}, f32[512,128]{1,0:T(8,128)S(1)}, u32[]{:S(2)}, u32[]{:S(2)}) collective-permute-start(f32[512,128]{1,0:T(8,128)} %get-tuple-element.326), channel_id=1, source_target_pairs={{0,1},{1,0},{2,3},{3,2},{4,5},{5,4},{6,7},{7,6},{8,9},{9,8},{10,11... | collective-permute-start | bytes 786440 | tf_op jit(solution)/shard_map/ppermute | solution.py:608
  37.5 1.1 scatter_strips.1
  38.7 2.3 %outer.12 = (f32[680,128]{1,0:T(8,128)S(1)}, f32[2,5,8,128]{3,2,1,0:T(8,128)S(1)}) custom-call(f32[16,128]{1,0:T(8,128)S(1)} %broadcast_in_dim.2.refs_0_, f32[2,128,128]{2,1,0:T(8,128)} %get-tuple-element.311.refs_1_, f32[640,128]{1,0:T(8,128)} %get-tuple-element.337.refs_2_, f32[640,128]{1,0:T(8,128)} %get-tuple-element.338.refs_3_, ...), custom_call_target="tpu_custom_call" | custom-call | flops 1 | bytes 1 | tf_op jit(solution)/shard_map/outer/pallas_call | solution.py:522
  41.1 1.9 %outer.13.refs_17_.refs_5_.refs_7_ = f32[640,128]{1,0:T(8,128)S(1)} custom-call(f32[16,128]{1,0:T(8,128)S(1)} %broadcast_in_dim.2.refs_0_, f32[2,128,128]{2,1,0:T(8,128)} %get-tuple-element.311.refs_1_, f32[640,128]{1,0:T(8,128)} %get-tuple-element.312.refs_2_, f32[640,128]{1,0:T(8,128)} %get-tuple-element.333.refs_3_, ...), custom_call_target="tpu_custom_call" | custom-call | flops 1 | bytes 1 | tf_op jit(solution)/shard_map/outer/pallas_call | solution.py:522
  43.0 1.8 %collective-permute-start.90 = (f32[640,128]{1,0:T(8,128)S(1)}, f32[640,128]{1,0:T(8,128)S(1)}, u32[]{:S(2)}, u32[]{:S(2)}) collective-permute-start(f32[640,128]{1,0:T(8,128)S(1)} %outer.13.refs_17_.refs_5_.refs_7_), channel_id=1, source_target_pairs={{0,15},{1,2},{2,1},{3,4},{4,3},{5,6},{6,5},{7,8},{8,7},{9,10},{10,... | collective-permute-start | bytes 983048 | tf_op jit(solution)/shard_map/ppermute | solution.py:603
  44.9 2.5 %inner.6 = (f32[5,2,3,128,128]{4,3,2,1,0:T(8,128)S(1)}, f32[512,128]{1,0:T(8,128)S(1)}, f32[384,128]{1,0:T(8,128)S(1)}, f32[424,128]{1,0:T(8,128)S(1)}, f32[2,5,3,8,128]{4,3,2,1,0:T(8,128)S(1)}) custom-call(f32[16,128]{1,0:T(8,128)S(1)} %broadcast_in_dim.2.refs_0_, f32[2,4,128,128]{3,2,1,0:T(8,128)S(1)} %copy-done.4, f32[5,2,4,128,128]{4,3,2,1,0:T(8,128)S(1)} %copy-done.1, ...), custom_call_target="tpu_custom_call" | custom-call | flops 1 | bytes 1 | tf_op jit(solution)/shard_map/inner/pallas_call | solution.py:522
  47.4 2.8 %collective-permute-start.86 = (f32[512,128]{1,0:T(8,128)S(1)}, f32[512,128]{1,0:T(8,128)S(1)}, u32[]{:S(2)}, u32[]{:S(2)}) collective-permute-start(f32[512,128]{1,0:T(8,128)S(1)} %get-tuple-element.345), channel_id=1, source_target_pairs={{0,1},{1,0},{2,3},{3,2},{4,5},{5,4},{6,7},{7,6},{8,9},{9,8},{10,11... | collective-permute-start | bytes 786440 | tf_op jit(solution)/shard_map/ppermute | solution.py:608
  50.8 8.6 %collective-permute-done.89.refs_7_ = f32[680,128]{1,0:T(8,128)S(1)} collective-permute-done((f32[680,128]{1,0:T(8,128)S(1)}, f32[680,128]{1,0:T(8,128)S(1)}, u32[]{:S(2)}, u32[]{:S(2)}) %collective-permute-start.89) | collective-permute-done | bytes 348192 | tf_op jit(solution)/shard_map/ppermute | solution.py:603
  59.4 0.7 outer.14
  60.1 2.5 %collective-permute-start.94 = (f32[670,128]{1,0:T(8,128)S(1)}, f32[670,128]{1,0:T(8,128)S(1)}, u32[]{:S(2)}, u32[]{:S(2)}) collective-permute-start(f32[670,128]{1,0:T(8,128)S(1)} %get-tuple-element.349.refs_16_.refs_4_.refs_6_), channel_id=1, source_target_pairs={{0,15},{1,2},{2,1},{3,4},{4,3},{5,6},{6,5},{7,8},{8,7},{9,10},{10,... | collective-permute-start | bytes 1029128 | tf_op jit(solution)/shard_map/ppermute | solution.py:603
  62.7 2.5 %inner.7 = (f32[5,2,3,128,128]{4,3,2,1,0:T(8,128)S(1)}, f32[512,128]{1,0:T(8,128)S(1)}, f32[384,128]{1,0:T(8,128)S(1)}, f32[414,128]{1,0:T(8,128)S(1)}, f32[2,5,3,8,128]{4,3,2,1,0:T(8,128)S(1)}) custom-call(f32[16,128]{1,0:T(8,128)S(1)} %broadcast_in_dim.2.refs_0_, f32[2,4,128,128]{3,2,1,0:T(8,128)S(1)} %copy-done.4, f32[5,2,4,128,128]{4,3,2,1,0:T(8,128)S(1)} %copy-done.1, ...), custom_call_target="tpu_custom_call" | custom-call | flops 1 | bytes 1 | tf_op jit(solution)/shard_map/inner/pallas_call | solution.py:522
  65.2 0.4 outer.15.refs_5_.refs_7_
  65.9 0.5 collective-permute-start.93
  66.4 3.8 %collective-permute-done.94.refs_7_ = f32[670,128]{1,0:T(8,128)S(1)} collective-permute-done((f32[670,128]{1,0:T(8,128)S(1)}, f32[670,128]{1,0:T(8,128)S(1)}, u32[]{:S(2)}, u32[]{:S(2)}) %collective-permute-start.94) | collective-permute-done | bytes 343072 | tf_op jit(solution)/shard_map/ppermute | solution.py:603
  70.3 0.7 outer.16
  71.1 2.6 %inner.8 = (f32[5,2,3,128,128]{4,3,2,1,0:T(8,128)S(1)}, f32[512,128]{1,0:T(8,128)S(1)}, f32[384,128]{1,0:T(8,128)S(1)}, f32[404,128]{1,0:T(8,128)S(1)}, f32[2,5,3,8,128]{4,3,2,1,0:T(8,128)S(1)}) custom-call(f32[16,128]{1,0:T(8,128)S(1)} %broadcast_in_dim.2.refs_0_, f32[2,4,128,128]{3,2,1,0:T(8,128)S(1)} %copy-done.4, f32[5,2,4,128,128]{4,3,2,1,0:T(8,128)S(1)} %copy-done.1, ...), custom_call_target="tpu_custom_call" | custom-call | flops 1 | bytes 1 | tf_op jit(solution)/shard_map/inner/pallas_call | solution.py:522
  73.7 3.8 %collective-permute-done.95.refs_7_ = f32[640,128]{1,0:T(8,128)S(1)} collective-permute-done((f32[640,128]{1,0:T(8,128)S(1)}, f32[640,128]{1,0:T(8,128)S(1)}, u32[]{:S(2)}, u32[]{:S(2)}) %collective-permute-start.95) | collective-permute-done | bytes 327712 | tf_op jit(solution)/shard_map/ppermute | solution.py:603
  77.4 0.5 outer.17.refs_5_.refs_7_
  78.1 0.5 collective-permute-start.98
  78.6 5.9 %collective-permute-done.99.refs_8_ = f32[660,128]{1,0:T(8,128)S(1)} collective-permute-done((f32[660,128]{1,0:T(8,128)S(1)}, f32[660,128]{1,0:T(8,128)S(1)}, u32[]{:S(2)}, u32[]{:S(2)}) %collective-permute-start.99) | collective-permute-done | bytes 337952 | tf_op jit(solution)/shard_map/ppermute | solution.py:603
  84.6 0.7 outer.18
  85.4 2.7 %inner.9 = (f32[5,2,3,128,128]{4,3,2,1,0:T(8,128)S(1)}, f32[512,128]{1,0:T(8,128)S(1)}, f32[384,128]{1,0:T(8,128)S(1)}, f32[394,128]{1,0:T(8,128)S(1)}, f32[2,5,3,8,128]{4,3,2,1,0:T(8,128)S(1)}) custom-call(f32[16,128]{1,0:T(8,128)S(1)} %broadcast_in_dim.2.refs_0_, f32[2,4,128,128]{3,2,1,0:T(8,128)S(1)} %copy-done.4, f32[5,2,4,128,128]{4,3,2,1,0:T(8,128)S(1)} %copy-done.1, ...), custom_call_target="tpu_custom_call" | custom-call | flops 1 | bytes 1 | tf_op jit(solution)/shard_map/inner/pallas_call | solution.py:522
  88.1 7.1 %collective-permute-done.100.refs_8_ = f32[640,128]{1,0:T(8,128)S(1)} collective-permute-done((f32[640,128]{1,0:T(8,128)S(1)}, f32[640,128]{1,0:T(8,128)S(1)}, u32[]{:S(2)}, u32[]{:S(2)}) %collective-permute-start.100) | collective-permute-done | bytes 327712 | tf_op jit(solution)/shard_map/ppermute | solution.py:603
  95.2 0.5 outer.19.refs_5_.refs_7_
  95.8 0.5 collective-permute-start.103
  96.4 2.4 %collective-permute-done.104.refs_8_ = f32[650,128]{1,0:T(8,128)S(1)} collective-permute-done((f32[650,128]{1,0:T(8,128)S(1)}, f32[650,128]{1,0:T(8,128)S(1)}, u32[]{:S(2)}, u32[]{:S(2)}) %collective-permute-start.104) | collective-permute-done | bytes 332832 | tf_op jit(solution)/shard_map/ppermute | solution.py:603
  98.8 0.7 outer.20
  99.6 2.7 %inner.10 = (f32[5,2,3,128,128]{4,3,2,1,0:T(8,128)S(1)}, f32[512,128]{1,0:T(8,128)S(1)}, f32[384,128]{1,0:T(8,128)S(1)}, f32[384,128]{1,0:T(8,128)S(1)}, f32[2,5,3,8,128]{4,3,2,1,0:T(8,128)S(1)}) custom-call(f32[16,128]{1,0:T(8,128)S(1)} %broadcast_in_dim.2.refs_0_, f32[2,4,128,128]{3,2,1,0:T(8,128)S(1)} %copy-done.4, f32[5,2,4,128,128]{4,3,2,1,0:T(8,128)S(1)} %copy-done.1, ...), custom_call_target="tpu_custom_call" | custom-call | flops 1 | bytes 1 | tf_op jit(solution)/shard_map/inner/pallas_call | solution.py:522
  102.4 0.5 outer.21.refs_7_.refs_5_
  102.9 1.8 %collective-permute-start.106 = (f32[640,128]{1,0:T(8,128)S(1)}, f32[640,128]{1,0:T(8,128)S(1)}, u32[]{:S(2)}, u32[]{:S(2)}) collective-permute-start(f32[640,128]{1,0:T(8,128)S(1)} %outer.21.refs_7_.refs_5_), channel_id=1, source_target_pairs={{0,15},{1,2},{2,1},{3,4},{4,3},{5,6},{6,5},{7,8},{8,7},{9,10},{10,... | collective-permute-start | bytes 983048 | tf_op jit(solution)/shard_map/ppermute | solution.py:603
  104.6 0.8 collective-permute-start.108
  105.4 0.5 collective-permute-start.110
  105.9 0.9 collective-permute-done.109.refs_9_
  107.1 3.3 %inner.11.refs_10_ = f32[5,2,4,128,128]{4,3,2,1,0:T(8,128)} custom-call(f32[16,128]{1,0:T(8,128)S(1)} %broadcast_in_dim.2.refs_0_, f32[2,4,128,128]{3,2,1,0:T(8,128)S(1)} %copy-done.4, f32[5,2,4,128,128]{4,3,2,1,0:T(8,128)S(1)} %copy-done.1, f32[5,2,4,128,128]{4,3,2,1,0:T(8,128)S(1)} %copy-done, ...), custom_call_target="tpu_custom_call" | custom-call | flops 1 | bytes 1 | tf_op jit(solution)/shard_map/inner/pallas_call | solution.py:522
  110.4 2.7 %collective-permute-done.107.refs_8_ = f32[640,128]{1,0:T(8,128)S(1)} collective-permute-done((f32[640,128]{1,0:T(8,128)S(1)}, f32[640,128]{1,0:T(8,128)S(1)}, u32[]{:S(2)}, u32[]{:S(2)}) %collective-permute-start.107) | collective-permute-done | bytes 327712 | tf_op jit(solution)/shard_map/ppermute | solution.py:603
  113.1 1.2 %outer.22.refs_10_ = f32[5,2,4,128,128]{4,3,2,1,0:T(8,128)} custom-call(f32[16,128]{1,0:T(8,128)S(1)} %broadcast_in_dim.2.refs_0_, f32[2,128,128]{2,1,0:T(8,128)S(1)} %copy-done.5, f32[640,128]{1,0:T(8,128)S(1)} %copy-done.7, f32[5,2,3,128,128]{4,3,2,1,0:T(8,128)S(1)} %get-tuple-element.371.refs_4_.refs_3_, ...), custom_call_target="tpu_custom_call", output_to_operand_aliasing={{}: (10, {})} | custom-call | flops 1 | bytes 1 | tf_op jit(solution)/shard_map/outer/pallas_call | solution.py:522
  114.3 2.3 %collective-permute-done.106.refs_8_ = f32[640,128]{1,0:T(8,128)S(1)} collective-permute-done((f32[640,128]{1,0:T(8,128)S(1)}, f32[640,128]{1,0:T(8,128)S(1)}, u32[]{:S(2)}, u32[]{:S(2)}) %collective-permute-start.106) | collective-permute-done | bytes 327712 | tf_op jit(solution)/shard_map/ppermute | solution.py:603
  116.6 1.2 %outer.23 = f32[5,2,4,128,128]{4,3,2,1,0:T(8,128)} custom-call(f32[16,128]{1,0:T(8,128)S(1)} %broadcast_in_dim.2.refs_0_, f32[2,128,128]{2,1,0:T(8,128)S(1)} %copy-done.5, f32[640,128]{1,0:T(8,128)S(1)} %copy-done.6, f32[5,2,3,128,128]{4,3,2,1,0:T(8,128)S(1)} %get-tuple-element.371.refs_4_.refs_3_, ...), custom_call_target="tpu_custom_call", output_to_operand_aliasing={{}: (10, {})} | custom-call | flops 1 | bytes 1 | tf_op jit(solution)/shard_map/outer/pallas_call | solution.py:522
  (72 shorter events, 3.0 us)
Async XLA Ops:
  1.0 36.3 %copy-start.9 = (f32[2,4]{1,0:T(2,128)S(1)}, f32[2,4]{1,0:T(2,128)}, u32[]{:S(2)}) copy-start(f32[2,4]{1,0:T(2,128)} %param.24) | copy-start | bytes 100
  1.0 13.0 %collective-permute-start.80 = (f32[640,128]{1,0:T(8,128)S(1)}, f32[640,128]{1,0:T(8,128)S(1)}, u32[]{:S(2)}, u32[]{:S(2)}) collective-permute-start(f32[640,128]{1,0:T(8,128)S(1)} %outer_layer.1._), channel_id=1, source_target_pairs={{0,15},{1,2},{2,1},{3,4},{4,3},{5,6},{6,5},{7,8},{8,7},{9,10},{10,... | collective-permute-start | bytes 983048 | tf_op jit(solution)/shard_map/ppermute | solution.py:603
  9.3 3.8 %collective-permute-start.81 = (f32[270,128]{1,0:T(8,128)S(1)}, f32[270,128]{1,0:T(8,128)S(1)}, u32[]{:S(2)}, u32[]{:S(2)}) collective-permute-start(f32[270,128]{1,0:T(8,128)S(1)} %get-tuple-element.317.refs_1_), channel_id=1, source_target_pairs={{0,1},{1,2},{2,3},{3,4},{4,5},{5,6},{6,7},{7,8},{8,9},{9,10},{10,1... | collective-permute-start | bytes 414728 | tf_op jit(solution)/shard_map/ppermute | solution.py:597
  9.4 4.5 %collective-permute-start.82 = (f32[270,128]{1,0:T(8,128)S(1)}, f32[270,128]{1,0:T(8,128)S(1)}, u32[]{:S(2)}, u32[]{:S(2)}) collective-permute-start(f32[270,128]{1,0:T(8,128)S(1)} %get-tuple-element.318.refs_2_), channel_id=1, source_target_pairs={{0,15},{1,0},{2,1},{3,2},{4,3},{5,4},{6,5},{7,6},{8,7},{9,8},{10,9... | collective-permute-start | bytes 414728 | tf_op jit(solution)/shard_map/ppermute | solution.py:597
  13.9 30.9 %copy-start.3 = (f32[640,128]{1,0:T(8,128)S(1)}, f32[640,128]{1,0:T(8,128)}, u32[]{:S(2)}) copy-start(f32[640,128]{1,0:T(8,128)} %get-tuple-element.324.refs_4_.refs_6_) | copy-start | bytes 983044
  13.9 30.9 %copy-start.4 = (f32[2,4,128,128]{3,2,1,0:T(8,128)S(1)}, f32[2,4,128,128]{3,2,1,0:T(8,128)}, u32[]{:S(2)}) copy-start(f32[2,4,128,128]{3,2,1,0:T(8,128)} %refs_1_.11) | copy-start | bytes 1572868
  14.0 24.7 %copy-start.8 = (f32[640,128]{1,0:T(8,128)}, f32[640,128]{1,0:T(8,128)S(1)}, u32[]{:S(2)}) copy-start(f32[640,128]{1,0:T(8,128)S(1)} %collective-permute-done.80.refs_7_) | copy-start | bytes 983044
  14.1 20.0 %collective-permute-start.73 = (f32[300,128]{1,0:T(8,128)S(1)}, f32[300,128]{1,0:T(8,128)}, u32[]{:S(2)}, u32[]{:S(2)}) collective-permute-start(f32[300,128]{1,0:T(8,128)S(1)} %get-tuple-element.238), channel_id=1, source_target_pairs={{0,14},{1,15},{2,0},{3,1},{4,2},{5,3},{6,4},{7,5},{8,6},{9,7},{10,... | collective-permute-start | bytes 460808 | tf_op jit(solution)/shard_map/cond/branch_14_fun/ppermute | solution.py:597
  23.8 10.2 %collective-permute-start.74 = (f32[300,128]{1,0:T(8,128)S(1)}, f32[300,128]{1,0:T(8,128)}, u32[]{:S(2)}, u32[]{:S(2)}) collective-permute-start(f32[300,128]{1,0:T(8,128)S(1)} %get-tuple-element.239), channel_id=1, source_target_pairs={{0,2},{1,3},{2,4},{3,5},{4,6},{5,7},{6,8},{7,9},{8,10},{9,11},{10,... | collective-permute-start | bytes 460808 | tf_op jit(solution)/shard_map/cond/branch_14_fun/ppermute | solution.py:597
  23.8 10.2 %collective-permute-start.70 = (f32[256,128]{1,0:T(8,128)}, f32[256,128]{1,0:T(8,128)}, u32[]{:S(2)}, u32[]{:S(2)}) collective-permute-start(f32[256,128]{1,0:T(8,128)} %get-tuple-element.235), channel_id=1, source_target_pairs={{0,15},{1,2},{2,1},{3,4},{4,3},{5,6},{6,5},{7,8},{8,7},{9,10},{10,... | collective-permute-start | bytes 393224 | tf_op jit(solution)/shard_map/cond/branch_14_fun/ppermute | solution.py:603
  23.8 8.9 %collective-permute-start.71 = (f32[192,128]{1,0:T(8,128)}, f32[192,128]{1,0:T(8,128)}, u32[]{:S(2)}, u32[]{:S(2)}) collective-permute-start(f32[192,128]{1,0:T(8,128)} %get-tuple-element.236), channel_id=1, source_target_pairs={{0,15},{1,2},{2,1},{3,4},{4,3},{5,6},{6,5},{7,8},{8,7},{9,10},{10,... | collective-permute-start | bytes 294920 | tf_op jit(solution)/shard_map/cond/branch_14_fun/ppermute | solution.py:603
  25.5 8.5 %collective-permute-start.72 = (f32[192,128]{1,0:T(8,128)}, f32[192,128]{1,0:T(8,128)}, u32[]{:S(2)}, u32[]{:S(2)}) collective-permute-start(f32[192,128]{1,0:T(8,128)} %get-tuple-element.237), channel_id=1, source_target_pairs={{0,15},{1,2},{2,1},{3,4},{4,3},{5,6},{6,5},{7,8},{8,7},{9,10},{10,... | collective-permute-start | bytes 294920 | tf_op jit(solution)/shard_map/cond/branch_14_fun/ppermute | solution.py:603
  34.2 10.6 %collective-permute-start.83 = (f32[512,128]{1,0:T(8,128)}, f32[512,128]{1,0:T(8,128)S(1)}, u32[]{:S(2)}, u32[]{:S(2)}) collective-permute-start(f32[512,128]{1,0:T(8,128)} %get-tuple-element.326), channel_id=1, source_target_pairs={{0,1},{1,0},{2,3},{3,2},{4,5},{5,4},{6,7},{7,6},{8,9},{9,8},{10,11... | collective-permute-start | bytes 786440 | tf_op jit(solution)/shard_map/ppermute | solution.py:608
  36.8 8.0 %collective-permute-start.84 = (f32[384,128]{1,0:T(8,128)}, f32[384,128]{1,0:T(8,128)S(1)}, u32[]{:S(2)}, u32[]{:S(2)}) collective-permute-start(f32[384,128]{1,0:T(8,128)} %get-tuple-element.327), channel_id=1, source_target_pairs={{0,1},{1,0},{2,3},{3,2},{4,5},{5,4},{6,7},{7,6},{8,9},{9,8},{10,11... | collective-permute-start | bytes 589832 | tf_op jit(solution)/shard_map/ppermute | solution.py:608
  36.9 8.0 %collective-permute-start.85 = (f32[384,128]{1,0:T(8,128)}, f32[384,128]{1,0:T(8,128)S(1)}, u32[]{:S(2)}, u32[]{:S(2)}) collective-permute-start(f32[384,128]{1,0:T(8,128)} %get-tuple-element.328), channel_id=1, source_target_pairs={{0,1},{1,0},{2,3},{3,2},{4,5},{5,4},{6,7},{7,6},{8,9},{9,8},{10,11... | collective-permute-start | bytes 589832 | tf_op jit(solution)/shard_map/ppermute | solution.py:608
  37.5 7.3 %copy-start.2 = (f32[640,128]{1,0:T(8,128)S(1)}, f32[640,128]{1,0:T(8,128)}, u32[]{:S(2)}) copy-start(f32[640,128]{1,0:T(8,128)} %get-tuple-element.325.refs_5_.refs_6_.refs_7_) | copy-start | bytes 983044
  38.7 6.1 %copy-start = (f32[5,2,4,128,128]{4,3,2,1,0:T(8,128)S(1)}, f32[5,2,4,128,128]{4,3,2,1,0:T(8,128)}, u32[]{:S(2)}) copy-start(f32[5,2,4,128,128]{4,3,2,1,0:T(8,128)} %refs_3_.11) | copy-start | bytes 7864324
  38.7 6.2 %copy-start.1 = (f32[5,2,4,128,128]{4,3,2,1,0:T(8,128)S(1)}, f32[5,2,4,128,128]{4,3,2,1,0:T(8,128)}, u32[]{:S(2)}) copy-start(f32[5,2,4,128,128]{4,3,2,1,0:T(8,128)} %refs_2_.11) | copy-start | bytes 7864324
  41.0 18.4 %collective-permute-start.89 = (f32[680,128]{1,0:T(8,128)S(1)}, f32[680,128]{1,0:T(8,128)S(1)}, u32[]{:S(2)}, u32[]{:S(2)}) collective-permute-start(f32[680,128]{1,0:T(8,128)S(1)} %get-tuple-element.342.refs_11_.refs_4_.refs_6_), channel_id=1, source_target_pairs={{0,15},{1,2},{2,1},{3,4},{4,3},{5,6},{6,5},{7,8},{8,7},{9,10},{10,... | collective-permute-start | bytes 1044488 | tf_op jit(solution)/shard_map/ppermute | solution.py:603
  43.0 22.2 %collective-permute-start.90 = (f32[640,128]{1,0:T(8,128)S(1)}, f32[640,128]{1,0:T(8,128)S(1)}, u32[]{:S(2)}, u32[]{:S(2)}) collective-permute-start(f32[640,128]{1,0:T(8,128)S(1)} %outer.13.refs_17_.refs_5_.refs_7_), channel_id=1, source_target_pairs={{0,15},{1,2},{2,1},{3,4},{4,3},{5,6},{6,5},{7,8},{8,7},{9,10},{10,... | collective-permute-start | bytes 983048 | tf_op jit(solution)/shard_map/ppermute | solution.py:603
  44.9 14.5 %copy-start.5 = (f32[2,128,128]{2,1,0:T(8,128)S(1)}, f32[2,128,128]{2,1,0:T(8,128)}, u32[]{:S(2)}) copy-start(f32[2,128,128]{2,1,0:T(8,128)} %get-tuple-element.311.refs_1_) | copy-start | bytes 393220
  44.9 14.5 %copy-start.7 = (f32[640,128]{1,0:T(8,128)S(1)}, f32[640,128]{1,0:T(8,128)}, u32[]{:S(2)}) copy-start(f32[640,128]{1,0:T(8,128)} %get-tuple-element.337.refs_2_) | copy-start | bytes 983044
  47.4 15.3 %collective-permute-start.86 = (f32[512,128]{1,0:T(8,128)S(1)}, f32[512,128]{1,0:T(8,128)S(1)}, u32[]{:S(2)}, u32[]{:S(2)}) collective-permute-start(f32[512,128]{1,0:T(8,128)S(1)} %get-tuple-element.345), channel_id=1, source_target_pairs={{0,1},{1,0},{2,3},{3,2},{4,5},{5,4},{6,7},{7,6},{8,9},{9,8},{10,11... | collective-permute-start | bytes 786440 | tf_op jit(solution)/shard_map/ppermute | solution.py:608
  50.3 12.4 %collective-permute-start.88 = (f32[424,128]{1,0:T(8,128)S(1)}, f32[424,128]{1,0:T(8,128)S(1)}, u32[]{:S(2)}, u32[]{:S(2)}) collective-permute-start(f32[424,128]{1,0:T(8,128)S(1)} %get-tuple-element.347), channel_id=1, source_target_pairs={{0,1},{1,0},{2,3},{3,2},{4,5},{5,4},{6,7},{7,6},{8,9},{9,8},{10,11... | collective-permute-start | bytes 651272 | tf_op jit(solution)/shard_map/ppermute | solution.py:608
  50.3 12.3 %collective-permute-start.87 = (f32[384,128]{1,0:T(8,128)S(1)}, f32[384,128]{1,0:T(8,128)S(1)}, u32[]{:S(2)}, u32[]{:S(2)}) collective-permute-start(f32[384,128]{1,0:T(8,128)S(1)} %get-tuple-element.346), channel_id=1, source_target_pairs={{0,1},{1,0},{2,3},{3,2},{4,5},{5,4},{6,7},{7,6},{8,9},{9,8},{10,11... | collective-permute-start | bytes 589832 | tf_op jit(solution)/shard_map/ppermute | solution.py:608
  60.1 5.1 %copy-start.6 = (f32[640,128]{1,0:T(8,128)S(1)}, f32[640,128]{1,0:T(8,128)}, u32[]{:S(2)}) copy-start(f32[640,128]{1,0:T(8,128)} %get-tuple-element.312.refs_2_) | copy-start | bytes 983044
  60.1 10.1 %collective-permute-start.94 = (f32[670,128]{1,0:T(8,128)S(1)}, f32[670,128]{1,0:T(8,128)S(1)}, u32[]{:S(2)}, u32[]{:S(2)}) collective-permute-start(f32[670,128]{1,0:T(8,128)S(1)} %get-tuple-element.349.refs_16_.refs_4_.refs_6_), channel_id=1, source_target_pairs={{0,15},{1,2},{2,1},{3,4},{4,3},{5,6},{6,5},{7,8},{8,7},{9,10},{10,... | collective-permute-start | bytes 1029128 | tf_op jit(solution)/shard_map/ppermute | solution.py:603
  65.7 11.7 %collective-permute-start.95 = (f32[640,128]{1,0:T(8,128)S(1)}, f32[640,128]{1,0:T(8,128)S(1)}, u32[]{:S(2)}, u32[]{:S(2)}) collective-permute-start(f32[640,128]{1,0:T(8,128)S(1)} %outer.15.refs_5_.refs_7_), channel_id=1, source_target_pairs={{0,15},{1,2},{2,1},{3,4},{4,3},{5,6},{6,5},{7,8},{8,7},{9,10},{10,... | collective-permute-start | bytes 983048 | tf_op jit(solution)/shard_map/ppermute | solution.py:603
  65.9 5.2 %collective-permute-start.91 = (f32[512,128]{1,0:T(8,128)S(1)}, f32[512,128]{1,0:T(8,128)S(1)}, u32[]{:S(2)}, u32[]{:S(2)}) collective-permute-start(f32[512,128]{1,0:T(8,128)S(1)} %get-tuple-element.352.refs_9_), channel_id=1, source_target_pairs={{0,1},{1,0},{2,3},{3,2},{4,5},{5,4},{6,7},{7,6},{8,9},{9,8},{10,11... | collective-permute-start | bytes 786440 | tf_op jit(solution)/shard_map/ppermute | solution.py:608
  65.9 5.2 %collective-permute-start.93 = (f32[414,128]{1,0:T(8,128)S(1)}, f32[414,128]{1,0:T(8,128)S(1)}, u32[]{:S(2)}, u32[]{:S(2)}) collective-permute-start(f32[414,128]{1,0:T(8,128)S(1)} %get-tuple-element.354), channel_id=1, source_target_pairs={{0,1},{1,0},{2,3},{3,2},{4,5},{5,4},{6,7},{7,6},{8,9},{9,8},{10,11... | collective-permute-start | bytes 635912 | tf_op jit(solution)/shard_map/ppermute | solution.py:608
  66.4 4.7 %collective-permute-start.92 = (f32[384,128]{1,0:T(8,128)S(1)}, f32[384,128]{1,0:T(8,128)S(1)}, u32[]{:S(2)}, u32[]{:S(2)}) collective-permute-start(f32[384,128]{1,0:T(8,128)S(1)} %get-tuple-element.353), channel_id=1, source_target_pairs={{0,1},{1,0},{2,3},{3,2},{4,5},{5,4},{6,7},{7,6},{8,9},{9,8},{10,11... | collective-permute-start | bytes 589832 | tf_op jit(solution)/shard_map/ppermute | solution.py:608
  71.0 13.6 %collective-permute-start.99 = (f32[660,128]{1,0:T(8,128)S(1)}, f32[660,128]{1,0:T(8,128)S(1)}, u32[]{:S(2)}, u32[]{:S(2)}) collective-permute-start(f32[660,128]{1,0:T(8,128)S(1)} %get-tuple-element.356.refs_16_.refs_4_.refs_7_.refs_6_), channel_id=1, source_target_pairs={{0,15},{1,2},{2,1},{3,4},{4,3},{5,6},{6,5},{7,8},{8,7},{9,10},{10,... | collective-permute-start | bytes 1013768 | tf_op jit(solution)/shard_map/ppermute | solution.py:603
  77.9 17.3 %collective-permute-start.100 = (f32[640,128]{1,0:T(8,128)S(1)}, f32[640,128]{1,0:T(8,128)S(1)}, u32[]{:S(2)}, u32[]{:S(2)}) collective-permute-start(f32[640,128]{1,0:T(8,128)S(1)} %outer.17.refs_5_.refs_7_), channel_id=1, source_target_pairs={{0,15},{1,2},{2,1},{3,4},{4,3},{5,6},{6,5},{7,8},{8,7},{9,10},{10,... | collective-permute-start | bytes 983048 | tf_op jit(solution)/shard_map/ppermute | solution.py:603
  78.0 7.4 %collective-permute-start.96 = (f32[512,128]{1,0:T(8,128)S(1)}, f32[512,128]{1,0:T(8,128)S(1)}, u32[]{:S(2)}, u32[]{:S(2)}) collective-permute-start(f32[512,128]{1,0:T(8,128)S(1)} %get-tuple-element.359.refs_9_), channel_id=1, source_target_pairs={{0,1},{1,0},{2,3},{3,2},{4,5},{5,4},{6,7},{7,6},{8,9},{9,8},{10,11... | collective-permute-start | bytes 786440 | tf_op jit(solution)/shard_map/ppermute | solution.py:608
  78.1 7.3 %collective-permute-start.98 = (f32[404,128]{1,0:T(8,128)S(1)}, f32[404,128]{1,0:T(8,128)S(1)}, u32[]{:S(2)}, u32[]{:S(2)}) collective-permute-start(f32[404,128]{1,0:T(8,128)S(1)} %get-tuple-element.361), channel_id=1, source_target_pairs={{0,1},{1,0},{2,3},{3,2},{4,5},{5,4},{6,7},{7,6},{8,9},{9,8},{10,11... | collective-permute-start | bytes 620552 | tf_op jit(solution)/shard_map/ppermute | solution.py:608
  78.6 6.8 %collective-permute-start.97 = (f32[384,128]{1,0:T(8,128)S(1)}, f32[384,128]{1,0:T(8,128)S(1)}, u32[]{:S(2)}, u32[]{:S(2)}) collective-permute-start(f32[384,128]{1,0:T(8,128)S(1)} %get-tuple-element.360), channel_id=1, source_target_pairs={{0,1},{1,0},{2,3},{3,2},{4,5},{5,4},{6,7},{7,6},{8,9},{9,8},{10,11... | collective-permute-start | bytes 589832 | tf_op jit(solution)/shard_map/ppermute | solution.py:608
  85.3 13.5 %collective-permute-start.104 = (f32[650,128]{1,0:T(8,128)S(1)}, f32[650,128]{1,0:T(8,128)S(1)}, u32[]{:S(2)}, u32[]{:S(2)}) collective-permute-start(f32[650,128]{1,0:T(8,128)S(1)} %get-tuple-element.363.refs_17_.refs_4_.refs_6_), channel_id=1, source_target_pairs={{0,15},{1,2},{2,1},{3,4},{4,3},{5,6},{6,5},{7,8},{8,7},{9,10},{10,... | collective-permute-start | bytes 998408 | tf_op jit(solution)/shard_map/ppermute | solution.py:603
  95.7 6.7 %collective-permute-start.105 = (f32[640,128]{1,0:T(8,128)S(1)}, f32[640,128]{1,0:T(8,128)S(1)}, u32[]{:S(2)}, u32[]{:S(2)}) collective-permute-start(f32[640,128]{1,0:T(8,128)S(1)} %outer.19.refs_5_.refs_7_), channel_id=1, source_target_pairs={{0,15},{1,2},{2,1},{3,4},{4,3},{5,6},{6,5},{7,8},{8,7},{9,10},{10,... | collective-permute-start | bytes 983048 | tf_op jit(solution)/shard_map/ppermute | solution.py:603
  95.8 3.8 %collective-permute-start.101 = (f32[512,128]{1,0:T(8,128)S(1)}, f32[512,128]{1,0:T(8,128)S(1)}, u32[]{:S(2)}, u32[]{:S(2)}) collective-permute-start(f32[512,128]{1,0:T(8,128)S(1)} %get-tuple-element.366.refs_10_), channel_id=1, source_target_pairs={{0,1},{1,0},{2,3},{3,2},{4,5},{5,4},{6,7},{7,6},{8,9},{9,8},{10,11... | collective-permute-start | bytes 786440 | tf_op jit(solution)/shard_map/ppermute | solution.py:608
  95.8 3.8 %collective-permute-start.103 = (f32[394,128]{1,0:T(8,128)S(1)}, f32[394,128]{1,0:T(8,128)S(1)}, u32[]{:S(2)}, u32[]{:S(2)}) collective-permute-start(f32[394,128]{1,0:T(8,128)S(1)} %get-tuple-element.368), channel_id=1, source_target_pairs={{0,1},{1,0},{2,3},{3,2},{4,5},{5,4},{6,7},{7,6},{8,9},{9,8},{10,11... | collective-permute-start | bytes 605192 | tf_op jit(solution)/shard_map/ppermute | solution.py:608
  96.3 3.2 %collective-permute-start.102 = (f32[384,128]{1,0:T(8,128)S(1)}, f32[384,128]{1,0:T(8,128)S(1)}, u32[]{:S(2)}, u32[]{:S(2)}) collective-permute-start(f32[384,128]{1,0:T(8,128)S(1)} %get-tuple-element.367), channel_id=1, source_target_pairs={{0,1},{1,0},{2,3},{3,2},{4,5},{5,4},{6,7},{7,6},{8,9},{9,8},{10,11... | collective-permute-start | bytes 589832 | tf_op jit(solution)/shard_map/ppermute | solution.py:608
  99.5 13.6 %collective-permute-start.107 = (f32[640,128]{1,0:T(8,128)S(1)}, f32[640,128]{1,0:T(8,128)S(1)}, u32[]{:S(2)}, u32[]{:S(2)}) collective-permute-start(f32[640,128]{1,0:T(8,128)S(1)} %get-tuple-element.370.refs_17_.refs_6_.refs_4_), channel_id=1, source_target_pairs={{0,15},{1,2},{2,1},{3,4},{4,3},{5,6},{6,5},{7,8},{8,7},{9,10},{10,... | collective-permute-start | bytes 983048 | tf_op jit(solution)/shard_map/ppermute | solution.py:603
  102.9 13.7 %collective-permute-start.106 = (f32[640,128]{1,0:T(8,128)S(1)}, f32[640,128]{1,0:T(8,128)S(1)}, u32[]{:S(2)}, u32[]{:S(2)}) collective-permute-start(f32[640,128]{1,0:T(8,128)S(1)} %outer.21.refs_7_.refs_5_), channel_id=1, source_target_pairs={{0,15},{1,2},{2,1},{3,4},{4,3},{5,6},{6,5},{7,8},{8,7},{9,10},{10,... | collective-permute-start | bytes 983048 | tf_op jit(solution)/shard_map/ppermute | solution.py:603
  104.6 2.5 %collective-permute-start.108 = (f32[512,128]{1,0:T(8,128)S(1)}, f32[512,128]{1,0:T(8,128)S(1)}, u32[]{:S(2)}, u32[]{:S(2)}) collective-permute-start(f32[512,128]{1,0:T(8,128)S(1)} %get-tuple-element.372.refs_10_), channel_id=1, source_target_pairs={{0,1},{1,0},{2,3},{3,2},{4,5},{5,4},{6,7},{7,6},{8,9},{9,8},{10,11... | collective-permute-start | bytes 786440 | tf_op jit(solution)/shard_map/ppermute | solution.py:608
  105.4 1.4 %collective-permute-start.109 = (f32[384,128]{1,0:T(8,128)S(1)}, f32[384,128]{1,0:T(8,128)S(1)}, u32[]{:S(2)}, u32[]{:S(2)}) collective-permute-start(f32[384,128]{1,0:T(8,128)S(1)} %get-tuple-element.375), channel_id=1, source_target_pairs={{0,1},{1,0},{2,3},{3,2},{4,5},{5,4},{6,7},{7,6},{8,9},{9,8},{10,11... | collective-permute-start | bytes 589832 | tf_op jit(solution)/shard_map/ppermute | solution.py:608
  105.4 1.7 %collective-permute-start.110 = (f32[384,128]{1,0:T(8,128)S(1)}, f32[384,128]{1,0:T(8,128)S(1)}, u32[]{:S(2)}, u32[]{:S(2)}) collective-permute-start(f32[384,128]{1,0:T(8,128)S(1)} %get-tuple-element.376), channel_id=1, source_target_pairs={{0,1},{1,0},{2,3},{3,2},{4,5},{5,4},{6,7},{7,6},{8,9},{9,8},{10,11... | collective-permute-start | bytes 589832 | tf_op jit(solution)/shard_map/ppermute | solution.py:608
